TPU v7x, 256 devices: a whole 4x4x8 slice. The times are simulated.
256 devices in a mesh: row: 16 (over y, x_hi, core), col: 16 (over x_lo, z).
Axes of the slice: x: 4 (x_hi: 2, x_lo: 2; x = x_hi * 2 + x_lo), y: 4, z: 8, core: 2. Of those that a mesh axis runs over, the one named last changes fastest.
Arguments:
- start_block: float32 [32768, 128], P('row'), may hold values from -400 to 400
- tiles: bfloat16 [16, 16, 16, 12, 128, 128], P('row', 'col'), may hold values from -0.02734375 to 0.02734375
- band_offsets: int32 [16, 16, 12], P('row', 'col'), may hold values from 0 to 15, as said below
Outputs:
- lanczos_alpha: float32 [2, 128], replicated
- lanczos_beta: float32 [2, 128], replicated
- next_vector: float32 [32768, 128], P('row')
Inputs may be any that keep to these rules, and one draw needn't show every extreme that they name: `band_offsets`: on each device the 12 offsets are distinct, the first is 0 and the second is 15.
All inputs are finite; a program needn't handle non-finite values.
Results may differ from a plain program's by a relative error of at most 0.0057.
Values may be sent and summed in bfloat16 or wider, within the bound.
No kernel may reach another device: no remote copies, remote signals or barrier semaphores. Data moves between devices by JAX's collectives and lax.ppermute only.
A program may use at most 128 MiB of HBM per device.

v0:
```python
import jax
import jax.numpy as jnp
from jax import lax
from jax.sharding import PartitionSpec as P

EPS = 1e-06


def shifted(value, axis, steps):
    count = lax.axis_size(axis)
    pairs = [(source, (source + steps) % count) for source in range(count)]
    return lax.ppermute(value, axis, pairs)


def fetch_segment(rounded, col_index):
    digits = (lax.axis_size("col") - 1).bit_length()
    moving = rounded
    for level in range(digits):
        arrived = shifted(moving, "row", -(1 << level))
        moving = jnp.where(col_index >> level & 1 == 1, arrived, moving)
    return moving


def return_segment(partial_back, col_index):
    digits = (lax.axis_size("col") - 1).bit_length()
    moving = partial_back
    for level in range(digits):
        arrived = shifted(moving, "row", 1 << level)
        moving = jnp.where(col_index >> level & 1 == 1, arrived, moving)
    return moving.astype(jnp.float32)


def apply_h(vector, tiles_dev, offsets, col_index):
    blocks = tiles_dev.shape[0]
    width = tiles_dev.shape[2]
    columns = vector.shape[1]
    rounded = vector.astype(jnp.bfloat16)
    remote = fetch_segment(rounded, col_index).reshape(blocks, width, columns)
    nearby = rounded.reshape(blocks, width, columns)
    column_index = (jnp.arange(blocks, dtype=jnp.int32)[:, None] + offsets[None, :]) % blocks
    forward = jnp.einsum(
        "bkij,bkjv->biv", tiles_dev, remote[column_index], preferred_element_type=jnp.float32
    )
    backward = jnp.einsum("bkji,bjv->bkiv", tiles_dev, nearby, preferred_element_type=jnp.float32)
    placed = (
        column_index[None, :, :] == jnp.arange(blocks, dtype=jnp.int32)[:, None, None]
    ).astype(jnp.float32)
    moved = jnp.einsum("sbk,bkiv->siv", placed, backward, precision=lax.Precision.HIGHEST)
    arrived = return_segment(moved.astype(jnp.bfloat16).reshape(blocks * width, columns), col_index)
    partial_sum = forward.reshape(blocks * width, columns) + arrived
    return lax.psum(partial_sum, "col")


def coefficients(q_vec, w_vec, count):
    alpha = lax.psum(jnp.sum(q_vec * w_vec, axis=0), "row") / count
    w_vec = w_vec - alpha * q_vec
    mean_square = lax.psum(jnp.sum(w_vec * w_vec, axis=0), "row") / count
    beta = jnp.sqrt(mean_square + EPS)
    return (alpha, beta, w_vec / beta)


def body(start_block, tiles, band_offsets):
    col_index = lax.axis_index("col")
    count = start_block.shape[0] * lax.axis_size("row")
    tiles_dev = tiles[0, 0]
    offsets = band_offsets[0, 0]
    start_sum = lax.psum(jnp.sum(start_block * start_block, axis=0), "row")
    q_first = start_block / jnp.sqrt(start_sum / count + EPS)
    w_vec = apply_h(q_first, tiles_dev, offsets, col_index)
    alpha_one, beta_one, q_second = coefficients(q_first, w_vec, count)
    w_vec = apply_h(q_second, tiles_dev, offsets, col_index) - beta_one * q_first
    alpha_two, beta_two, q_third = coefficients(q_second, w_vec, count)
    return (jnp.stack([alpha_one, alpha_two]), jnp.stack([beta_one, beta_two]), q_third)


def solution(mesh):
    placed = (P("row", None), P("row", "col", None, None, None, None), P("row", "col", None))
    return jax.shard_map(
        body, mesh=mesh, in_specs=placed, out_specs=(P(), P(), P("row", None)), check_vma=False
    )
```

profile of v0, /device:TPU:1, one launch (start us, length us, event | category | flops | bytes accessed | tf_op | source)
XLA Modules:
  0.0 687.7 jit_solution(17327099699873255033)
XLA Ops:
  8.7 35.7 %psum.49 = f32[128]{0:T(128)S(1)} all-reduce(f32[128]{0:T(128)S(1)} %multiply_reduce_fusion.4), channel_id=1, replica_groups=mesh['row'=16,'col'=16] {'row'}, use_global_device_ids=true, to_apply=%region_1.0 | all-reduce | flops 128 | bytes 1024 | tf_op jit(solution)/shard_map/psum | solution.py:67
  45.8 3.9 collective-permute-start
  49.7 9.2 %fusion.8 = f32[16,128,12,128]{3,1,2,0:T(8,128)} fusion(bf16[16,128,128,1]{2,1,3,0:T(8,128)(2,1)S(1)} %bitcast.89, bf16[1,1,16,12,128,128]{5,4,3,2,1,0:T(8,128)(2,1)} %param.4), kind=kOutput, calls=%fused_computation.10 | convolution fusion | flops 805306368 | bytes 19398656 | tf_op jit(solution)/shard_map/bkji,bjv->bkiv/dot_general | solution.py:44
  58.9 12.6 %copy.10 = f32[16,128,12,128]{1,0,2,3:T(8,128)} copy(f32[16,128,12,128]{3,1,2,0:T(8,128)} %fusion.8) | data formatting | bytes 25165824 | tf_op jit(solution)/shard_map/bkji,bjv->bkiv/dot_general | solution.py:44
  71.6 8.9 %fusion.21 = bf16[16,128,128]{2,0,1:T(8,128)(2,1)S(1)} fusion(f32[16,128,12,128]{1,0,2,3:T(8,128)} %copy.10, s32[16,12]{0,1:T(8,128)S(1)} %add_select_fusion), kind=kOutput, calls=%fused_computation.17 | convolution fusion | flops 604244992 | bytes 13107968 | tf_op jit(solution)/shard_map/sbk,bkiv->siv/dot_general | solution.py:48
  80.9 5.0 collective-permute-start.1
  86.0 5.6 collective-permute-done.4
  91.8 7.6 %collective-permute-done.1 = bf16[2048,128]{1,0:T(8,128)(2,1)} collective-permute-done((bf16[2048,128]{1,0:T(8,128)(2,1)S(1)}, bf16[2048,128]{1,0:T(8,128)(2,1)}, u32[]{:S(2)}, u32[]{:S(2)}) %collective-permute-start.1) | collective-permute-done | bytes 524320 | tf_op jit(solution)/shard_map/ppermute | solution.py:12
  99.6 9.8 %collective-permute-done.5 = bf16[2048,128]{1,0:T(8,128)(2,1)S(1)} collective-permute-done((bf16[2048,128]{1,0:T(8,128)(2,1)S(1)}, bf16[2048,128]{1,0:T(8,128)(2,1)S(1)}, u32[]{:S(2)}, u32[]{:S(2)}) %collective-permute-start.5) | collective-permute-done | bytes 524320 | tf_op jit(solution)/shard_map/ppermute | solution.py:12
  109.5 2.8 collective-permute-done.2
  112.5 11.8 %collective-permute-done.6 = bf16[2048,128]{1,0:T(8,128)(2,1)} collective-permute-done((bf16[2048,128]{1,0:T(8,128)(2,1)S(1)}, bf16[2048,128]{1,0:T(8,128)(2,1)}, u32[]{:S(2)}, u32[]{:S(2)}) %collective-permute-start.6) | collective-permute-done | bytes 524320 | tf_op jit(solution)/shard_map/ppermute | solution.py:12
  124.6 8.5 %collective-permute-done.3 = bf16[2048,128]{1,0:T(8,128)(2,1)S(1)} collective-permute-done((bf16[2048,128]{1,0:T(8,128)(2,1)S(1)}, bf16[2048,128]{1,0:T(8,128)(2,1)S(1)}, u32[]{:S(2)}, u32[]{:S(2)}) %collective-permute-start.3) | collective-permute-done | bytes 524320 | tf_op jit(solution)/shard_map/ppermute | solution.py:12
  133.1 8.0 %gather_fusion = bf16[192,128,128]{2,1,0:T(8,128)(2,1)} fusion(bf16[16,128,128]{2,1,0:T(8,128)(2,1)S(1)} %bitcast.85, s32[1024]{0:T(1024)S(1)} %pad_clamp_fusion), kind=kCustom, calls=%fused_computation | custom fusion | bytes 12583680 | tf_op jit(solution)/shard_map/gather | solution.py:42
  141.2 6.4 fusion.6
  148.9 138.9 %all-reduce.3.cloned.1.call-done = f32[2048,128]{1,0:T(8,128)} async-done(((f32[2048,128]{1,0:T(8,128)}), f32[2048,128]{1,0:T(8,128)}) %all-reduce.3.cloned.1.call-update) | async-done | bytes 1048592 | tf_op jit(solution)/shard_map/psum | solution.py:51
  289.3 43.4 %psum.51 = f32[128]{0:T(128)S(1)} all-reduce(f32[128]{0:T(128)S(1)} %multiply_reduce_fusion.3), channel_id=1, replica_groups=mesh['row'=16,'col'=16] {'row'}, use_global_device_ids=true, to_apply=%region_4.5 | all-reduce | flops 128 | bytes 1024 | tf_op jit(solution)/shard_map/psum | solution.py:55
  334.2 33.2 %psum.52 = f32[128]{0:T(128)S(1)} all-reduce(f32[128]{0:T(128)S(1)} %multiply_reduce_fusion.2), channel_id=1, replica_groups=mesh['row'=16,'col'=16] {'row'}, use_global_device_ids=true, to_apply=%region_6.7 | all-reduce | flops 128 | bytes 1024 | tf_op jit(solution)/shard_map/psum | solution.py:57
  369.6 9.2 %fusion.4 = f32[16,128,12,128]{3,1,2,0:T(8,128)} fusion(bf16[16,128,128,1]{2,1,3,0:T(8,128)(2,1)S(1)} %bitcast.88, bf16[1,1,16,12,128,128]{5,4,3,2,1,0:T(8,128)(2,1)} %param.4), kind=kOutput, calls=%fused_computation.6 | convolution fusion | flops 805306368 | bytes 19398656 | tf_op jit(solution)/shard_map/bkji,bjv->bkiv/dot_general | solution.py:44
  378.8 12.6 %copy.14 = f32[16,128,12,128]{1,0,2,3:T(8,128)} copy(f32[16,128,12,128]{3,1,2,0:T(8,128)} %fusion.4) | data formatting | bytes 25165824 | tf_op jit(solution)/shard_map/bkji,bjv->bkiv/dot_general | solution.py:44
  391.4 8.8 %fusion.18 = bf16[16,128,128]{2,0,1:T(8,128)(2,1)S(1)} fusion(f32[16,128,12,128]{1,0,2,3:T(8,128)} %copy.14, s32[16,12]{0,1:T(8,128)S(1)} %add_select_fusion), kind=kOutput, calls=%fused_computation.16 | convolution fusion | flops 604244992 | bytes 13107968 | tf_op jit(solution)/shard_map/sbk,bkiv->siv/dot_general | solution.py:48
  400.4 2.7 collective-permute-start.12
  403.1 2.7 collective-permute-start.9
  405.8 7.5 %collective-permute-done.12 = bf16[2048,128]{1,0:T(8,128)(2,1)S(1)} collective-permute-done((bf16[2048,128]{1,0:T(8,128)(2,1)S(1)}, bf16[2048,128]{1,0:T(8,128)(2,1)S(1)}, u32[]{:S(2)}, u32[]{:S(2)}) %collective-permute-start.12) | collective-permute-done | bytes 524320 | tf_op jit(solution)/shard_map/ppermute | solution.py:12
  413.5 6.1 collective-permute-done.9
  419.7 10.7 %collective-permute-done.13 = bf16[2048,128]{1,0:T(8,128)(2,1)S(1)} collective-permute-done((bf16[2048,128]{1,0:T(8,128)(2,1)S(1)}, bf16[2048,128]{1,0:T(8,128)(2,1)S(1)}, u32[]{:S(2)}, u32[]{:S(2)}) %collective-permute-start.13) | collective-permute-done | bytes 524320 | tf_op jit(solution)/shard_map/ppermute | solution.py:12
  432.2 23.1 %collective-permute-done.14 = bf16[2048,128]{1,0:T(8,128)(2,1)S(1)} collective-permute-done((bf16[2048,128]{1,0:T(8,128)(2,1)S(1)}, bf16[2048,128]{1,0:T(8,128)(2,1)S(1)}, u32[]{:S(2)}, u32[]{:S(2)}) %collective-permute-start.14) | collective-permute-done | bytes 524320 | tf_op jit(solution)/shard_map/ppermute | solution.py:12
  455.6 8.0 %gather_fusion.1 = bf16[192,128,128]{2,1,0:T(8,128)(2,1)} fusion(bf16[16,128,128]{2,1,0:T(8,128)(2,1)S(1)} %bitcast.84, s32[1024]{0:T(1024)S(1)} %pad_clamp_fusion), kind=kCustom, calls=%fused_computation.1 | custom fusion | bytes 12583680 | tf_op jit(solution)/shard_map/gather | solution.py:42
  463.6 6.5 fusion.10
  471.3 127.6 %all-reduce.5.cloned.1.call-done = f32[2048,128]{1,0:T(8,128)} async-done(((f32[2048,128]{1,0:T(8,128)}), f32[2048,128]{1,0:T(8,128)}) %all-reduce.5.cloned.1.call-update) | async-done | bytes 1048592 | tf_op jit(solution)/shard_map/psum | solution.py:51
  600.4 43.4 %psum.54 = f32[128]{0:T(128)S(1)} all-reduce(f32[128]{0:T(128)S(1)} %multiply_reduce_fusion.1), channel_id=1, replica_groups=mesh['row'=16,'col'=16] {'row'}, use_global_device_ids=true, to_apply=%region_9.10 | all-reduce | flops 128 | bytes 1024 | tf_op jit(solution)/shard_map/psum | solution.py:55
  643.9 1.6 multiply_reduce_fusion
  645.5 33.2 %psum.55 = f32[128]{0:T(128)S(1)} all-reduce(f32[128]{0:T(128)S(1)} %get-tuple-element.3), channel_id=1, replica_groups=mesh['row'=16,'col'=16] {'row'}, use_global_device_ids=true, to_apply=%region_11.12 | all-reduce | flops 128 | bytes 1024 | tf_op jit(solution)/shard_map/psum | solution.py:57
  (64 shorter events, 18.4 us)
Async XLA Ops:
  7.2 280.6 %all-reduce.3.cloned.1.call-start = ((), (), s32[]{:S(2)}) async-start(), calls=%async_computation | async-start | bytes 2097152 | tf_op jit(solution)/shard_map/psum | solution.py:51
  45.8 35.0 %collective-permute-start = (bf16[2048,128]{1,0:T(8,128)(2,1)S(1)}, bf16[2048,128]{1,0:T(8,128)(2,1)S(1)}, u32[]{:S(2)}, u32[]{:S(2)}) collective-permute-start(bf16[2048,128]{1,0:T(8,128)(2,1)S(1)} %fusion.41), channel_id=1, source_target_pairs={{0,240},{16,0},{32,16},{48,32},{64,48},{80,64},{96,80},{112,96},{1... | collective-permute-start | bytes 1572872 | tf_op jit(solution)/shard_map/ppermute | solution.py:12
  58.9 12.6 %copy-start.2 = (s32[1,1,12]{2,1,0:T(1,128)S(1)}, s32[1,1,12]{2,1,0:T(1,128)}, u32[]{:S(2)}) copy-start(s32[1,1,12]{2,1,0:T(1,128)} %param.5) | copy-start | bytes 148
  71.6 9.2 %copy-start = (f32[2048,128]{1,0:T(8,128)S(1)}, f32[2048,128]{1,0:T(8,128)}, u32[]{:S(2)}) copy-start(f32[2048,128]{1,0:T(8,128)} %param.3) | copy-start | bytes 3145732
  80.7 10.9 %collective-permute-start.4 = (bf16[2048,128]{1,0:T(8,128)(2,1)S(1)}, bf16[2048,128]{1,0:T(8,128)(2,1)S(1)}, u32[]{:S(2)}, u32[]{:S(2)}) collective-permute-start(bf16[2048,128]{1,0:T(8,128)(2,1)S(1)} %bitcast.90), channel_id=1, source_target_pairs={{0,16},{16,32},{32,48},{48,64},{64,80},{80,96},{96,112},{112,128},... | collective-permute-start | bytes 1572872 | tf_op jit(solution)/shard_map/ppermute | solution.py:12
  80.9 18.4 %collective-permute-start.1 = (bf16[2048,128]{1,0:T(8,128)(2,1)S(1)}, bf16[2048,128]{1,0:T(8,128)(2,1)}, u32[]{:S(2)}, u32[]{:S(2)}) collective-permute-start(bf16[2048,128]{1,0:T(8,128)(2,1)S(1)} %broadcast_select_fusion.3), channel_id=1, source_target_pairs={{0,224},{16,240},{32,0},{48,16},{64,32},{80,48},{96,64},{112,80},{... | collective-permute-start | bytes 1572872 | tf_op jit(solution)/shard_map/ppermute | solution.py:12
  91.7 17.7 %collective-permute-start.5 = (bf16[2048,128]{1,0:T(8,128)(2,1)S(1)}, bf16[2048,128]{1,0:T(8,128)(2,1)S(1)}, u32[]{:S(2)}, u32[]{:S(2)}) collective-permute-start(bf16[2048,128]{1,0:T(8,128)(2,1)S(1)} %broadcast_select_fusion.2), channel_id=1, source_target_pairs={{0,32},{16,48},{32,64},{48,80},{64,96},{80,112},{96,128},{112,144}... | collective-permute-start | bytes 1572872 | tf_op jit(solution)/shard_map/ppermute | solution.py:12
  99.4 12.9 %collective-permute-start.2 = (bf16[2048,128]{1,0:T(8,128)(2,1)S(1)}, bf16[2048,128]{1,0:T(8,128)(2,1)}, u32[]{:S(2)}, u32[]{:S(2)}) collective-permute-start(bf16[2048,128]{1,0:T(8,128)(2,1)S(1)} %broadcast_select_fusion.7), channel_id=1, source_target_pairs={{0,192},{16,208},{32,224},{48,240},{64,0},{80,16},{96,32},{112,48}... | collective-permute-start | bytes 1572872 | tf_op jit(solution)/shard_map/ppermute | solution.py:12
  109.4 14.9 %collective-permute-start.6 = (bf16[2048,128]{1,0:T(8,128)(2,1)S(1)}, bf16[2048,128]{1,0:T(8,128)(2,1)}, u32[]{:S(2)}, u32[]{:S(2)}) collective-permute-start(bf16[2048,128]{1,0:T(8,128)(2,1)S(1)} %broadcast_select_fusion.6), channel_id=1, source_target_pairs={{0,64},{16,80},{32,96},{48,112},{64,128},{80,144},{96,160},{112,17... | collective-permute-start | bytes 1572872 | tf_op jit(solution)/shard_map/ppermute | solution.py:12
  112.4 20.7 %collective-permute-start.3 = (bf16[2048,128]{1,0:T(8,128)(2,1)S(1)}, bf16[2048,128]{1,0:T(8,128)(2,1)S(1)}, u32[]{:S(2)}, u32[]{:S(2)}) collective-permute-start(bf16[2048,128]{1,0:T(8,128)(2,1)S(1)} %broadcast_select_fusion.11), channel_id=1, source_target_pairs={{0,128},{16,144},{32,160},{48,176},{64,192},{80,208},{96,224},{112... | collective-permute-start | bytes 1572872 | tf_op jit(solution)/shard_map/ppermute | solution.py:12
  124.3 23.2 %collective-permute-start.7 = (bf16[2048,128]{1,0:T(8,128)(2,1)S(1)}, bf16[2048,128]{1,0:T(8,128)(2,1)}, u32[]{:S(2)}, u32[]{:S(2)}) collective-permute-start(bf16[2048,128]{1,0:T(8,128)(2,1)S(1)} %broadcast_select_fusion.10), channel_id=1, source_target_pairs={{0,128},{16,144},{32,160},{48,176},{64,192},{80,208},{96,224},{112... | collective-permute-start | bytes 1572872 | tf_op jit(solution)/shard_map/ppermute | solution.py:12
  148.8 450.1 %all-reduce.5.cloned.1.call-start = ((), (), s32[]{:S(2)}) async-start(), calls=%async_computation.1 | async-start | bytes 2097152 | tf_op jit(solution)/shard_map/psum | solution.py:51
  368.9 34.2 %collective-permute-start.8 = (bf16[2048,128]{1,0:T(8,128)(2,1)S(1)}, bf16[2048,128]{1,0:T(8,128)(2,1)S(1)}, u32[]{:S(2)}, u32[]{:S(2)}) collective-permute-start(bf16[2048,128]{1,0:T(8,128)(2,1)S(1)} %fusion.42), channel_id=1, source_target_pairs={{0,240},{16,0},{32,16},{48,32},{64,48},{80,64},{96,80},{112,96},{1... | collective-permute-start | bytes 1572872 | tf_op jit(solution)/shard_map/ppermute | solution.py:12
  400.4 12.9 %collective-permute-start.12 = (bf16[2048,128]{1,0:T(8,128)(2,1)S(1)}, bf16[2048,128]{1,0:T(8,128)(2,1)S(1)}, u32[]{:S(2)}, u32[]{:S(2)}) collective-permute-start(bf16[2048,128]{1,0:T(8,128)(2,1)S(1)} %bitcast.91), channel_id=1, source_target_pairs={{0,16},{16,32},{32,48},{48,64},{64,80},{80,96},{96,112},{112,128},... | collective-permute-start | bytes 1572872 | tf_op jit(solution)/shard_map/ppermute | solution.py:12
  403.1 16.4 %collective-permute-start.9 = (bf16[2048,128]{1,0:T(8,128)(2,1)S(1)}, bf16[2048,128]{1,0:T(8,128)(2,1)S(1)}, u32[]{:S(2)}, u32[]{:S(2)}) collective-permute-start(bf16[2048,128]{1,0:T(8,128)(2,1)S(1)} %broadcast_select_fusion.1), channel_id=1, source_target_pairs={{0,224},{16,240},{32,0},{48,16},{64,32},{80,48},{96,64},{112,80},{... | collective-permute-start | bytes 1572872 | tf_op jit(solution)/shard_map/ppermute | solution.py:12
  413.4 17.0 %collective-permute-start.13 = (bf16[2048,128]{1,0:T(8,128)(2,1)S(1)}, bf16[2048,128]{1,0:T(8,128)(2,1)S(1)}, u32[]{:S(2)}, u32[]{:S(2)}) collective-permute-start(bf16[2048,128]{1,0:T(8,128)(2,1)S(1)} %broadcast_select_fusion), channel_id=1, source_target_pairs={{0,32},{16,48},{32,64},{48,80},{64,96},{80,112},{96,128},{112,144}... | collective-permute-start | bytes 1572872 | tf_op jit(solution)/shard_map/ppermute | solution.py:12
  419.6 12.5 %collective-permute-start.10 = (bf16[2048,128]{1,0:T(8,128)(2,1)S(1)}, bf16[2048,128]{1,0:T(8,128)(2,1)S(1)}, u32[]{:S(2)}, u32[]{:S(2)}) collective-permute-start(bf16[2048,128]{1,0:T(8,128)(2,1)S(1)} %broadcast_select_fusion.5), channel_id=1, source_target_pairs={{0,192},{16,208},{32,224},{48,240},{64,0},{80,16},{96,32},{112,48}... | collective-permute-start | bytes 1572872 | tf_op jit(solution)/shard_map/ppermute | solution.py:12
  430.4 24.9 %collective-permute-start.14 = (bf16[2048,128]{1,0:T(8,128)(2,1)S(1)}, bf16[2048,128]{1,0:T(8,128)(2,1)S(1)}, u32[]{:S(2)}, u32[]{:S(2)}) collective-permute-start(bf16[2048,128]{1,0:T(8,128)(2,1)S(1)} %broadcast_select_fusion.4), channel_id=1, source_target_pairs={{0,64},{16,80},{32,96},{48,112},{64,128},{80,144},{96,160},{112,17... | collective-permute-start | bytes 1572872 | tf_op jit(solution)/shard_map/ppermute | solution.py:12
  432.1 23.4 %collective-permute-start.11 = (bf16[2048,128]{1,0:T(8,128)(2,1)S(1)}, bf16[2048,128]{1,0:T(8,128)(2,1)S(1)}, u32[]{:S(2)}, u32[]{:S(2)}) collective-permute-start(bf16[2048,128]{1,0:T(8,128)(2,1)S(1)} %broadcast_select_fusion.9), channel_id=1, source_target_pairs={{0,128},{16,144},{32,160},{48,176},{64,192},{80,208},{96,224},{112... | collective-permute-start | bytes 1572872 | tf_op jit(solution)/shard_map/ppermute | solution.py:12
  455.4 14.7 %collective-permute-start.15 = (bf16[2048,128]{1,0:T(8,128)(2,1)S(1)}, bf16[2048,128]{1,0:T(8,128)(2,1)S(1)}, u32[]{:S(2)}, u32[]{:S(2)}) collective-permute-start(bf16[2048,128]{1,0:T(8,128)(2,1)S(1)} %broadcast_select_fusion.8), channel_id=1, source_target_pairs={{0,128},{16,144},{32,160},{48,176},{64,192},{80,208},{96,224},{112... | collective-permute-start | bytes 1572872 | tf_op jit(solution)/shard_map/ppermute | solution.py:12
  463.6 135.3 %copy-start.1 = (f32[2048,128]{1,0:T(8,128)S(1)}, f32[2048,128]{1,0:T(8,128)}, u32[]{:S(2)}) copy-start(f32[2048,128]{1,0:T(8,128)} %all-reduce.3.cloned.1.call-done) | copy-start | bytes 3145732
Sparse Core Ops, SparseCore 0:
  148.9 138.7 all-reduce.2
  471.4 127.4 all-reduce.4
where the time goes:
time: 689 us; the launch traced here: 688 us
  waiting for transfers between devices  360 us (52%)
  blocking collectives  189 us (27%)
  matrix products  49 us (7%)
  local copies, waits for them, and re-layouts  41.7 us (6%)
  starting transfers between devices  17.4 us (3%)
  other arithmetic  16.1 us (2%)
  between operations  14.3 us (2%)
    psum x2, waiting for transfers between devices, apply_h(): return lax.psum(partial_sum, 'col')  267 us
    ppermute x16, waiting for transfers between devices, shifted(): return lax.ppermute(value, axis, pairs)  93.7 us
    psum x2, blocking collectives, coefficients(): alpha = lax.psum(jnp.sum(q_vec * w_vec, axis=0), 'row') / count  86.8 us
    psum x2, blocking collectives, coefficients(): mean_square = lax.psum(jnp.sum(w_vec * w_vec, axis=0), 'row') / count  66.4 us
    psum x1, blocking collectives, body(): start_sum = lax.psum(jnp.sum(start_block * start_block, axis=0), 'row')  35.7 us
    dot_general x2, local copies, waits for them, and re-layouts, apply_h(): jnp.einsum('bkji,bjv->bkiv', tiles_dev, nearby, preferred_element_type=jn...  25.3 us
    dot_general x2, matrix products, apply_h(): jnp.einsum('bkji,bjv->bkiv', tiles_dev, nearby, preferred_element_type=jn...  18.4 us
    dot_general x2, matrix products, apply_h(): jnp.einsum('sbk,bkiv->siv', placed, backward, precision=lax.Precision.HIG...  17.8 us
  transfers between devices with their start and end apart: 18, of which 13 were waited for; matrix products, arithmetic and copies ran while one was open for 13% of the time, Pallas kernels for 0%

commit v1 on v0

v1 whole, which is shorter than its diff:
```python
import functools

import jax
import jax.numpy as jnp
from jax import lax
from jax.experimental import pallas as pl
from jax.experimental.pallas import tpu as pltpu
from jax.sharding import PartitionSpec as P

EPS = 1e-06
TINY = 1e-30
WIRE = jnp.float16
PRODUCT_SCALE = 128.0
SEGMENT_SCALE = 1024.0
ROWS_PER_STEP = 2


def split_halves(value):
    high = value.astype(jnp.bfloat16)
    low = (value - high.astype(jnp.float32)).astype(jnp.bfloat16)
    return jnp.concatenate([high, low], axis=1)


def forward_kernel(offsets, tiles, far, out, halves):
    step = pl.program_id(0)
    blocks, width, columns = far.shape

    @pl.when(step == 0)
    def _():
        for block in range(blocks):
            halves[block] = split_halves(far[block])

    kept = tiles.shape[1]
    for local in range(tiles.shape[0]):
        row = step * tiles.shape[0] + local
        total = jnp.zeros((width, 2 * columns), jnp.float32)
        for k in range(0, kept, 2):
            first = halves[lax.rem(row + offsets[k], blocks)]
            second = halves[lax.rem(row + offsets[k + 1], blocks)]
            left = jnp.concatenate([tiles[local, k], tiles[local, k + 1]], axis=1)
            right = jnp.concatenate([first, second], axis=0)
            total += jnp.dot(left, right, preferred_element_type=jnp.float32)
        out[local] = total[:, :columns] + total[:, columns:]


def backward_kernel(exact, offsets, tiles, near, out, squares, total):
    step = pl.program_id(0)
    blocks, columns, width = total.shape
    kept = tiles.shape[1]

    @pl.when(step == 0)
    def _():
        total[...] = jnp.zeros_like(total)
        squares[...] = jnp.zeros_like(squares)

    for local in range(tiles.shape[0]):
        row = step * tiles.shape[0] + local
        value = near[local]
        squares[...] += jnp.sum(value * value, axis=0, keepdims=True)
        turned = value.T
        high = turned.astype(jnp.bfloat16)
        if exact:
            low = (turned - high.astype(jnp.float32)).astype(jnp.bfloat16)
            left = jnp.concatenate([high, low], axis=0)
        else:
            left = high
        for k in range(0, kept, 2):
            right = jnp.concatenate([tiles[local, k], tiles[local, k + 1]], axis=1)
            part = jnp.dot(left, right, preferred_element_type=jnp.float32)
            if exact:
                part = part[:columns] + part[columns:]
            total[lax.rem(row + offsets[k], blocks)] += part[:, :width]
            total[lax.rem(row + offsets[k + 1], blocks)] += part[:, width:]

    @pl.when(step == pl.num_programs(0) - 1)
    def _():
        rows = blocks * width
        scale = SEGMENT_SCALE * lax.rsqrt(squares[...] * (1.0 / rows) + TINY)
        for block in range(blocks):
            out[block] = total[block].T * scale


def cost(tiles, passes):
    blocks, kept, width, _ = tiles.shape
    flops = 2 * passes * blocks * kept * width**3
    return pl.CostEstimate(flops=flops, bytes_accessed=2 * tiles.size, transcendentals=0)


def forward_product(tiles, offsets, far):
    blocks, kept, width, _ = tiles.shape
    columns = far.shape[-1]
    per = ROWS_PER_STEP
    return pl.pallas_call(
        forward_kernel,
        out_shape=jax.ShapeDtypeStruct((blocks, width, columns), jnp.float32),
        grid_spec=pltpu.PrefetchScalarGridSpec(
            num_scalar_prefetch=1,
            grid=(blocks // per,),
            in_specs=[
                pl.BlockSpec((per, kept, width, width), lambda i, o: (i, 0, 0, 0)),
                pl.BlockSpec((blocks, width, columns), lambda i, o: (0, 0, 0)),
            ],
            out_specs=pl.BlockSpec((per, width, columns), lambda i, o: (i, 0, 0)),
            scratch_shapes=[pltpu.VMEM((blocks, width, 2 * columns), jnp.bfloat16)],
        ),
        compiler_params=pltpu.CompilerParams(vmem_limit_bytes=24 * 2**20),
        cost_estimate=cost(tiles, 2),
        name="forward_product",
    )(offsets, tiles, far.reshape(blocks, width, columns))


def backward_product(tiles, offsets, near, exact):
    blocks, kept, width, _ = tiles.shape
    columns = near.shape[-1]
    per = ROWS_PER_STEP
    return pl.pallas_call(
        functools.partial(backward_kernel, exact),
        out_shape=(
            jax.ShapeDtypeStruct((blocks, width, columns), jnp.float32),
            jax.ShapeDtypeStruct((1, columns), jnp.float32),
        ),
        grid_spec=pltpu.PrefetchScalarGridSpec(
            num_scalar_prefetch=1,
            grid=(blocks // per,),
            in_specs=[
                pl.BlockSpec((per, kept, width, width), lambda i, o: (i, 0, 0, 0)),
                pl.BlockSpec((per, width, columns), lambda i, o: (i, 0, 0)),
            ],
            out_specs=(
                pl.BlockSpec((blocks, width, columns), lambda i, o: (0, 0, 0)),
                pl.BlockSpec((1, columns), lambda i, o: (0, 0)),
            ),
            scratch_shapes=[pltpu.VMEM((blocks, columns, width), jnp.float32)],
        ),
        compiler_params=pltpu.CompilerParams(vmem_limit_bytes=24 * 2**20),
        cost_estimate=cost(tiles, 2 if exact else 1),
        name="backward_product",
    )(offsets, tiles, near.reshape(blocks, width, columns))


def permute(value, place):
    rows, cols = lax.axis_size("row"), lax.axis_size("col")
    pairs = []
    for r in range(rows):
        for c in range(cols):
            to_row, to_col = place(r, c)
            pairs.append((r * cols + c, to_row % rows * cols + to_col % cols))
    return lax.ppermute(value, ("row", "col"), pairs)


def fetch_segment(value):
    half = lax.axis_size("col") // 2
    return permute(value, lambda r, c: (r - (c ^ half), c ^ half))


def return_segment(value):
    half = lax.axis_size("col") // 2
    return permute(value, lambda r, c: (r + c, c ^ half))


def sum_blocks(partial):
    count = lax.axis_size("col")
    rows, columns = partial.shape
    parts = partial.reshape(count, rows // count, columns)
    parts = lax.all_to_all(parts, "col", 0, 0)
    share = jnp.sum(parts.astype(jnp.float32), axis=0).astype(WIRE)
    copies = jnp.broadcast_to(share[None], parts.shape)
    return lax.all_to_all(copies, "col", 0, 0).reshape(rows, columns)


def row_values(*values):
    own = jnp.stack(values)
    copies = jnp.broadcast_to(own[None], (lax.axis_size("row"),) + own.shape)
    found = lax.all_to_all(copies, "row", 0, 0)
    return [found[:, k] for k in range(len(values))]


def pick(values, index):
    return lax.dynamic_index_in_dim(values, index, 0, keepdims=True)


def safe_ratio(top, bottom):
    return jnp.where(bottom > 0, top / jnp.where(bottom > 0, bottom, 1.0), 0.0)


def combine(products, residuals, weights, count):
    alpha = jnp.sum(products, axis=0) / count
    shift = safe_ratio(products, weights) - alpha
    mean_square = jnp.sum(residuals + shift * shift * weights, axis=0) / count
    return alpha, jnp.sqrt(mean_square + EPS)


def body(start_block, tiles, band_offsets):
    rows, cols = lax.axis_size("row"), lax.axis_size("col")
    row, col = lax.axis_index("row"), lax.axis_index("col")
    height, columns = start_block.shape
    count = height * rows
    tiles_dev = tiles[0, 0]
    offsets = band_offsets[0, 0]
    far_row = (row + col) % rows
    back_row = (row - (col ^ (cols // 2))) % rows

    def scale_of(squares):
        return lax.rsqrt(squares * (1.0 / height) + TINY)

    own_scale = scale_of(jnp.sum(start_block * start_block, axis=0))
    far = fetch_segment((start_block * (own_scale * SEGMENT_SCALE)).astype(WIRE))
    back, squares = backward_product(tiles_dev, offsets, start_block, True)
    back = return_segment(back.reshape(height, columns).astype(WIRE))
    (start_squares,) = row_values(squares[0])
    norm = jnp.sqrt(jnp.sum(start_squares, axis=0) / count + EPS)
    unit = (PRODUCT_SCALE / SEGMENT_SCALE) / (scale_of(start_squares) * norm)
    forward = forward_product(tiles_dev, offsets, far.astype(jnp.float32))
    back_unit = pick(unit, back_row)
    first = forward.reshape(height, columns) * pick(unit, far_row) + back.astype(jnp.float32) * back_unit
    first = first.astype(WIRE)
    product = sum_blocks(first)

    far = fetch_segment(product)
    near = product.astype(jnp.float32)
    back, squares = backward_product(tiles_dev, offsets, near, False)
    back = return_segment(back.reshape(height, columns).astype(WIRE))
    q_first = start_block / norm
    w_first = near * (1.0 / PRODUCT_SCALE)
    weights = start_squares / (norm * norm)
    own_weight = pick(weights, row)[0]
    inner = jnp.sum(q_first * w_first, axis=0)
    rest = w_first - safe_ratio(inner, own_weight) * q_first
    residual = jnp.sum(rest * rest, axis=0)
    squares, inner, residual = row_values(squares[0], inner, residual)
    alpha_one, beta_one = combine(inner, residual, weights, count)
    forward = forward_product(tiles_dev, offsets, far.astype(jnp.float32))
    back_unit = 1.0 / (SEGMENT_SCALE * pick(scale_of(squares), back_row))
    second = forward.reshape(height, columns) + back.astype(jnp.float32) * back_unit
    second = (second - alpha_one * first.astype(jnp.float32)) / beta_one
    product = sum_blocks(second.astype(WIRE))

    q_second = (w_first - alpha_one * q_first) / beta_one
    w_second = product.astype(jnp.float32) * (1.0 / PRODUCT_SCALE) - beta_one * q_first
    inner = jnp.sum(q_second * w_second, axis=0)
    weight = jnp.sum(q_second * q_second, axis=0)
    rest = w_second - safe_ratio(inner, weight) * q_second
    residual = jnp.sum(rest * rest, axis=0)
    inner, residual, weight = row_values(inner, residual, weight)
    alpha_two, beta_two = combine(inner, residual, weight, count)
    q_third = (w_second - alpha_two * q_second) / beta_two
    return (jnp.stack([alpha_one, alpha_two]), jnp.stack([beta_one, beta_two]), q_third)


def solution(mesh):
    placed = (P("row", None), P("row", "col", None, None, None, None), P("row", "col", None))
    return jax.shard_map(
        body, mesh=mesh, in_specs=placed, out_specs=(P(), P(), P("row", None)), check_vma=False
    )
```

time: 689 us -> 207 us (0.30)
  waiting for transfers between devices: 360 us -> 58.7 us
  blocking collectives: 189 us -> 73.7 us
  matrix products: 49 us -> 0 us
  local copies, waits for them, and re-layouts: 41.7 us -> 16.2 us
  Pallas kernels: 0 us -> 18.2 us
  starting transfers between devices: 17.4 us -> 31.7 us
  between operations: 14.3 us -> 0.88 us
  other arithmetic: 16.1 us -> 7.03 us
    psum x2 -> x0, waiting for transfers between devices: 267 us -> none  [apply_h(): return lax.psum(partial_sum, 'col')]
    psum x5 -> x0, blocking collectives: 189 us -> none  [the longest x2 86.8 us: coefficients(): alpha = lax.psum(jnp.sum(q_vec * w_vec, axis=0), 'row') / count]
    all_to_all x0 -> x4, blocking collectives: none -> 73.7 us  [the longest x2 38.8 us: sum_blocks(): parts = lax.all_to_all(parts, 'col', 0, 0)]
    ppermute x16 -> x4, waiting for transfers between devices: 93.7 us -> 40.8 us  [permute(): return lax.ppermute(value, ('row', 'col'), pairs)]
    dot_general x6 -> x0, matrix products: 49 us -> none  [the longest x2 18.4 us: apply_h(): jnp.einsum('bkji,bjv->bkiv', tiles_dev, nearby, preferred_element_type=jn...]
    dot_general x2 -> x0, local copies, waits for them, and re-layouts: 25.3 us -> none  [apply_h(): jnp.einsum('bkji,bjv->bkiv', tiles_dev, nearby, preferred_element_type=jn...]
    all_to_all x0 -> x3, starting transfers between devices: none -> 23.8 us  [the longest x2 17.6 us: row_values(): found = lax.all_to_all(copies, 'row', 0, 0)]
    pallas_call x0 -> x4, Pallas kernels: none -> 18.2 us  [the longest x2 10.6 us: backward_product(): pl.pallas_call(functools.partial(backward_kernel, exact), out_shape=(jax....]
  transfers between devices with their start and end apart: 18 -> 7, of which waited for: 13 -> 5; matrix products, arithmetic and copies ran while one was open for 13% -> 1% of each run, Pallas kernels for 0% -> 4%
where the time goes in v1:
time: 207 us; the launch traced here: 206 us
  blocking collectives  73.7 us (36%)
  waiting for transfers between devices  58.7 us (28%)
  starting transfers between devices  31.7 us (15%)
  Pallas kernels  18.2 us (9%)
  local copies, waits for them, and re-layouts  16.2 us (8%)
  other arithmetic  7.03 us (3%)
    ppermute x4, waiting for transfers between devices, permute(): return lax.ppermute(value, ('row', 'col'), pairs)  40.8 us
    all_to_all x2, blocking collectives, sum_blocks(): parts = lax.all_to_all(parts, 'col', 0, 0)  38.8 us
    all_to_all x1, blocking collectives, sum_blocks(): return lax.all_to_all(copies, 'col', 0, 0).reshape(rows, columns)  18.7 us
    all_to_all x2, starting transfers between devices, row_values(): found = lax.all_to_all(copies, 'row', 0, 0)  17.6 us
    all_to_all x1, blocking collectives, row_values(): found = lax.all_to_all(copies, 'row', 0, 0)  16.2 us
    unnamed x18, local copies, waits for them, and re-layouts  14 us
    all_to_all x1, waiting for transfers between devices, sum_blocks(): return lax.all_to_all(copies, 'col', 0, 0).reshape(rows, columns)  12.9 us
    pallas_call x2, Pallas kernels, backward_product(): pl.pallas_call(functools.partial(backward_kernel, exact), out_shape=(jax....  10.6 us
  transfers between devices with their start and end apart: 7, of which 5 were waited for; matrix products, arithmetic and copies ran while one was open for 1% of the time, Pallas kernels for 4%

profile of v1, /device:TPU:1, one launch (start us, length us, event | category | flops | bytes accessed | tf_op | source)
XLA Modules:
  0.0 206.4 jit_solution(17921349666428106530)
XLA Ops:
  0.6 2.8 %copy-done = bf16[1,1,16,12,128,128]{5,4,3,2,1,0:T(8,128)(2,1)S(1)} copy-done((bf16[1,1,16,12,128,128]{5,4,3,2,1,0:T(8,128)(2,1)S(1)}, bf16[1,1,16,12,128,128]{5,4,3,2,1,0:T(8,128)(2,1)}, u32[]{:S(2)}) %copy-start) | copy-done | bytes 6291480
  3.4 1.2 copy-done.4
  4.6 0.7 copy-done.6
  5.3 6.1 %backward_product.2 = (f32[16,128,128]{2,1,0:T(8,128)S(1)}, f32[1,128]{1,0:T(1,128)S(1)}) custom-call(s32[12]{0:T(128)S(1)} %bitcast.78, bf16[16,12,128,128]{3,2,1,0:T(8,128)(2,1)S(1)} %bitcast.73, f32[16,128,128]{2,1,0:T(8,128)S(1)} %bitcast.77), custom_call_target="tpu_custom_call" | custom-call | flops 1610612736 | bytes 6291456 | tf_op jit(solution)/shard_map/backward_product/pallas_call | solution.py:116
  11.4 0.6 broadcast_in_dim.29
  12.0 8.4 %all-to-all-start = ((f32[16,1,128]{2,1,0:T(1,128)}), f32[16,1,128]{2,1,0:T(1,128)S(1)}, u32[]{:S(2)}, u32[]{:S(2)}) async-start(f32[16,1,128]{2,1,0:T(1,128)} %broadcast_in_dim.29), calls=%async_computation | async-start | bytes 16384 | tf_op jit(solution)/shard_map/all_to_all | solution.py:174
  21.4 3.6 %collective-permute-start = (f16[2048,128]{1,0:T(8,128)(2,1)S(1)}, f16[2048,128]{1,0:T(8,128)(2,1)S(1)}, u32[]{:S(2)}, u32[]{:S(2)}) collective-permute-start(f16[2048,128]{1,0:T(8,128)(2,1)S(1)} %multiply_convert_fusion), channel_id=1, source_target_pairs={{0,136},{1,121},{2,106},{3,91},{4,76},{5,61},{6,46},{7,31},{8,0},{... | collective-permute-start | bytes 1572872 | tf_op jit(solution)/shard_map/ppermute | solution.py:148
  25.0 2.4 %all-to-all-done = f32[16,1,128]{2,1,0:T(1,128)S(1)} async-done(((f32[16,1,128]{2,1,0:T(1,128)}), f32[16,1,128]{2,1,0:T(1,128)S(1)}, u32[]{:S(2)}, u32[]{:S(2)}) %all-to-all-start) | async-done | bytes 8224 | tf_op jit(solution)/shard_map/all_to_all | solution.py:174
  27.5 20.1 %collective-permute-done = f16[2048,128]{1,0:T(8,128)(2,1)S(1)} collective-permute-done((f16[2048,128]{1,0:T(8,128)(2,1)S(1)}, f16[2048,128]{1,0:T(8,128)(2,1)S(1)}, u32[]{:S(2)}, u32[]{:S(2)}) %collective-permute-start) | collective-permute-done | bytes 524320 | tf_op jit(solution)/shard_map/ppermute | solution.py:148
  47.8 2.8 %copy-done.1 = bf16[1,1,16,12,128,128]{5,4,3,2,1,0:T(8,128)(2,1)S(1)} copy-done((bf16[1,1,16,12,128,128]{5,4,3,2,1,0:T(8,128)(2,1)S(1)}, bf16[1,1,16,12,128,128]{5,4,3,2,1,0:T(8,128)(2,1)}, u32[]{:S(2)}) %copy-start.1) | copy-done | bytes 6291480
  50.5 3.8 %forward_product.2 = f32[16,128,128]{2,1,0:T(8,128)S(1)} custom-call(s32[12]{0:T(128)S(1)} %bitcast.79, bf16[16,12,128,128]{3,2,1,0:T(8,128)(2,1)S(1)} %bitcast.74, f32[16,128,128]{2,1,0:T(8,128)S(1)} %convert.2.far), custom_call_target="tpu_custom_call" | custom-call | flops 1610612736 | bytes 6291456 | tf_op jit(solution)/shard_map/forward_product/pallas_call | solution.py:93
  54.6 21.0 %all_to_all.35 = f16[16,128,128]{2,1,0:T(8,128)(2,1)S(1)} all-to-all(f16[16,128,128]{2,1,0:T(8,128)(2,1)S(1)} %bitcast.84), channel_id=1, replica_groups=mesh['row'=16,'col'=16] {'col'}, dimensions={0} | all-to-all | bytes 1048576 | tf_op jit(solution)/shard_map/all_to_all | solution.py:165
  75.7 0.9 broadcast_in_dim.30
  76.6 6.1 %all-to-all-start.2 = ((f16[16,128,128]{2,1,0:T(8,128)(2,1)}), f16[16,128,128]{2,1,0:T(8,128)(2,1)S(1)}, u32[]{:S(2)}, u32[]{:S(2)}) async-start(f16[16,128,128]{2,1,0:T(8,128)(2,1)} %broadcast_in_dim.30), calls=%async_computation.2 | async-start | bytes 1048576 | tf_op jit(solution)/shard_map/all_to_all | solution.py:168
  82.7 12.9 %all-to-all-done.2 = f16[16,128,128]{2,1,0:T(8,128)(2,1)S(1)} async-done(((f16[16,128,128]{2,1,0:T(8,128)(2,1)}), f16[16,128,128]{2,1,0:T(8,128)(2,1)S(1)}, u32[]{:S(2)}, u32[]{:S(2)}) %all-to-all-start.2) | async-done | bytes 524320 | tf_op jit(solution)/shard_map/all_to_all | solution.py:168
  95.7 2.8 %copy-done.2 = bf16[1,1,16,12,128,128]{5,4,3,2,1,0:T(8,128)(2,1)S(1)} copy-done((bf16[1,1,16,12,128,128]{5,4,3,2,1,0:T(8,128)(2,1)S(1)}, bf16[1,1,16,12,128,128]{5,4,3,2,1,0:T(8,128)(2,1)}, u32[]{:S(2)}) %copy-start.2) | copy-done | bytes 6291480
  98.5 4.5 %backward_product.3 = (f32[16,128,128]{2,1,0:T(8,128)S(1)}, f32[1,128]{1,0:T(1,128)S(1)}) custom-call(s32[12]{0:T(128)S(1)} %bitcast.80, bf16[16,12,128,128]{3,2,1,0:T(8,128)(2,1)S(1)} %bitcast.75, f32[16,128,128]{2,1,0:T(8,128)S(1)} %convert_element_type.69.near), custom_call_target="tpu_custom_call" | custom-call | flops 805306368 | bytes 6291456 | tf_op jit(solution)/shard_map/backward_product/pallas_call | solution.py:116
  103.7 0.6 broadcast_in_dim.32
  104.3 9.2 %all-to-all-start.3 = ((f32[16,3,128]{2,1,0:T(4,128)}), f32[16,3,128]{2,1,0:T(4,128)S(1)}, u32[]{:S(2)}, u32[]{:S(2)}) async-start(f32[16,3,128]{2,1,0:T(4,128)} %broadcast_in_dim.32), calls=%async_computation.3 | async-start | bytes 65536 | tf_op jit(solution)/shard_map/all_to_all | solution.py:174
  113.5 0.9 convert_element_type.71
  114.4 0.6 collective-permute-start.3
  115.0 3.3 %collective-permute-start.2 = (f16[2048,128]{1,0:T(8,128)(2,1)S(1)}, f16[2048,128]{1,0:T(8,128)(2,1)S(1)}, u32[]{:S(2)}, u32[]{:S(2)}) collective-permute-start(f16[2048,128]{1,0:T(8,128)(2,1)S(1)} %bitcast.83), channel_id=1, source_target_pairs={{0,136},{1,121},{2,106},{3,91},{4,76},{5,61},{6,46},{7,31},{8,0},{... | collective-permute-start | bytes 1572872 | tf_op jit(solution)/shard_map/ppermute | solution.py:148
  118.3 2.5 %all-to-all-done.3 = f32[16,3,128]{2,1,0:T(4,128)S(1)} async-done(((f32[16,3,128]{2,1,0:T(4,128)}), f32[16,3,128]{2,1,0:T(4,128)S(1)}, u32[]{:S(2)}, u32[]{:S(2)}) %all-to-all-start.3) | async-done | bytes 24608 | tf_op jit(solution)/shard_map/all_to_all | solution.py:174
  120.9 20.7 %collective-permute-done.2 = f16[2048,128]{1,0:T(8,128)(2,1)S(1)} collective-permute-done((f16[2048,128]{1,0:T(8,128)(2,1)S(1)}, f16[2048,128]{1,0:T(8,128)(2,1)S(1)}, u32[]{:S(2)}, u32[]{:S(2)}) %collective-permute-start.2) | collective-permute-done | bytes 524320 | tf_op jit(solution)/shard_map/ppermute | solution.py:148
  141.7 2.8 %copy-done.3 = bf16[1,1,16,12,128,128]{5,4,3,2,1,0:T(8,128)(2,1)S(1)} copy-done((bf16[1,1,16,12,128,128]{5,4,3,2,1,0:T(8,128)(2,1)S(1)}, bf16[1,1,16,12,128,128]{5,4,3,2,1,0:T(8,128)(2,1)}, u32[]{:S(2)}) %copy-start.3) | copy-done | bytes 6291480
  144.5 3.8 %forward_product.3 = f32[16,128,128]{2,1,0:T(8,128)S(1)} custom-call(s32[12]{0:T(128)S(1)} %bitcast.81, bf16[16,12,128,128]{3,2,1,0:T(8,128)(2,1)S(1)} %bitcast.76, f32[16,128,128]{2,1,0:T(8,128)S(1)} %convert.3.far), custom_call_target="tpu_custom_call" | custom-call | flops 1610612736 | bytes 6291456 | tf_op jit(solution)/shard_map/forward_product/pallas_call | solution.py:93
  148.6 17.8 %all_to_all.36 = f16[16,128,128]{2,1,0:T(8,128)(2,1)S(1)} all-to-all(f16[16,128,128]{2,1,0:T(8,128)(2,1)S(1)} %bitcast.85), channel_id=1, replica_groups=mesh['row'=16,'col'=16] {'col'}, dimensions={0} | all-to-all | bytes 1048576 | tf_op jit(solution)/shard_map/all_to_all | solution.py:165
  166.6 18.7 %all_to_all.37 = f16[16,128,128]{2,1,0:T(8,128)(2,1)S(1)} all-to-all(f16[16,128,128]{2,1,0:T(8,128)(2,1)S(1)} %broadcast_in_dim.34), channel_id=1, replica_groups=mesh['row'=16,'col'=16] {'col'}, dimensions={0} | all-to-all | bytes 1048576 | tf_op jit(solution)/shard_map/all_to_all | solution.py:168
  185.9 0.9 copy-done.8
  187.2 16.2 %all_to_all.38 = f32[16,3,128]{2,1,0:T(4,128)S(1)} all-to-all(f32[16,3,128]{2,1,0:T(4,128)S(1)} %broadcast_in_dim.36), channel_id=1, replica_groups=mesh['row'=16,'col'=16] {'row'}, dimensions={0} | all-to-all | bytes 49152 | tf_op jit(solution)/shard_map/all_to_all | solution.py:174
  203.5 2.3 %subtract_divide_fusion = f32[2048,128]{1,0:T(8,128)} fusion(f32[2048,128]{1,0:T(8,128)S(1)} %get-tuple-element.13, f32[2048,128]{1,0:T(8,128)} %copy-done.8, f32[128]{0:T(128)S(1)} %get-tuple-element.25, f32[128]{0:T(128)S(1)} %get-tuple-element.29), kind=kLoop, calls=%fused_computation.8 | loop fusion | flops 786432 | bytes 3146752 | tf_op jit(solution)/shard_map/div | solution.py:246
  205.8 0.6 pad_maximum_fusion.2
  (53 shorter events, 3.8 us)
Async XLA Ops:
  0.6 2.8 %copy-start = (bf16[1,1,16,12,128,128]{5,4,3,2,1,0:T(8,128)(2,1)S(1)}, bf16[1,1,16,12,128,128]{5,4,3,2,1,0:T(8,128)(2,1)}, u32[]{:S(2)}) copy-start(bf16[1,1,16,12,128,128]{5,4,3,2,1,0:T(8,128)(2,1)} %param.4) | copy-start | bytes 18874372
  3.4 1.2 copy-start.4
  4.6 0.7 copy-start.6
  5.3 15.7 %copy-start.5 = (f32[2048,128]{1,0:T(8,128)S(1)}, f32[2048,128]{1,0:T(8,128)}, u32[]{:S(2)}) copy-start(f32[2048,128]{1,0:T(8,128)} %param.3) | copy-start | bytes 3145732
  5.3 42.4 %copy-start.7 = (s32[1,1,12]{2,1,0:T(1,128)S(1)}, s32[1,1,12]{2,1,0:T(1,128)}, u32[]{:S(2)}) copy-start(s32[1,1,12]{2,1,0:T(1,128)} %param.5) | copy-start | bytes 148
  12.0 15.4 %all-to-all-start = ((f32[16,1,128]{2,1,0:T(1,128)}), f32[16,1,128]{2,1,0:T(1,128)S(1)}, u32[]{:S(2)}, u32[]{:S(2)}) async-start(f32[16,1,128]{2,1,0:T(1,128)} %broadcast_in_dim.29), calls=%async_computation | async-start | bytes 16384 | tf_op jit(solution)/shard_map/all_to_all | solution.py:174
  20.6 33.7 %collective-permute-start.1 = (f16[2048,128]{1,0:T(8,128)(2,1)S(1)}, f16[2048,128]{1,0:T(8,128)(2,1)S(1)}, u32[]{:S(2)}, u32[]{:S(2)}) collective-permute-start(f16[2048,128]{1,0:T(8,128)(2,1)S(1)} %bitcast.86), channel_id=1, source_target_pairs={{0,8},{1,25},{2,42},{3,59},{4,76},{5,93},{6,110},{7,127},{8,128},{... | collective-permute-start | bytes 1572872 | tf_op jit(solution)/shard_map/ppermute | solution.py:148
  21.4 26.2 %collective-permute-start = (f16[2048,128]{1,0:T(8,128)(2,1)S(1)}, f16[2048,128]{1,0:T(8,128)(2,1)S(1)}, u32[]{:S(2)}, u32[]{:S(2)}) collective-permute-start(f16[2048,128]{1,0:T(8,128)(2,1)S(1)} %multiply_convert_fusion), channel_id=1, source_target_pairs={{0,136},{1,121},{2,106},{3,91},{4,76},{5,61},{6,46},{7,31},{8,0},{... | collective-permute-start | bytes 1572872 | tf_op jit(solution)/shard_map/ppermute | solution.py:148
  47.7 2.8 %copy-start.1 = (bf16[1,1,16,12,128,128]{5,4,3,2,1,0:T(8,128)(2,1)S(1)}, bf16[1,1,16,12,128,128]{5,4,3,2,1,0:T(8,128)(2,1)}, u32[]{:S(2)}) copy-start(bf16[1,1,16,12,128,128]{5,4,3,2,1,0:T(8,128)(2,1)} %param.4) | copy-start | bytes 18874372
  76.6 19.1 %all-to-all-start.2 = ((f16[16,128,128]{2,1,0:T(8,128)(2,1)}), f16[16,128,128]{2,1,0:T(8,128)(2,1)S(1)}, u32[]{:S(2)}, u32[]{:S(2)}) async-start(f16[16,128,128]{2,1,0:T(8,128)(2,1)} %broadcast_in_dim.30), calls=%async_computation.2 | async-start | bytes 1048576 | tf_op jit(solution)/shard_map/all_to_all | solution.py:168
  95.7 2.8 %copy-start.2 = (bf16[1,1,16,12,128,128]{5,4,3,2,1,0:T(8,128)(2,1)S(1)}, bf16[1,1,16,12,128,128]{5,4,3,2,1,0:T(8,128)(2,1)}, u32[]{:S(2)}) copy-start(bf16[1,1,16,12,128,128]{5,4,3,2,1,0:T(8,128)(2,1)} %param.4) | copy-start | bytes 18874372
  104.3 16.5 %all-to-all-start.3 = ((f32[16,3,128]{2,1,0:T(4,128)}), f32[16,3,128]{2,1,0:T(4,128)S(1)}, u32[]{:S(2)}, u32[]{:S(2)}) async-start(f32[16,3,128]{2,1,0:T(4,128)} %broadcast_in_dim.32), calls=%async_computation.3 | async-start | bytes 65536 | tf_op jit(solution)/shard_map/all_to_all | solution.py:174
  114.4 33.9 %collective-permute-start.3 = (f16[2048,128]{1,0:T(8,128)(2,1)}, f16[2048,128]{1,0:T(8,128)(2,1)S(1)}, u32[]{:S(2)}, u32[]{:S(2)}) collective-permute-start(f16[2048,128]{1,0:T(8,128)(2,1)} %bitcast.20), channel_id=1, source_target_pairs={{0,8},{1,25},{2,42},{3,59},{4,76},{5,93},{6,110},{7,127},{8,128},{... | collective-permute-start | bytes 1572872 | tf_op jit(solution)/shard_map/ppermute | solution.py:148
  115.0 26.6 %collective-permute-start.2 = (f16[2048,128]{1,0:T(8,128)(2,1)S(1)}, f16[2048,128]{1,0:T(8,128)(2,1)S(1)}, u32[]{:S(2)}, u32[]{:S(2)}) collective-permute-start(f16[2048,128]{1,0:T(8,128)(2,1)S(1)} %bitcast.83), channel_id=1, source_target_pairs={{0,136},{1,121},{2,106},{3,91},{4,76},{5,61},{6,46},{7,31},{8,0},{... | collective-permute-start | bytes 1572872 | tf_op jit(solution)/shard_map/ppermute | solution.py:148
  141.7 2.8 %copy-start.3 = (bf16[1,1,16,12,128,128]{5,4,3,2,1,0:T(8,128)(2,1)S(1)}, bf16[1,1,16,12,128,128]{5,4,3,2,1,0:T(8,128)(2,1)}, u32[]{:S(2)}) copy-start(bf16[1,1,16,12,128,128]{5,4,3,2,1,0:T(8,128)(2,1)} %param.4) | copy-start | bytes 18874372
  185.9 1.0 copy-start.8

commit v2 on v1

v2 whole, which is shorter than its diff:
```python
import functools

import jax
import jax.numpy as jnp
from jax import lax
from jax.experimental import pallas as pl
from jax.experimental.pallas import tpu as pltpu
from jax.sharding import PartitionSpec as P

EPS = 1e-06
TINY = 1e-30
WIRE = jnp.float16
PRODUCT_SCALE = 128.0
SEGMENT_SCALE = 1024.0
ROWS_PER_STEP = 2
VMEM_LIMIT = 56 * 2**20


def split_halves(value):
    high = value.astype(jnp.bfloat16)
    low = (value - high.astype(jnp.float32)).astype(jnp.bfloat16)
    return jnp.concatenate([high, low], axis=1)


def forward_kernel(places, tiles, near_half, far_half, out, halves):
    step = pl.program_id(0)
    blocks, width, columns = halves.shape[0], halves.shape[1], near_half.shape[2]
    each = blocks // 2
    kept = tiles.shape[1]
    start = places[kept] * each

    @pl.when(step == 0)
    def _():
        for block in range(each):
            halves[start + block] = split_halves(near_half[block])
            halves[each - start + block] = split_halves(far_half[block])

    for local in range(tiles.shape[0]):
        row = each - start + step * tiles.shape[0] + local
        total = jnp.zeros((width, 2 * columns), jnp.float32)
        for k in range(0, kept, 2):
            first = halves[lax.rem(row + places[k], blocks)]
            second = halves[lax.rem(row + places[k + 1], blocks)]
            left = jnp.concatenate([tiles[local, k], tiles[local, k + 1]], axis=1)
            right = jnp.concatenate([first, second], axis=0)
            total += jnp.dot(left, right, preferred_element_type=jnp.float32)
        out[local] = total[:, :columns] + total[:, columns:]


def backward_kernel(exact, places, tiles, near, out, squares, total):
    step = pl.program_id(0)
    blocks, columns, width = total.shape
    each = blocks // 2
    kept = tiles.shape[1]
    start = places[kept] * each

    @pl.when(step == 0)
    def _():
        total[...] = jnp.zeros_like(total)
        squares[...] = jnp.zeros_like(squares)

    for local in range(tiles.shape[0]):
        row = start + step * tiles.shape[0] + local
        value = near[local]
        squares[...] += jnp.sum(value * value, axis=0, keepdims=True)
        turned = value.T
        high = turned.astype(jnp.bfloat16)
        if exact:
            low = (turned - high.astype(jnp.float32)).astype(jnp.bfloat16)
            left = jnp.concatenate([high, low], axis=0)
        else:
            left = high
        for k in range(0, kept, 2):
            right = jnp.concatenate([tiles[local, k], tiles[local, k + 1]], axis=1)
            part = jnp.dot(left, right, preferred_element_type=jnp.float32)
            if exact:
                part = part[:columns] + part[columns:]
            total[lax.rem(row + places[k], blocks)] += part[:, :width]
            total[lax.rem(row + places[k + 1], blocks)] += part[:, width:]

    @pl.when(step == pl.num_programs(0) - 1)
    def _():
        rows = blocks * width
        scale = SEGMENT_SCALE * lax.rsqrt(squares[...] * (1.0 / rows) + TINY)
        for block in range(blocks):
            out[block] = total[lax.rem(start + block, blocks)].T * scale


def cost(tiles):
    return pl.CostEstimate(flops=0, bytes_accessed=tiles.size // 16, transcendentals=0)


def forward_product(tiles, places, own_half, other_half):
    blocks, kept, width, _ = tiles.shape
    columns = own_half.shape[-1]
    each = blocks // 2
    per = ROWS_PER_STEP
    steps = blocks // per
    whole = pl.BlockSpec((each, width, columns), lambda i, p: (0, 0, 0))
    out = pl.pallas_call(
        forward_kernel,
        out_shape=jax.ShapeDtypeStruct((blocks, width, columns), jnp.float32),
        grid_spec=pltpu.PrefetchScalarGridSpec(
            num_scalar_prefetch=1,
            grid=(steps,),
            in_specs=[
                pl.BlockSpec(
                    (per, kept, width, width),
                    lambda i, p: (lax.rem(i + (1 - p[kept]) * (steps // 2), steps), 0, 0, 0),
                ),
                whole,
                whole,
            ],
            out_specs=pl.BlockSpec((per, width, columns), lambda i, p: (i, 0, 0)),
            scratch_shapes=[pltpu.VMEM((blocks, width, 2 * columns), jnp.bfloat16)],
        ),
        compiler_params=pltpu.CompilerParams(vmem_limit_bytes=VMEM_LIMIT),
        cost_estimate=cost(tiles),
        name="forward_product",
    )(places, tiles, own_half.reshape(each, width, columns), other_half.reshape(each, width, columns))
    return out[:each].reshape(each * width, columns), out[each:].reshape(each * width, columns)


def backward_product(tiles, places, near, turn, exact):
    blocks, kept, width, _ = tiles.shape
    columns = near.shape[-1]
    each = blocks // 2
    per = ROWS_PER_STEP
    steps = blocks // per

    def block(i, p):
        return lax.rem(i + p[kept] * (steps // 2), steps)

    out = pl.pallas_call(
        functools.partial(backward_kernel, exact),
        out_shape=(
            jax.ShapeDtypeStruct((blocks, width, columns), jnp.float32),
            jax.ShapeDtypeStruct((1, columns), jnp.float32),
        ),
        grid_spec=pltpu.PrefetchScalarGridSpec(
            num_scalar_prefetch=1,
            grid=(steps,),
            in_specs=[
                pl.BlockSpec((per, kept, width, width), lambda i, p: (block(i, p), 0, 0, 0)),
                pl.BlockSpec(
                    (per, width, columns), lambda i, p: (i if turn else block(i, p), 0, 0)
                ),
            ],
            out_specs=(
                pl.BlockSpec((blocks, width, columns), lambda i, p: (0, 0, 0)),
                pl.BlockSpec((1, columns), lambda i, p: (0, 0)),
            ),
            scratch_shapes=[pltpu.VMEM((blocks, columns, width), jnp.float32)],
        ),
        compiler_params=pltpu.CompilerParams(vmem_limit_bytes=VMEM_LIMIT),
        cost_estimate=cost(tiles),
        name="backward_product",
    )(places, tiles, near.reshape(blocks, width, columns))[0]
    return out[:each].reshape(each * width, columns), out[each:].reshape(each * width, columns)


AXES = ("row", "half", "line")


def permute(value, place):
    rows = lax.axis_size("row")
    cols = lax.axis_size("half") * lax.axis_size("line")
    pairs = []
    for r in range(rows):
        for c in range(cols):
            to_row, to_col = place(r, c, c ^ (cols // 2))
            pairs.append((r * cols + c, to_row % rows * cols + to_col))
    return lax.ppermute(value, AXES, pairs)


def swap(value):
    return permute(value, lambda r, c, o: (r, o))


def fetch(value):
    own = permute(value, lambda r, c, o: (r - c, c))
    return own, permute(value, lambda r, c, o: (r - o, o))


def give_back(own, other):
    same = permute(own, lambda r, c, o: (r + c, c))
    return same, permute(other, lambda r, c, o: (r + c, o))


def sum_line(partial):
    count = lax.axis_size("line")
    rows, columns = partial.shape
    parts = partial.reshape(count, rows // count, columns)
    parts = lax.all_to_all(parts, "line", 0, 0)
    share = jnp.sum(parts.astype(jnp.float32), axis=0).astype(WIRE)
    copies = jnp.broadcast_to(share[None], parts.shape)
    return lax.all_to_all(copies, "line", 0, 0).reshape(rows, columns)


def segment_values(*values):
    own = jnp.stack(values)
    rows = lax.axis_size("row")
    copies = jnp.broadcast_to(own[None], (2 * rows,) + own.shape)
    found = lax.all_to_all(copies, ("row", "half"), 0, 0).reshape((rows, 2) + own.shape)
    return [found[:, :, k] for k in range(len(values))]


def pick(values, index):
    return lax.dynamic_index_in_dim(values, index, 0, keepdims=True)


def safe_ratio(top, bottom):
    return jnp.where(bottom > 0, top / jnp.where(bottom > 0, bottom, 1.0), 0.0)


def residual_of(vector, weight, product):
    inner = jnp.sum(vector * product, axis=0)
    rest = product - safe_ratio(inner, weight) * vector
    return inner, jnp.sum(rest * rest, axis=0)


def combine(inner, residual, weight, count):
    alpha = jnp.sum(inner, axis=(0, 1)) / count
    shift = safe_ratio(inner, weight) - alpha
    mean_square = jnp.sum(residual + shift * shift * weight, axis=(0, 1)) / count
    return alpha, jnp.sqrt(mean_square + EPS)


def wide(value):
    return value.astype(jnp.float32)


def body(start_block, tiles, band_offsets):
    rows, cols = lax.axis_size("row"), lax.axis_size("half") * lax.axis_size("line")
    row, half, line = lax.axis_index("row"), lax.axis_index("half"), lax.axis_index("line")
    col = half * (cols // 2) + line
    partner = (1 - half) * (cols // 2) + line
    height, columns = start_block.shape
    count = height * rows
    tiles_dev = tiles[0, 0]
    places = jnp.concatenate([band_offsets[0, 0], half[None].astype(jnp.int32)])
    far_row, partner_far_row = lax.rem(row + col, rows), lax.rem(row + partner, rows)
    back_row = lax.rem(row + cols - col, rows)
    partner_back_row = lax.rem(row + cols - partner, rows)
    start_half = lax.dynamic_slice_in_dim(start_block, half * (height // 2), height // 2, 0)

    def scale_of(squares):
        return lax.rsqrt(squares * (1.0 / height) + TINY)

    def ordered(own, other):
        first = jnp.where(half == 0, own, other)
        second = jnp.where(half == 0, other, own)
        return jnp.concatenate([first, second], axis=0)

    own_scale = scale_of(jnp.sum(start_block * start_block, axis=0))
    far = fetch((start_half * (own_scale * SEGMENT_SCALE)).astype(WIRE))
    start_weight = jnp.sum(start_half * start_half, axis=0)
    own, other = backward_product(tiles_dev, places, start_block, False, True)
    own, other, start_weight = lax.optimization_barrier(
        (own.astype(WIRE), other.astype(WIRE), start_weight)
    )
    back = give_back(own, other)
    (weights,) = segment_values(start_weight)
    norm = jnp.sqrt(jnp.sum(weights, axis=(0, 1)) / count + EPS)
    unit = (PRODUCT_SCALE / SEGMENT_SCALE) / (scale_of(jnp.sum(weights, axis=1)) * norm)
    weights = weights / (norm * norm)
    other, own = forward_product(tiles_dev, places, wide(far[0]), wide(far[1]))
    given = swap(other.astype(WIRE))
    first = own * pick(unit, far_row) + wide(given) * pick(unit, partner_far_row)
    first += wide(back[0]) * pick(unit, back_row) + wide(back[1]) * pick(unit, partner_back_row)
    first = first.astype(WIRE)
    product_half = sum_line(first)

    product_rest = swap(product_half)
    far = fetch(product_half)
    near = jnp.concatenate([wide(product_half), wide(product_rest)], axis=0)
    own, other = backward_product(tiles_dev, places, near, True, False)
    own, other, kept_half = lax.optimization_barrier((own.astype(WIRE), other.astype(WIRE), product_half))
    back = give_back(own, other)
    q_first = start_half / norm
    wide_half = wide(kept_half)
    w_first = wide_half * (1.0 / PRODUCT_SCALE)
    weight = start_weight / (norm * norm)
    inner, residual = residual_of(q_first, weight, w_first)
    squares = jnp.sum(wide_half * wide_half, axis=0)
    squares, inner, residual = segment_values(squares, inner, residual)
    alpha_one, beta_one = combine(inner, residual, weights, count)
    scale = SEGMENT_SCALE * scale_of(jnp.sum(squares, axis=1))
    unit = 1.0 / scale
    other, own = forward_product(tiles_dev, places, wide(far[0]), wide(far[1]))
    given = swap((other * pick(scale, far_row)).astype(WIRE))
    second = own + wide(given) * pick(unit, partner_far_row)
    second += wide(back[0]) * pick(unit, back_row) + wide(back[1]) * pick(unit, partner_back_row)
    second = (second - alpha_one * wide(first)) / beta_one
    last_half = sum_line(second.astype(WIRE))

    last_rest = swap(last_half)
    q_second = (w_first - alpha_one * q_first) / beta_one
    w_second = wide(last_half) * (1.0 / PRODUCT_SCALE) - beta_one * q_first
    weight = jnp.sum(q_second * q_second, axis=0)
    inner, residual = residual_of(q_second, weight, w_second)
    inner, residual, weight = segment_values(inner, residual, weight)
    alpha_two, beta_two = combine(inner, residual, weight, count)
    alpha_two, last_rest = lax.optimization_barrier((alpha_two, last_rest))
    q_first = start_block / norm
    q_second = ordered(wide(product_half), wide(product_rest)) * (1.0 / PRODUCT_SCALE)
    q_second = (q_second - alpha_one * q_first) / beta_one
    w_second = ordered(wide(last_half), wide(last_rest)) * (1.0 / PRODUCT_SCALE) - beta_one * q_first
    q_third = (w_second - alpha_two * q_second) / beta_two
    return (jnp.stack([alpha_one, alpha_two]), jnp.stack([beta_one, beta_two]), q_third)


def solution(mesh):
    rows, cols = mesh.devices.shape
    parted = jax.sharding.Mesh(mesh.devices.reshape(rows, 2, cols // 2), AXES)
    split = ("half", "line")
    placed = (P("row", None), P("row", split, None, None, None, None), P("row", split, None))
    return jax.shard_map(
        body, mesh=parted, in_specs=placed, out_specs=(P(), P(), P("row", None)), check_vma=False
    )
```

time: 207 us -> 194 us (0.937)
  blocking collectives: 73.7 us -> 42.8 us
  waiting for transfers between devices: 58.7 us -> 33.6 us
  starting transfers between devices: 31.7 us -> 56.6 us
  Pallas kernels: 18.2 us -> 36.7 us
  local copies, waits for them, and re-layouts: 16.2 us -> 5.11 us
  other arithmetic: 7.03 us -> 16.4 us
    all_to_all x4 -> x3, blocking collectives: 73.7 us -> 42.8 us  [the longest x2 30.9 us: sum_line(): parts = lax.all_to_all(parts, 'line', 0, 0)]
    ppermute x4 -> x12, waiting for transfers between devices: 40.8 us -> 14 us  [permute(): return lax.ppermute(value, AXES, pairs)]
    ppermute x4 -> x12, starting transfers between devices: 7.93 us -> 22.9 us  [permute(): return lax.ppermute(value, AXES, pairs)]
    unnamed x18 -> x2, local copies, waits for them, and re-layouts: 14 us -> 0.01 us
    pallas_call x2, Pallas kernels: 7.58 us -> 17.5 us  [forward_product(): pl.pallas_call(forward_kernel, out_shape=jax.ShapeDtypeStruct((blocks, wi...]
    all_to_all x3 -> x4, starting transfers between devices: 23.8 us -> 33.7 us  [the longest x3 30.3 us: segment_values(): lax.all_to_all(copies, ('row', 'half'), 0, 0).reshape((rows, 2) + own.shape)]
    pallas_call x2, Pallas kernels: 10.6 us -> 19.2 us  [backward_product(): pl.pallas_call(functools.partial(backward_kernel, exact), out_shape=(jax....]
    another operation x2 -> x5, other arithmetic: 0.02 us -> 3.95 us  [row_values(): own = jnp.stack(values)]
  transfers between devices with their start and end apart: 7 -> 16, of which waited for: 5 -> 6; matrix products, arithmetic and copies ran while one was open for 1% -> 7% of each run, Pallas kernels for 4% -> 19%
where the time goes in v2:
time: 194 us; the launch traced here: 192 us
  starting transfers between devices  56.6 us (29%)
  blocking collectives  42.8 us (22%)
  Pallas kernels  36.7 us (19%)
  waiting for transfers between devices  33.6 us (17%)
  other arithmetic  16.4 us (8%)
  local copies, waits for them, and re-layouts  5.11 us (3%)
    all_to_all x2, blocking collectives, sum_line(): parts = lax.all_to_all(parts, 'line', 0, 0)  30.9 us
    all_to_all x3, starting transfers between devices, segment_values(): lax.all_to_all(copies, ('row', 'half'), 0, 0).reshape((rows, 2) + own.shape)  30.3 us
    ppermute x12, starting transfers between devices, permute(): return lax.ppermute(value, AXES, pairs)  22.9 us
    pallas_call x2, Pallas kernels, backward_product(): pl.pallas_call(functools.partial(backward_kernel, exact), out_shape=(jax....  19.2 us
    pallas_call x2, Pallas kernels, forward_product(): pl.pallas_call(forward_kernel, out_shape=jax.ShapeDtypeStruct((blocks, wi...  17.5 us
    ppermute x12, waiting for transfers between devices, permute(): return lax.ppermute(value, AXES, pairs)  14 us
    all_to_all x1, blocking collectives, sum_line(): return lax.all_to_all(copies, 'line', 0, 0).reshape(rows, columns)  11.9 us
    all_to_all x3, waiting for transfers between devices, segment_values(): lax.all_to_all(copies, ('row', 'half'), 0, 0).reshape((rows, 2) + own.shape)  10.2 us
  transfers between devices with their start and end apart: 16, of which 6 were waited for; matrix products, arithmetic and copies ran while one was open for 7% of the time, Pallas kernels for 19%

profile of v2, /device:TPU:1, one launch (start us, length us, event | category | flops | bytes accessed | tf_op | source)
XLA Modules:
  0.0 192.2 jit_solution(2631763223997270434)
XLA Ops:
  0.6 1.5 multiply_reduce_fusion
  2.2 1.2 multiply_reduce_fusion.4
  4.0 6.0 %collective-permute-start.1 = (f16[1024,128]{1,0:T(8,128)(2,1)S(1)}, f16[1024,128]{1,0:T(8,128)(2,1)S(1)}, u32[]{:S(2)}, u32[]{:S(2)}) collective-permute-start(f16[1024,128]{1,0:T(8,128)(2,1)S(1)} %get-tuple-element.32), channel_id=1, source_target_pairs={{0,136},{1,121},{2,106},{3,91},{4,76},{5,61},{6,46},{7,31},{8,0},{... | collective-permute-start | bytes 786440 | tf_op jit(solution)/shard_map/ppermute | solution.py:173
  10.1 1.2 pad_add_fusion.places
  11.3 10.1 %backward_product.2 = (f32[16,128,128]{2,1,0:T(8,128)}, f32[1,128]{1,0:T(1,128)}) custom-call(s32[13]{0:T(128)} %pad_add_fusion.places, bf16[16,12,128,128]{3,2,1,0:T(8,128)(2,1)} %bitcast.98, f32[16,128,128]{2,1,0:T(8,128)} %bitcast.102), custom_call_target="tpu_custom_call" | custom-call | bytes 196608 | tf_op jit(solution)/shard_map/backward_product/pallas_call | solution.py:134
  21.4 1.3 convert.15
  23.5 8.0 %all-to-all-start = ((f32[32,1,128]{2,1,0:T(1,128)}), f32[32,1,128]{2,1,0:T(1,128)S(1)}, u32[]{:S(2)}, u32[]{:S(2)}) async-start(f32[32,1,128]{2,1,0:T(1,128)} %broadcast_in_dim.27), calls=%async_computation | async-start | bytes 32768 | tf_op jit(solution)/shard_map/all_to_all | solution.py:204
  31.5 1.5 collective-permute-start.4
  33.7 4.7 %all-to-all-done = f32[32,1,128]{2,1,0:T(1,128)S(1)} async-done(((f32[32,1,128]{2,1,0:T(1,128)}), f32[32,1,128]{2,1,0:T(1,128)S(1)}, u32[]{:S(2)}, u32[]{:S(2)}) %all-to-all-start) | async-done | bytes 16416 | tf_op jit(solution)/shard_map/all_to_all | solution.py:204
  40.2 8.8 %forward_product.2 = f32[16,128,128]{2,1,0:T(8,128)} custom-call(s32[13]{0:T(128)} %pad_add_fusion.places, bf16[16,12,128,128]{3,2,1,0:T(8,128)(2,1)} %bitcast.99, f32[8,128,128]{2,1,0:T(8,128)} %convert.18.near_half, f32[8,128,128]{2,1,0:T(8,128)} %convert.19.far_half), custom_call_target="tpu_custom_call" | custom-call | bytes 196608 | tf_op jit(solution)/shard_map/forward_product/pallas_call | solution.py:100
  48.9 1.3 slice_convert_fusion
  50.6 6.8 %collective-permute-done.2 = f16[1024,128]{1,0:T(8,128)(2,1)S(1)} collective-permute-done((f16[1024,128]{1,0:T(8,128)(2,1)S(1)}, f16[1024,128]{1,0:T(8,128)(2,1)S(1)}, u32[]{:S(2)}, u32[]{:S(2)}) %collective-permute-start.2) | collective-permute-done | bytes 262176 | tf_op jit(solution)/shard_map/ppermute | solution.py:173
  57.6 17.6 %all_to_all.35 = f16[8,128,128]{2,1,0:T(8,128)(2,1)S(1)} all-to-all(f16[8,128,128]{2,1,0:T(8,128)(2,1)S(1)} %bitcast.112), channel_id=1, replica_groups=mesh['row'=16,'half'=2,'line'=8] {'line'}, dimensions={0} | all-to-all | bytes 524288 | tf_op jit(solution)/shard_map/all_to_all | solution.py:194
  75.3 11.9 %all_to_all.36 = f16[8,128,128]{2,1,0:T(8,128)(2,1)S(1)} all-to-all(f16[8,128,128]{2,1,0:T(8,128)(2,1)S(1)} %broadcast_in_dim.28), channel_id=1, replica_groups=mesh['row'=16,'half'=2,'line'=8] {'line'}, dimensions={0} | all-to-all | bytes 524288 | tf_op jit(solution)/shard_map/all_to_all | solution.py:197
  89.0 4.3 %collective-permute-start.7 = (f16[1024,128]{1,0:T(8,128)(2,1)S(1)}, f16[1024,128]{1,0:T(8,128)(2,1)S(1)}, u32[]{:S(2)}, u32[]{:S(2)}) collective-permute-start(f16[1024,128]{1,0:T(8,128)(2,1)S(1)} %bitcast.105), channel_id=1, source_target_pairs={{0,136},{1,121},{2,106},{3,91},{4,76},{5,61},{6,46},{7,31},{8,0},{... | collective-permute-start | bytes 786440 | tf_op jit(solution)/shard_map/ppermute | solution.py:173
  94.5 9.1 %backward_product.3 = (f32[16,128,128]{2,1,0:T(8,128)}, f32[1,128]{1,0:T(1,128)}) custom-call(s32[13]{0:T(128)} %pad_add_fusion.places, bf16[16,12,128,128]{3,2,1,0:T(8,128)(2,1)} %bitcast.100, f32[16,128,128]{2,1,0:T(8,128)} %bitcast.111), custom_call_target="tpu_custom_call" | custom-call | bytes 196608 | tf_op jit(solution)/shard_map/backward_product/pallas_call | solution.py:134
  103.6 1.3 convert.17
  106.9 11.9 %all-to-all-start.3 = ((f32[32,3,128]{2,1,0:T(4,128)}), f32[32,3,128]{2,1,0:T(4,128)S(1)}, u32[]{:S(2)}, u32[]{:S(2)}) async-start(f32[32,3,128]{2,1,0:T(4,128)} %broadcast_in_dim.30), calls=%async_computation.3 | async-start | bytes 131072 | tf_op jit(solution)/shard_map/all_to_all | solution.py:204
  118.8 1.5 collective-permute-start.10
  120.3 1.6 collective-permute-start.9
  123.6 8.8 %forward_product.3 = f32[16,128,128]{2,1,0:T(8,128)} custom-call(s32[13]{0:T(128)} %pad_add_fusion.places, bf16[16,12,128,128]{3,2,1,0:T(8,128)(2,1)} %bitcast.101, f32[8,128,128]{2,1,0:T(8,128)} %convert.20.near_half, f32[8,128,128]{2,1,0:T(8,128)} %convert.21.far_half), custom_call_target="tpu_custom_call" | custom-call | bytes 196608 | tf_op jit(solution)/shard_map/forward_product/pallas_call | solution.py:100
  132.3 1.3 fusion.39
  133.8 3.2 %collective-permute-start.8 = (f16[1024,128]{1,0:T(8,128)(2,1)S(1)}, f16[1024,128]{1,0:T(8,128)(2,1)S(1)}, u32[]{:S(2)}, u32[]{:S(2)}) collective-permute-start(f16[1024,128]{1,0:T(8,128)(2,1)S(1)} %fusion.15), channel_id=1, source_target_pairs={{0,8},{1,9},{2,10},{3,11},{4,12},{5,13},{6,14},{7,15},{8,0},{9,1},... | collective-permute-start | bytes 786440 | tf_op jit(solution)/shard_map/ppermute | solution.py:173
  137.1 5.8 %collective-permute-done.8 = f16[1024,128]{1,0:T(8,128)(2,1)S(1)} collective-permute-done((f16[1024,128]{1,0:T(8,128)(2,1)S(1)}, f16[1024,128]{1,0:T(8,128)(2,1)S(1)}, u32[]{:S(2)}, u32[]{:S(2)}) %collective-permute-start.8) | collective-permute-done | bytes 262176 | tf_op jit(solution)/shard_map/ppermute | solution.py:173
  143.2 13.3 %all_to_all.37 = f16[8,128,128]{2,1,0:T(8,128)(2,1)S(1)} all-to-all(f16[8,128,128]{2,1,0:T(8,128)(2,1)S(1)} %bitcast.113), channel_id=1, replica_groups=mesh['row'=16,'half'=2,'line'=8] {'line'}, dimensions={0} | all-to-all | bytes 524288 | tf_op jit(solution)/shard_map/all_to_all | solution.py:194
  157.3 3.4 %all-to-all-start.5 = ((f16[8,128,128]{2,1,0:T(8,128)(2,1)}), f16[8,128,128]{2,1,0:T(8,128)(2,1)S(1)}, u32[]{:S(2)}, u32[]{:S(2)}) async-start(f16[8,128,128]{2,1,0:T(8,128)(2,1)} %broadcast_in_dim.32), calls=%async_computation.5 | async-start | bytes 524288 | tf_op jit(solution)/shard_map/all_to_all | solution.py:197
  160.7 9.4 %all-to-all-done.5 = f16[8,128,128]{2,1,0:T(8,128)(2,1)S(1)} async-done(((f16[8,128,128]{2,1,0:T(8,128)(2,1)}), f16[8,128,128]{2,1,0:T(8,128)(2,1)S(1)}, u32[]{:S(2)}, u32[]{:S(2)}) %all-to-all-start.5) | async-done | bytes 262176 | tf_op jit(solution)/shard_map/all_to_all | solution.py:197
  171.3 10.3 %all-to-all-start.6 = ((f32[32,3,128]{2,1,0:T(4,128)}), f32[32,3,128]{2,1,0:T(4,128)S(1)}, u32[]{:S(2)}, u32[]{:S(2)}) async-start(f32[32,3,128]{2,1,0:T(4,128)} %broadcast_in_dim.33), calls=%async_computation.6 | async-start | bytes 131072 | tf_op jit(solution)/shard_map/all_to_all | solution.py:204
  181.8 1.5 collective-permute-start.11
  183.2 5.5 %all-to-all-done.6 = f32[32,3,128]{2,1,0:T(4,128)S(1)} async-done(((f32[32,3,128]{2,1,0:T(4,128)}), f32[32,3,128]{2,1,0:T(4,128)S(1)}, u32[]{:S(2)}, u32[]{:S(2)}) %all-to-all-start.6) | async-done | bytes 49184 | tf_op jit(solution)/shard_map/all_to_all | solution.py:204
  188.9 1.3 collective-permute-done.11
  190.9 1.4 fusion.2
  (68 shorter events, 14.5 us)
Async XLA Ops:
  3.4 35.1 %collective-permute-start = (f16[1024,128]{1,0:T(8,128)(2,1)S(1)}, f16[1024,128]{1,0:T(8,128)(2,1)S(1)}, u32[]{:S(2)}, u32[]{:S(2)}) collective-permute-start(f16[1024,128]{1,0:T(8,128)(2,1)S(1)} %get-tuple-element.32), channel_id=1, source_target_pairs={{0,0},{1,241},{2,226},{3,211},{4,196},{5,181},{6,166},{7,151},{8,1... | collective-permute-start | bytes 786440 | tf_op jit(solution)/shard_map/ppermute | solution.py:173
  4.0 35.3 %collective-permute-start.1 = (f16[1024,128]{1,0:T(8,128)(2,1)S(1)}, f16[1024,128]{1,0:T(8,128)(2,1)S(1)}, u32[]{:S(2)}, u32[]{:S(2)}) collective-permute-start(f16[1024,128]{1,0:T(8,128)(2,1)S(1)} %get-tuple-element.32), channel_id=1, source_target_pairs={{0,136},{1,121},{2,106},{3,91},{4,76},{5,61},{6,46},{7,31},{8,0},{... | collective-permute-start | bytes 786440 | tf_op jit(solution)/shard_map/ppermute | solution.py:173
  23.5 14.9 %all-to-all-start = ((f32[32,1,128]{2,1,0:T(1,128)}), f32[32,1,128]{2,1,0:T(1,128)S(1)}, u32[]{:S(2)}, u32[]{:S(2)}) async-start(f32[32,1,128]{2,1,0:T(1,128)} %broadcast_in_dim.27), calls=%async_computation | async-start | bytes 32768 | tf_op jit(solution)/shard_map/all_to_all | solution.py:204
  31.5 19.1 %collective-permute-start.4 = (f16[1024,128]{1,0:T(8,128)(2,1)S(1)}, f16[1024,128]{1,0:T(8,128)(2,1)S(1)}, u32[]{:S(2)}, u32[]{:S(2)}) collective-permute-start(f16[1024,128]{1,0:T(8,128)(2,1)S(1)} %bitcast.122), channel_id=1, source_target_pairs={{0,8},{1,25},{2,42},{3,59},{4,76},{5,93},{6,110},{7,127},{8,128},{... | collective-permute-start | bytes 786440 | tf_op jit(solution)/shard_map/ppermute | solution.py:173
  33.0 17.6 %collective-permute-start.3 = (f16[1024,128]{1,0:T(8,128)(2,1)S(1)}, f16[1024,128]{1,0:T(8,128)(2,1)S(1)}, u32[]{:S(2)}, u32[]{:S(2)}) collective-permute-start(f16[1024,128]{1,0:T(8,128)(2,1)S(1)} %bitcast.121), channel_id=1, source_target_pairs={{0,0},{1,17},{2,34},{3,51},{4,68},{5,85},{6,102},{7,119},{8,136},{... | collective-permute-start | bytes 786440 | tf_op jit(solution)/shard_map/ppermute | solution.py:173
  50.2 7.2 %collective-permute-start.2 = (f16[1024,128]{1,0:T(8,128)(2,1)S(1)}, f16[1024,128]{1,0:T(8,128)(2,1)S(1)}, u32[]{:S(2)}, u32[]{:S(2)}) collective-permute-start(f16[1024,128]{1,0:T(8,128)(2,1)S(1)} %bitcast.118), channel_id=1, source_target_pairs={{0,8},{1,9},{2,10},{3,11},{4,12},{5,13},{6,14},{7,15},{8,0},{9,1},... | collective-permute-start | bytes 786440 | tf_op jit(solution)/shard_map/ppermute | solution.py:173
  87.2 6.2 %collective-permute-start.5 = (f16[1024,128]{1,0:T(8,128)(2,1)S(1)}, f16[1024,128]{1,0:T(8,128)(2,1)S(1)}, u32[]{:S(2)}, u32[]{:S(2)}) collective-permute-start(f16[1024,128]{1,0:T(8,128)(2,1)S(1)} %bitcast.103), channel_id=1, source_target_pairs={{0,8},{1,9},{2,10},{3,11},{4,12},{5,13},{6,14},{7,15},{8,0},{9,1},... | collective-permute-start | bytes 786440 | tf_op jit(solution)/shard_map/ppermute | solution.py:173
  88.3 33.6 %collective-permute-start.6 = (f16[1024,128]{1,0:T(8,128)(2,1)S(1)}, f16[1024,128]{1,0:T(8,128)(2,1)S(1)}, u32[]{:S(2)}, u32[]{:S(2)}) collective-permute-start(f16[1024,128]{1,0:T(8,128)(2,1)S(1)} %bitcast.104), channel_id=1, source_target_pairs={{0,0},{1,241},{2,226},{3,211},{4,196},{5,181},{6,166},{7,151},{8,1... | collective-permute-start | bytes 786440 | tf_op jit(solution)/shard_map/ppermute | solution.py:173
  89.0 33.7 %collective-permute-start.7 = (f16[1024,128]{1,0:T(8,128)(2,1)S(1)}, f16[1024,128]{1,0:T(8,128)(2,1)S(1)}, u32[]{:S(2)}, u32[]{:S(2)}) collective-permute-start(f16[1024,128]{1,0:T(8,128)(2,1)S(1)} %bitcast.105), channel_id=1, source_target_pairs={{0,136},{1,121},{2,106},{3,91},{4,76},{5,61},{6,46},{7,31},{8,0},{... | collective-permute-start | bytes 786440 | tf_op jit(solution)/shard_map/ppermute | solution.py:173
  93.4 12.5 %copy-start = (f32[2048,128]{1,0:T(8,128)S(1)}, f32[2048,128]{1,0:T(8,128)}, u32[]{:S(2)}) copy-start(f32[2048,128]{1,0:T(8,128)} %param.3) | copy-start | bytes 3145732
  106.9 26.7 %all-to-all-start.3 = ((f32[32,3,128]{2,1,0:T(4,128)}), f32[32,3,128]{2,1,0:T(4,128)S(1)}, u32[]{:S(2)}, u32[]{:S(2)}) async-start(f32[32,3,128]{2,1,0:T(4,128)} %broadcast_in_dim.30), calls=%async_computation.3 | async-start | bytes 131072 | tf_op jit(solution)/shard_map/all_to_all | solution.py:204
  118.8 18.3 %collective-permute-start.10 = (f16[1024,128]{1,0:T(8,128)(2,1)}, f16[1024,128]{1,0:T(8,128)(2,1)S(1)}, u32[]{:S(2)}, u32[]{:S(2)}) collective-permute-start(f16[1024,128]{1,0:T(8,128)(2,1)} %bitcast.19), channel_id=1, source_target_pairs={{0,8},{1,25},{2,42},{3,59},{4,76},{5,93},{6,110},{7,127},{8,128},{... | collective-permute-start | bytes 786440 | tf_op jit(solution)/shard_map/ppermute | solution.py:173
  120.3 16.8 %collective-permute-start.9 = (f16[1024,128]{1,0:T(8,128)(2,1)}, f16[1024,128]{1,0:T(8,128)(2,1)S(1)}, u32[]{:S(2)}, u32[]{:S(2)}) collective-permute-start(f16[1024,128]{1,0:T(8,128)(2,1)} %bitcast.18), channel_id=1, source_target_pairs={{0,0},{1,17},{2,34},{3,51},{4,68},{5,85},{6,102},{7,119},{8,136},{... | collective-permute-start | bytes 786440 | tf_op jit(solution)/shard_map/ppermute | solution.py:173
  133.8 9.1 %collective-permute-start.8 = (f16[1024,128]{1,0:T(8,128)(2,1)S(1)}, f16[1024,128]{1,0:T(8,128)(2,1)S(1)}, u32[]{:S(2)}, u32[]{:S(2)}) collective-permute-start(f16[1024,128]{1,0:T(8,128)(2,1)S(1)} %fusion.15), channel_id=1, source_target_pairs={{0,8},{1,9},{2,10},{3,11},{4,12},{5,13},{6,14},{7,15},{8,0},{9,1},... | collective-permute-start | bytes 786440 | tf_op jit(solution)/shard_map/ppermute | solution.py:173
  157.3 12.8 %all-to-all-start.5 = ((f16[8,128,128]{2,1,0:T(8,128)(2,1)}), f16[8,128,128]{2,1,0:T(8,128)(2,1)S(1)}, u32[]{:S(2)}, u32[]{:S(2)}) async-start(f16[8,128,128]{2,1,0:T(8,128)(2,1)} %broadcast_in_dim.32), calls=%async_computation.5 | async-start | bytes 524288 | tf_op jit(solution)/shard_map/all_to_all | solution.py:197
  171.3 17.4 %all-to-all-start.6 = ((f32[32,3,128]{2,1,0:T(4,128)}), f32[32,3,128]{2,1,0:T(4,128)S(1)}, u32[]{:S(2)}, u32[]{:S(2)}) async-start(f32[32,3,128]{2,1,0:T(4,128)} %broadcast_in_dim.33), calls=%async_computation.6 | async-start | bytes 131072 | tf_op jit(solution)/shard_map/all_to_all | solution.py:204
  181.8 8.5 %collective-permute-start.11 = (f16[1024,128]{1,0:T(8,128)(2,1)S(1)}, f16[1024,128]{1,0:T(8,128)(2,1)S(1)}, u32[]{:S(2)}, u32[]{:S(2)}) collective-permute-start(f16[1024,128]{1,0:T(8,128)(2,1)S(1)} %bitcast.110), channel_id=1, source_target_pairs={{0,8},{1,9},{2,10},{3,11},{4,12},{5,13},{6,14},{7,15},{8,0},{9,1},... | collective-permute-start | bytes 786440 | tf_op jit(solution)/shard_map/ppermute | solution.py:173

commit v3 on v2

v3 whole, which is shorter than its diff:
```python
import functools

import jax
import jax.numpy as jnp
from jax import lax
from jax.experimental import pallas as pl
from jax.experimental.pallas import tpu as pltpu
from jax.sharding import PartitionSpec as P

EPS = 1e-06
TINY = 1e-30
WIRE = jnp.float16
PRODUCT_SCALE = 128.0
SEGMENT_SCALE = 1024.0
ROWS_PER_STEP = 2
VMEM_LIMIT = 24 * 2**20
LOADING_VMEM_LIMIT = 53 * 2**20


def whole_vmem():
    return pl.BlockSpec(memory_space=pltpu.VMEM)


def whole_smem():
    return pl.BlockSpec(memory_space=pltpu.SMEM)


def low_part(value, high):
    return (value - high.astype(jnp.float32)).astype(jnp.bfloat16)


def forward_rows(begin, offsets, tiles, halves, out, factor):
    blocks, width, columns = halves.shape
    columns = columns // 2
    kept = tiles.shape[1]

    @pl.loop(0, out.shape[0] // ROWS_PER_STEP)
    def _(step):
        for local in range(ROWS_PER_STEP):
            at = step * ROWS_PER_STEP + local
            row = begin + at
            total = jnp.zeros((width, 2 * columns), jnp.float32)
            for k in range(0, kept, 2):
                first = halves[lax.rem(row + offsets[k], blocks)]
                second = halves[lax.rem(row + offsets[k + 1], blocks)]
                left = jnp.concatenate([tiles[row, k], tiles[row, k + 1]], axis=1)
                right = jnp.concatenate([first, second], axis=0)
                total += jnp.dot(left, right, preferred_element_type=jnp.float32)
            result = total[:, :columns] + total[:, columns:]
            out[at] = result if factor is None else result * factor


def forward_first_kernel(offsets, half, tiles, own_half, other_half, out, halves):
    each, width, columns = own_half.shape
    start = half[0] * each
    squares = jnp.zeros((1, columns), jnp.float32)
    for block in range(each):
        for source, base in ((own_half, start), (other_half, each - start)):
            value = source[block]
            squares += jnp.sum(value * value, axis=0, keepdims=True)
            high = value.astype(jnp.bfloat16)
            halves[base + block] = jnp.concatenate([high, low_part(value, high)], axis=1)
    factor = SEGMENT_SCALE * lax.rsqrt(squares * (0.5 / (each * width)) + TINY)
    forward_rows(each - start, offsets, tiles, halves, out, factor)


def forward_second_kernel(offsets, half, tiles, halves, out):
    forward_rows(half[0] * out.shape[0], offsets, tiles, halves, out, None)


def backward_rows(row, exact, offsets, tiles, value, squares, total):
    blocks, columns, width = total.shape
    squares[...] += jnp.sum(value * value, axis=0, keepdims=True)
    turned = value.T
    left = turned.astype(jnp.bfloat16)
    if exact:
        left = jnp.concatenate([left, low_part(turned, left)], axis=0)
    for k in range(0, tiles.shape[1], 2):
        right = jnp.concatenate([tiles[row, k], tiles[row, k + 1]], axis=1)
        part = jnp.dot(left, right, preferred_element_type=jnp.float32)
        if exact:
            part = part[:columns] + part[columns:]
        total[lax.rem(row + offsets[k], blocks)] += part[:, :width]
        total[lax.rem(row + offsets[k + 1], blocks)] += part[:, width:]


def backward_result(start, squares, total, given, out):
    blocks, _, width = total.shape
    scale = SEGMENT_SCALE * lax.rsqrt(squares * (1.0 / (blocks * width)) + TINY)
    for block in range(blocks):
        place = lax.rem(start + block, blocks)
        value = total[place] if given is None else total[place] + given[place]
        out[block] = value.T * scale


def backward_loading_kernel(offsets, half, source, near, out, tiles, squares, total, arrived):
    blocks = total.shape[0]
    start = half[0] * (blocks // 2)
    steps = blocks // ROWS_PER_STEP

    def load(step):
        part = pl.ds(step * ROWS_PER_STEP, ROWS_PER_STEP)
        return pltpu.make_async_copy(source.at[part], tiles.at[part], arrived.at[step])

    for step in range(steps):
        load(step).start()
    total[...] = jnp.zeros_like(total)
    squares[...] = jnp.zeros_like(squares)

    @pl.loop(0, steps)
    def _(step):
        load(step).wait()
        for local in range(ROWS_PER_STEP):
            row = step * ROWS_PER_STEP + local
            backward_rows(row, True, offsets, tiles, near[row], squares, total)

    backward_result(start, squares[...], total, None, out)


def backward_first_kernel(offsets, half, tiles, near, total, squares):
    each = near.shape[0]
    total[...] = jnp.zeros_like(total)
    squares[...] = jnp.zeros_like(squares)

    @pl.loop(0, each // ROWS_PER_STEP)
    def _(step):
        for local in range(ROWS_PER_STEP):
            at = step * ROWS_PER_STEP + local
            row = half[0] * each + at
            backward_rows(row, False, offsets, tiles, near[at], squares, total)


def backward_second_kernel(offsets, half, tiles, near, given, given_squares, out, squares, total):
    each = near.shape[0]
    total[...] = jnp.zeros_like(total)
    squares[...] = given_squares[...]

    @pl.loop(0, each // ROWS_PER_STEP)
    def _(step):
        for local in range(ROWS_PER_STEP):
            at = step * ROWS_PER_STEP + local
            row = (1 - half[0]) * each + at
            backward_rows(row, False, offsets, tiles, near[at], squares, total)

    backward_result(half[0] * each, squares[...], total, given, out)


def call(kernel, name, out_shape, scratch, offsets, half, tiles, *values):
    loading = kernel is backward_loading_kernel
    tiles_spec = pl.BlockSpec(memory_space=pl.ANY) if loading else whole_vmem()
    return pl.pallas_call(
        kernel,
        out_shape=out_shape,
        in_specs=[whole_smem(), whole_smem(), tiles_spec] + [whole_vmem()] * len(values),
        out_specs=tuple(whole_vmem() for _ in out_shape),
        scratch_shapes=scratch or [],
        compiler_params=pltpu.CompilerParams(vmem_limit_bytes=LOADING_VMEM_LIMIT if loading else VMEM_LIMIT),
        cost_estimate=pl.CostEstimate(flops=0, bytes_accessed=2**16, transcendentals=0),
        name=name,
    )(offsets, half, tiles, *values)


def forward_product(tiles, offsets, half, own_half, other_half):
    blocks, _, width, _ = tiles.shape
    columns = own_half.shape[-1]
    each = blocks // 2
    shape = (each, width, columns)
    part = jax.ShapeDtypeStruct(shape, jnp.float32)
    other, halves = call(
        forward_first_kernel,
        "forward_first",
        (part, pltpu.VMEM((blocks, width, 2 * columns), jnp.bfloat16)),
        None,
        offsets, half, tiles, own_half.reshape(shape), other_half.reshape(shape),
    )
    (own,) = call(forward_second_kernel, "forward_second", (part,), None, offsets, half, tiles, halves)
    return other.reshape(each * width, columns), own.reshape(each * width, columns)


def in_halves(value):
    each = value.shape[0] // 2
    value = value.reshape(2, each * value.shape[1], value.shape[2])
    return value[0].astype(WIRE), value[1].astype(WIRE)


def backward_loading(tiles, offsets, half, near):
    blocks, _, width, _ = tiles.shape
    columns = near.shape[-1]
    shape = (blocks, width, columns)
    out, kept = call(
        backward_loading_kernel,
        "backward_loading",
        (pltpu.VMEM(shape, jnp.float32), pltpu.VMEM(tiles.shape, tiles.dtype)),
        [
            pltpu.VMEM((1, columns), jnp.float32),
            pltpu.VMEM((blocks, columns, width), jnp.float32),
            pltpu.SemaphoreType.DMA((blocks // ROWS_PER_STEP,)),
        ],
        offsets, half, tiles, near.reshape(shape),
    )
    return in_halves(out), kept


def backward_product(tiles, offsets, half, own_half, other_half):
    blocks, _, width, _ = tiles.shape
    columns = own_half.shape[-1]
    shape = (blocks // 2, width, columns)
    total = (blocks, columns, width)
    given, squares = call(
        backward_first_kernel,
        "backward_first",
        (jax.ShapeDtypeStruct(total, jnp.float32), jax.ShapeDtypeStruct((1, columns), jnp.float32)),
        None,
        offsets, half, tiles, own_half.reshape(shape),
    )
    (out,) = call(
        backward_second_kernel,
        "backward_second",
        (jax.ShapeDtypeStruct((blocks, width, columns), jnp.float32),),
        [pltpu.VMEM((1, columns), jnp.float32), pltpu.VMEM(total, jnp.float32)],
        offsets, half, tiles, other_half.reshape(shape), given, squares,
    )
    return in_halves(out)


AXES = ("row", "half", "line")


def permute(value, place):
    rows = lax.axis_size("row")
    cols = lax.axis_size("half") * lax.axis_size("line")
    pairs = []
    for r in range(rows):
        for c in range(cols):
            to_row, to_col = place(r, c, c ^ (cols // 2))
            pairs.append((r * cols + c, to_row % rows * cols + to_col))
    return lax.ppermute(value, AXES, pairs)


def swap(value):
    return permute(value, lambda r, c, o: (r, o))


def fetch(value):
    own = permute(value, lambda r, c, o: (r - c, c))
    return own, permute(value, lambda r, c, o: (r - o, o))


def give_back(own, other):
    same = permute(own, lambda r, c, o: (r + c, c))
    return same, permute(other, lambda r, c, o: (r + c, o))


def sum_line(partial):
    count = lax.axis_size("line")
    rows, columns = partial.shape
    parts = partial.reshape(count, rows // count, columns)
    parts = lax.all_to_all(parts, "line", 0, 0)
    share = jnp.sum(parts.astype(jnp.float32), axis=0).astype(WIRE)
    copies = jnp.broadcast_to(share[None], parts.shape)
    return lax.all_to_all(copies, "line", 0, 0).reshape(rows, columns)


def segment_values(*values):
    own = jnp.stack(values)
    rows = lax.axis_size("row")
    copies = jnp.broadcast_to(own[None], (2 * rows,) + own.shape)
    found = lax.all_to_all(copies, ("row", "half"), 0, 0).reshape((rows, 2) + own.shape)
    return [found[:, :, k] for k in range(len(values))]


def pick(values, index):
    return lax.dynamic_index_in_dim(values, index, 0, keepdims=True)


def safe_ratio(top, bottom):
    return jnp.where(bottom > 0, top / jnp.where(bottom > 0, bottom, 1.0), 0.0)


def residual_of(vector, weight, product):
    inner = jnp.sum(vector * product, axis=0)
    rest = product - safe_ratio(inner, weight) * vector
    return inner, jnp.sum(rest * rest, axis=0)


def combine(inner, residual, weight, count):
    alpha = jnp.sum(inner, axis=(0, 1)) / count
    shift = safe_ratio(inner, weight) - alpha
    mean_square = jnp.sum(residual + shift * shift * weight, axis=(0, 1)) / count
    return alpha, jnp.sqrt(mean_square + EPS)


def wide(value):
    return value.astype(jnp.float32)


def body(start_block, tiles, band_offsets):
    rows, cols = lax.axis_size("row"), lax.axis_size("half") * lax.axis_size("line")
    row, half, line = lax.axis_index("row"), lax.axis_index("half"), lax.axis_index("line")
    col = half * (cols // 2) + line
    partner = (1 - half) * (cols // 2) + line
    height, columns = start_block.shape
    count = height * rows
    offsets = band_offsets[0, 0]
    place = half[None].astype(jnp.int32)
    far_row, partner_far_row = lax.rem(row + col, rows), lax.rem(row + partner, rows)
    back_row = lax.rem(row + cols - col, rows)
    partner_back_row = lax.rem(row + cols - partner, rows)
    start_half = lax.dynamic_slice_in_dim(start_block, half * (height // 2), height // 2, 0)

    def scale_of(squares):
        return lax.rsqrt(squares * (1.0 / height) + TINY)

    def ordered(own, other):
        first = jnp.where(half == 0, own, other)
        second = jnp.where(half == 0, other, own)
        return jnp.concatenate([first, second], axis=0)

    own_scale = scale_of(jnp.sum(start_block * start_block, axis=0))
    far_own, far_other = fetch((start_half * (own_scale * SEGMENT_SCALE)).astype(WIRE))
    back, kept = backward_loading(tiles[0, 0], offsets, place, start_block)
    back = give_back(*back)
    start_weight = jnp.sum(start_half * start_half, axis=0)
    far_own, start_weight = lax.optimization_barrier((far_own, start_weight))
    (weights,) = segment_values(start_weight)
    norm = jnp.sqrt(jnp.sum(weights, axis=(0, 1)) / count + EPS)
    unit = (PRODUCT_SCALE / SEGMENT_SCALE) / (scale_of(jnp.sum(weights, axis=1)) * norm)
    weights = weights / (norm * norm)
    other, own = forward_product(kept, offsets, place, wide(far_own), wide(far_other))
    given = swap(other.astype(WIRE))
    first = own * pick(unit, far_row) + wide(given) * pick(unit, partner_far_row)
    first += wide(back[0]) * pick(unit, back_row) + wide(back[1]) * pick(unit, partner_back_row)
    first = first.astype(WIRE)
    product_half = sum_line(first)

    product_rest = swap(product_half)
    far_own, far_other = fetch(product_half)
    back = give_back(
        *backward_product(kept, offsets, place, wide(product_half), wide(product_rest))
    )
    far_own, kept_half = lax.optimization_barrier((far_own, product_half))
    q_first = start_half / norm
    wide_half = wide(kept_half)
    w_first = wide_half * (1.0 / PRODUCT_SCALE)
    weight = start_weight / (norm * norm)
    inner, residual = residual_of(q_first, weight, w_first)
    squares = jnp.sum(wide_half * wide_half, axis=0)
    squares, inner, residual = segment_values(squares, inner, residual)
    alpha_one, beta_one = combine(inner, residual, weights, count)
    unit = 1.0 / (SEGMENT_SCALE * scale_of(jnp.sum(squares, axis=1)))
    other, own = forward_product(kept, offsets, place, wide(far_own), wide(far_other))
    given = swap(other.astype(WIRE))
    second = own + wide(given) * pick(unit, partner_far_row)
    second += wide(back[0]) * pick(unit, back_row) + wide(back[1]) * pick(unit, partner_back_row)
    second = (second - alpha_one * wide(first)) / beta_one
    last_half = sum_line(second.astype(WIRE))

    last_rest = swap(last_half)
    q_second = (w_first - alpha_one * q_first) / beta_one
    w_second = wide(last_half) * (1.0 / PRODUCT_SCALE) - beta_one * q_first
    weight = jnp.sum(q_second * q_second, axis=0)
    inner, residual = residual_of(q_second, weight, w_second)
    inner, residual, weight = segment_values(inner, residual, weight)
    alpha_two, beta_two = combine(inner, residual, weight, count)
    q_first = start_block / norm
    q_second = ordered(wide(product_half), wide(product_rest)) * (1.0 / PRODUCT_SCALE)
    q_second = (q_second - alpha_one * q_first) / beta_one
    w_second = ordered(wide(last_half), wide(last_rest)) * (1.0 / PRODUCT_SCALE) - beta_one * q_first
    q_third = (w_second - alpha_two * q_second) / beta_two
    return (jnp.stack([alpha_one, alpha_two]), jnp.stack([beta_one, beta_two]), q_third)


def solution(mesh):
    rows, cols = mesh.devices.shape
    parted = jax.sharding.Mesh(mesh.devices.reshape(rows, 2, cols // 2), AXES)
    split = ("half", "line")
    placed = (P("row", None), P("row", split, None, None, None, None), P("row", split, None))
    return jax.shard_map(
        body, mesh=parted, in_specs=placed, out_specs=(P(), P(), P("row", None)), check_vma=False
    )
```

time: 194 us -> 185 us (0.954)
  blocking collectives: 42.8 us -> 67.1 us
  Pallas kernels: 36.7 us -> 21.7 us
  waiting for transfers between devices: 33.6 us -> 19.9 us
  local copies, waits for them, and re-layouts: 5.11 us -> 14.6 us
  other arithmetic: 16.4 us -> 8.1 us
  starting transfers between devices: 56.6 us -> 51.3 us
    pallas_call x4 -> x7, Pallas kernels: 36.7 us -> 21.7 us  [call(): pl.pallas_call(kernel, out_shape=out_shape, in_specs=[whole_smem(), whole...]
    all_to_all x2, blocking collectives: 30.9 us -> 43.5 us  [sum_line(): parts = lax.all_to_all(parts, 'line', 0, 0)]
    all_to_all x1 -> x2, blocking collectives: 11.9 us -> 23.6 us  [sum_line(): return lax.all_to_all(copies, 'line', 0, 0).reshape(rows, columns)]
    unnamed x2 -> x14, local copies, waits for them, and re-layouts: 0.01 us -> 11.7 us
    all_to_all x1 -> x0, waiting for transfers between devices: 9.39 us -> none  [sum_line(): return lax.all_to_all(copies, 'line', 0, 0).reshape(rows, columns)]
    all_to_all x3, starting transfers between devices: 30.3 us -> 26 us  [segment_values(): lax.all_to_all(copies, ('row', 'half'), 0, 0).reshape((rows, 2) + own.shape)]
    all_to_all x3, waiting for transfers between devices: 10.2 us -> 6.07 us  [segment_values(): lax.all_to_all(copies, ('row', 'half'), 0, 0).reshape((rows, 2) + own.shape)]
    another operation x3 -> x2, other arithmetic: 3.92 us -> 0.2 us
  transfers between devices with their start and end apart: 16 -> 15, of which waited for: 6 -> 4; matrix products, arithmetic and copies ran while one was open for 7% -> 2% of each run, Pallas kernels for 19% -> 12%
where the time goes in v3:
time: 185 us; the launch traced here: 184 us
  blocking collectives  67.1 us (36%)
  starting transfers between devices  51.3 us (28%)
  Pallas kernels  21.7 us (12%)
  waiting for transfers between devices  19.9 us (11%)
  local copies, waits for them, and re-layouts  14.6 us (8%)
  other arithmetic  8.1 us (4%)
    all_to_all x2, blocking collectives, sum_line(): parts = lax.all_to_all(parts, 'line', 0, 0)  43.5 us
    all_to_all x3, starting transfers between devices, segment_values(): lax.all_to_all(copies, ('row', 'half'), 0, 0).reshape((rows, 2) + own.shape)  26 us
    ppermute x12, starting transfers between devices, permute(): return lax.ppermute(value, AXES, pairs)  25.3 us
    all_to_all x2, blocking collectives, sum_line(): return lax.all_to_all(copies, 'line', 0, 0).reshape(rows, columns)  23.6 us
    pallas_call x7, Pallas kernels, call(): pl.pallas_call(kernel, out_shape=out_shape, in_specs=[whole_smem(), whole...  21.7 us
    ppermute x12, waiting for transfers between devices, permute(): return lax.ppermute(value, AXES, pairs)  13.8 us
    unnamed x14, local copies, waits for them, and re-layouts  11.7 us
    all_to_all x3, waiting for transfers between devices, segment_values(): lax.all_to_all(copies, ('row', 'half'), 0, 0).reshape((rows, 2) + own.shape)  6.07 us
  transfers between devices with their start and end apart: 15, of which 4 were waited for; matrix products, arithmetic and copies ran while one was open for 2% of the time, Pallas kernels for 12%

profile of v3, /device:TPU:1, one launch (start us, length us, event | category | flops | bytes accessed | tf_op | source)
XLA Modules:
  0.0 183.9 jit_solution(14160552509661908063)
XLA Ops:
  0.6 1.5 multiply_reduce_fusion
  2.2 1.2 multiply_reduce_fusion.4
  4.0 6.0 %collective-permute-start.1 = (f16[1024,128]{1,0:T(8,128)(2,1)S(1)}, f16[1024,128]{1,0:T(8,128)(2,1)S(1)}, u32[]{:S(2)}, u32[]{:S(2)}) collective-permute-start(f16[1024,128]{1,0:T(8,128)(2,1)S(1)} %get-tuple-element.32), channel_id=1, source_target_pairs={{0,136},{1,121},{2,106},{3,91},{4,76},{5,61},{6,46},{7,31},{8,0},{... | collective-permute-start | bytes 786440 | tf_op jit(solution)/shard_map/ppermute | solution.py:237
  10.1 7.9 %backward_loading.1 = (f32[16,128,128]{2,1,0:T(8,128)S(1)}, bf16[16,12,128,128]{3,2,1,0:T(8,128)(2,1)S(1)}) custom-call(s32[12]{0:T(128)} %bitcast.94, s32[1]{0:T(128)} %bitcast.1.half, bf16[16,12,128,128]{3,2,1,0:T(8,128)(2,1)} %bitcast.109, f32[16,128,128]{2,1,0:T(8,128)} %bitcast.101), custom_call_target="tpu_custom_call" | custom-call | bytes 65536 | tf_op jit(solution)/shard_map/backward_loading/pallas_call | solution.py:151
  18.0 2.7 %copy-done = bf16[16,12,128,128]{3,2,1,0:T(8,128)(2,1)} copy-done((bf16[16,12,128,128]{3,2,1,0:T(8,128)(2,1)}, bf16[16,12,128,128]{3,2,1,0:T(8,128)(2,1)S(1)}, u32[]{:S(2)}) %copy-start) | copy-done | bytes 6291480
  21.3 8.0 %all-to-all-start = ((f32[32,1,128]{2,1,0:T(1,128)}), f32[32,1,128]{2,1,0:T(1,128)S(1)}, u32[]{:S(2)}, u32[]{:S(2)}) async-start(f32[32,1,128]{2,1,0:T(1,128)} %broadcast_in_dim.27), calls=%async_computation | async-start | bytes 32768 | tf_op jit(solution)/shard_map/all_to_all | solution.py:268
  29.5 1.5 collective-permute-start.4
  31.8 2.8 %copy-done.1 = bf16[16,12,128,128]{3,2,1,0:T(8,128)(2,1)S(1)} copy-done((bf16[16,12,128,128]{3,2,1,0:T(8,128)(2,1)S(1)}, bf16[16,12,128,128]{3,2,1,0:T(8,128)(2,1)}, u32[]{:S(2)}) %copy-start.1) | copy-done | bytes 6291480
  34.6 2.3 %forward_first.2 = (f32[8,128,128]{2,1,0:T(8,128)S(1)}, bf16[16,128,256]{2,1,0:T(8,128)(2,1)S(1)}) custom-call(s32[12]{0:T(128)S(1)} %bitcast.95, s32[1]{0:T(128)} %bitcast.1.half, bf16[16,12,128,128]{3,2,1,0:T(8,128)(2,1)S(1)} %copy-done.1, f32[8,128,128]{2,1,0:T(8,128)S(1)} %convert.14.own_half, f32[8,128,128]{2,1,0:T(8,128)S(1)} %convert.15.other_half), custom_call_target="tpu_custom_call" | custom-call | bytes 65536 | tf_op jit(solution)/shard_map/forward_first/pallas_call | solution.py:151
  36.9 2.1 %forward_second.2 = f32[8,128,128]{2,1,0:T(8,128)S(1)} custom-call(s32[12]{0:T(128)S(1)} %bitcast.96, s32[1]{0:T(128)} %bitcast.1.half, bf16[16,12,128,128]{3,2,1,0:T(8,128)(2,1)S(1)} %copy-done.1, bf16[16,128,256]{2,1,0:T(8,128)(2,1)S(1)} %get-tuple-element.17.halves), custom_call_target="tpu_custom_call" | custom-call | bytes 65536 | tf_op jit(solution)/shard_map/forward_second/pallas_call | solution.py:151
  39.0 4.1 %collective-permute-start.2 = (f16[1024,128]{1,0:T(8,128)(2,1)S(1)}, f16[1024,128]{1,0:T(8,128)(2,1)S(1)}, u32[]{:S(2)}, u32[]{:S(2)}) collective-permute-start(f16[1024,128]{1,0:T(8,128)(2,1)S(1)} %bitcast.119), channel_id=1, source_target_pairs={{0,8},{1,9},{2,10},{3,11},{4,12},{5,13},{6,14},{7,15},{8,0},{9,1},... | collective-permute-start | bytes 786440 | tf_op jit(solution)/shard_map/ppermute | solution.py:237
  43.3 5.7 %collective-permute-done.2 = f16[1024,128]{1,0:T(8,128)(2,1)S(1)} collective-permute-done((f16[1024,128]{1,0:T(8,128)(2,1)S(1)}, f16[1024,128]{1,0:T(8,128)(2,1)S(1)}, u32[]{:S(2)}, u32[]{:S(2)}) %collective-permute-start.2) | collective-permute-done | bytes 262176 | tf_op jit(solution)/shard_map/ppermute | solution.py:237
  49.2 22.9 %all_to_all.35 = f16[8,128,128]{2,1,0:T(8,128)(2,1)S(1)} all-to-all(f16[8,128,128]{2,1,0:T(8,128)(2,1)S(1)} %bitcast.110), channel_id=1, replica_groups=mesh['row'=16,'half'=2,'line'=8] {'line'}, dimensions={0} | all-to-all | bytes 524288 | tf_op jit(solution)/shard_map/all_to_all | solution.py:258
  72.2 11.7 %all_to_all.36 = f16[8,128,128]{2,1,0:T(8,128)(2,1)S(1)} all-to-all(f16[8,128,128]{2,1,0:T(8,128)(2,1)S(1)} %broadcast_in_dim.28), channel_id=1, replica_groups=mesh['row'=16,'half'=2,'line'=8] {'line'}, dimensions={0} | all-to-all | bytes 524288 | tf_op jit(solution)/shard_map/all_to_all | solution.py:261
  84.5 1.9 %collective-permute-start.8 = (f16[1024,128]{1,0:T(8,128)(2,1)S(1)}, f16[1024,128]{1,0:T(8,128)(2,1)S(1)}, u32[]{:S(2)}, u32[]{:S(2)}) collective-permute-start(f16[1024,128]{1,0:T(8,128)(2,1)S(1)} %bitcast.103), channel_id=1, source_target_pairs={{0,8},{1,9},{2,10},{3,11},{4,12},{5,13},{6,14},{7,15},{8,0},{9,1},... | collective-permute-start | bytes 786440 | tf_op jit(solution)/shard_map/ppermute | solution.py:237
  86.4 2.7 %collective-permute-start.6 = (f16[1024,128]{1,0:T(8,128)(2,1)S(1)}, f16[1024,128]{1,0:T(8,128)(2,1)S(1)}, u32[]{:S(2)}, u32[]{:S(2)}) collective-permute-start(f16[1024,128]{1,0:T(8,128)(2,1)S(1)} %bitcast.104), channel_id=1, source_target_pairs={{0,136},{1,121},{2,106},{3,91},{4,76},{5,61},{6,46},{7,31},{8,0},{... | collective-permute-start | bytes 786440 | tf_op jit(solution)/shard_map/ppermute | solution.py:237
  89.2 2.8 %copy-done.2 = bf16[16,12,128,128]{3,2,1,0:T(8,128)(2,1)S(1)} copy-done((bf16[16,12,128,128]{3,2,1,0:T(8,128)(2,1)S(1)}, bf16[16,12,128,128]{3,2,1,0:T(8,128)(2,1)}, u32[]{:S(2)}) %copy-start.2) | copy-done | bytes 6291480
  92.0 2.4 %backward_first.1 = (f32[16,128,128]{2,1,0:T(8,128)S(1)}, f32[1,128]{1,0:T(1,128)S(1)}) custom-call(s32[12]{0:T(128)S(1)} %bitcast.97, s32[1]{0:T(128)} %bitcast.1.half, bf16[16,12,128,128]{3,2,1,0:T(8,128)(2,1)S(1)} %copy-done.2, f32[8,128,128]{2,1,0:T(8,128)S(1)} %convert_element_type.119.near), custom_call_target="tpu_custom_call" | custom-call | bytes 65536 | tf_op jit(solution)/shard_map/backward_first/pallas_call | solution.py:151
  95.5 2.7 %backward_second.1 = f32[16,128,128]{2,1,0:T(8,128)S(1)} custom-call(s32[12]{0:T(128)S(1)} %bitcast.98, s32[1]{0:T(128)} %bitcast.1.half, bf16[16,12,128,128]{3,2,1,0:T(8,128)(2,1)S(1)} %copy-done.2, f32[8,128,128]{2,1,0:T(8,128)S(1)} %convert.20.near, f32[16,128,128]{2,1,0:T(8,128)S(1)} %get-tuple-element.25.given, f32[1,128]{1,0:T(1,128)S(1)} %get-tuple-element.26.given_squares), custom_call_target="tpu_custom_call" | custom-call | bytes 65536 | tf_op jit(solution)/shard_map/backward_second/pallas_call | solution.py:151
  99.0 8.5 %all-to-all-start.3 = ((f32[32,3,128]{2,1,0:T(4,128)}), f32[32,3,128]{2,1,0:T(4,128)S(1)}, u32[]{:S(2)}, u32[]{:S(2)}) async-start(f32[32,3,128]{2,1,0:T(4,128)} %broadcast_in_dim.30), calls=%async_computation.3 | async-start | bytes 131072 | tf_op jit(solution)/shard_map/all_to_all | solution.py:268
  108.3 1.4 collective-permute-start.10
  110.5 2.8 %copy-done.3 = bf16[16,12,128,128]{3,2,1,0:T(8,128)(2,1)S(1)} copy-done((bf16[16,12,128,128]{3,2,1,0:T(8,128)(2,1)S(1)}, bf16[16,12,128,128]{3,2,1,0:T(8,128)(2,1)}, u32[]{:S(2)}) %copy-start.3) | copy-done | bytes 6291480
  113.3 2.3 %forward_first.3 = (f32[8,128,128]{2,1,0:T(8,128)S(1)}, bf16[16,128,256]{2,1,0:T(8,128)(2,1)S(1)}) custom-call(s32[12]{0:T(128)S(1)} %bitcast.99, s32[1]{0:T(128)} %bitcast.1.half, bf16[16,12,128,128]{3,2,1,0:T(8,128)(2,1)S(1)} %copy-done.3, f32[8,128,128]{2,1,0:T(8,128)S(1)} %convert.16.own_half, f32[8,128,128]{2,1,0:T(8,128)S(1)} %convert.17.other_half), custom_call_target="tpu_custom_call" | custom-call | bytes 65536 | tf_op jit(solution)/shard_map/forward_first/pallas_call | solution.py:151
  115.6 4.3 %collective-permute-start.7 = (f16[1024,128]{1,0:T(8,128)(2,1)S(1)}, f16[1024,128]{1,0:T(8,128)(2,1)S(1)}, u32[]{:S(2)}, u32[]{:S(2)}) collective-permute-start(f16[1024,128]{1,0:T(8,128)(2,1)S(1)} %bitcast.118), channel_id=1, source_target_pairs={{0,8},{1,9},{2,10},{3,11},{4,12},{5,13},{6,14},{7,15},{8,0},{9,1},... | collective-permute-start | bytes 786440 | tf_op jit(solution)/shard_map/ppermute | solution.py:237
  119.9 2.1 %forward_second.3 = f32[8,128,128]{2,1,0:T(8,128)S(1)} custom-call(s32[12]{0:T(128)S(1)} %bitcast.100, s32[1]{0:T(128)} %bitcast.1.half, bf16[16,12,128,128]{3,2,1,0:T(8,128)(2,1)S(1)} %copy-done.3, bf16[16,128,256]{2,1,0:T(8,128)(2,1)S(1)} %get-tuple-element.23.halves), custom_call_target="tpu_custom_call" | custom-call | bytes 65536 | tf_op jit(solution)/shard_map/forward_second/pallas_call | solution.py:151
  122.2 3.6 %collective-permute-done.7 = f16[1024,128]{1,0:T(8,128)(2,1)S(1)} collective-permute-done((f16[1024,128]{1,0:T(8,128)(2,1)S(1)}, f16[1024,128]{1,0:T(8,128)(2,1)S(1)}, u32[]{:S(2)}, u32[]{:S(2)}) %collective-permute-start.7) | collective-permute-done | bytes 262176 | tf_op jit(solution)/shard_map/ppermute | solution.py:237
  126.1 20.7 %all_to_all.37 = f16[8,128,128]{2,1,0:T(8,128)(2,1)S(1)} all-to-all(f16[8,128,128]{2,1,0:T(8,128)(2,1)S(1)} %bitcast.112), channel_id=1, replica_groups=mesh['row'=16,'half'=2,'line'=8] {'line'}, dimensions={0} | all-to-all | bytes 524288 | tf_op jit(solution)/shard_map/all_to_all | solution.py:258
  146.8 11.9 %all_to_all.38 = f16[8,128,128]{2,1,0:T(8,128)(2,1)S(1)} all-to-all(f16[8,128,128]{2,1,0:T(8,128)(2,1)S(1)} %broadcast_in_dim.32), channel_id=1, replica_groups=mesh['row'=16,'half'=2,'line'=8] {'line'}, dimensions={0} | all-to-all | bytes 524288 | tf_op jit(solution)/shard_map/all_to_all | solution.py:261
  159.5 4.5 %collective-permute-done.11 = f16[1024,128]{1,0:T(8,128)(2,1)S(1)} collective-permute-done((f16[1024,128]{1,0:T(8,128)(2,1)S(1)}, f16[1024,128]{1,0:T(8,128)(2,1)S(1)}, u32[]{:S(2)}, u32[]{:S(2)}) %collective-permute-start.11) | collective-permute-done | bytes 262176 | tf_op jit(solution)/shard_map/ppermute | solution.py:237
  165.2 9.5 %all-to-all-start.6 = ((f32[32,3,128]{2,1,0:T(4,128)}), f32[32,3,128]{2,1,0:T(4,128)S(1)}, u32[]{:S(2)}, u32[]{:S(2)}) async-start(f32[32,3,128]{2,1,0:T(4,128)} %broadcast_in_dim.33), calls=%async_computation.6 | async-start | bytes 131072 | tf_op jit(solution)/shard_map/all_to_all | solution.py:268
  175.8 6.1 %all-to-all-done.6 = f32[32,3,128]{2,1,0:T(4,128)S(1)} async-done(((f32[32,3,128]{2,1,0:T(4,128)}), f32[32,3,128]{2,1,0:T(4,128)S(1)}, u32[]{:S(2)}, u32[]{:S(2)}) %all-to-all-start.6) | async-done | bytes 49184 | tf_op jit(solution)/shard_map/all_to_all | solution.py:268
  182.6 1.4 fusion.2
  (77 shorter events, 11.2 us)
Async XLA Ops:
  2.1 29.6 %copy-start.4 = (s32[1,1,12]{2,1,0:T(1,128)S(1)}, s32[1,1,12]{2,1,0:T(1,128)}, u32[]{:S(2)}) copy-start(s32[1,1,12]{2,1,0:T(1,128)} %param.5) | copy-start | bytes 148
  3.4 17.4 %collective-permute-start = (f16[1024,128]{1,0:T(8,128)(2,1)S(1)}, f16[1024,128]{1,0:T(8,128)(2,1)S(1)}, u32[]{:S(2)}, u32[]{:S(2)}) collective-permute-start(f16[1024,128]{1,0:T(8,128)(2,1)S(1)} %get-tuple-element.32), channel_id=1, source_target_pairs={{0,0},{1,241},{2,226},{3,211},{4,196},{5,181},{6,166},{7,151},{8,1... | collective-permute-start | bytes 786440 | tf_op jit(solution)/shard_map/ppermute | solution.py:237
  4.0 27.7 %collective-permute-start.1 = (f16[1024,128]{1,0:T(8,128)(2,1)S(1)}, f16[1024,128]{1,0:T(8,128)(2,1)S(1)}, u32[]{:S(2)}, u32[]{:S(2)}) collective-permute-start(f16[1024,128]{1,0:T(8,128)(2,1)S(1)} %get-tuple-element.32), channel_id=1, source_target_pairs={{0,136},{1,121},{2,106},{3,91},{4,76},{5,61},{6,46},{7,31},{8,0},{... | collective-permute-start | bytes 786440 | tf_op jit(solution)/shard_map/ppermute | solution.py:237
  17.9 2.7 %copy-start = (bf16[16,12,128,128]{3,2,1,0:T(8,128)(2,1)}, bf16[16,12,128,128]{3,2,1,0:T(8,128)(2,1)S(1)}, u32[]{:S(2)}) copy-start(bf16[16,12,128,128]{3,2,1,0:T(8,128)(2,1)S(1)} %get-tuple-element.15.tiles) | copy-start | bytes 18874372
  21.3 21.8 %all-to-all-start = ((f32[32,1,128]{2,1,0:T(1,128)}), f32[32,1,128]{2,1,0:T(1,128)S(1)}, u32[]{:S(2)}, u32[]{:S(2)}) async-start(f32[32,1,128]{2,1,0:T(1,128)} %broadcast_in_dim.27), calls=%async_computation | async-start | bytes 32768 | tf_op jit(solution)/shard_map/all_to_all | solution.py:268
  29.5 13.7 %collective-permute-start.4 = (f16[1024,128]{1,0:T(8,128)(2,1)S(1)}, f16[1024,128]{1,0:T(8,128)(2,1)S(1)}, u32[]{:S(2)}, u32[]{:S(2)}) collective-permute-start(f16[1024,128]{1,0:T(8,128)(2,1)S(1)} %bitcast.123), channel_id=1, source_target_pairs={{0,8},{1,25},{2,42},{3,59},{4,76},{5,93},{6,110},{7,127},{8,128},{... | collective-permute-start | bytes 786440 | tf_op jit(solution)/shard_map/ppermute | solution.py:237
  31.0 12.3 %collective-permute-start.3 = (f16[1024,128]{1,0:T(8,128)(2,1)S(1)}, f16[1024,128]{1,0:T(8,128)(2,1)S(1)}, u32[]{:S(2)}, u32[]{:S(2)}) collective-permute-start(f16[1024,128]{1,0:T(8,128)(2,1)S(1)} %bitcast.122), channel_id=1, source_target_pairs={{0,0},{1,17},{2,34},{3,51},{4,68},{5,85},{6,102},{7,119},{8,136},{... | collective-permute-start | bytes 786440 | tf_op jit(solution)/shard_map/ppermute | solution.py:237
  31.8 2.8 %copy-start.1 = (bf16[16,12,128,128]{3,2,1,0:T(8,128)(2,1)S(1)}, bf16[16,12,128,128]{3,2,1,0:T(8,128)(2,1)}, u32[]{:S(2)}) copy-start(bf16[16,12,128,128]{3,2,1,0:T(8,128)(2,1)} %copy-done) | copy-start | bytes 18874372
  39.0 55.4 %copy-start.5 = (f32[2048,128]{1,0:T(8,128)S(1)}, f32[2048,128]{1,0:T(8,128)}, u32[]{:S(2)}) copy-start(f32[2048,128]{1,0:T(8,128)} %param.3) | copy-start | bytes 3145732
  39.0 10.0 %collective-permute-start.2 = (f16[1024,128]{1,0:T(8,128)(2,1)S(1)}, f16[1024,128]{1,0:T(8,128)(2,1)S(1)}, u32[]{:S(2)}, u32[]{:S(2)}) collective-permute-start(f16[1024,128]{1,0:T(8,128)(2,1)S(1)} %bitcast.119), channel_id=1, source_target_pairs={{0,8},{1,9},{2,10},{3,11},{4,12},{5,13},{6,14},{7,15},{8,0},{9,1},... | collective-permute-start | bytes 786440 | tf_op jit(solution)/shard_map/ppermute | solution.py:237
  83.9 10.5 %collective-permute-start.5 = (f16[1024,128]{1,0:T(8,128)(2,1)S(1)}, f16[1024,128]{1,0:T(8,128)(2,1)S(1)}, u32[]{:S(2)}, u32[]{:S(2)}) collective-permute-start(f16[1024,128]{1,0:T(8,128)(2,1)S(1)} %bitcast.102), channel_id=1, source_target_pairs={{0,0},{1,241},{2,226},{3,211},{4,196},{5,181},{6,166},{7,151},{8,1... | collective-permute-start | bytes 786440 | tf_op jit(solution)/shard_map/ppermute | solution.py:237
  84.5 10.3 %collective-permute-start.8 = (f16[1024,128]{1,0:T(8,128)(2,1)S(1)}, f16[1024,128]{1,0:T(8,128)(2,1)S(1)}, u32[]{:S(2)}, u32[]{:S(2)}) collective-permute-start(f16[1024,128]{1,0:T(8,128)(2,1)S(1)} %bitcast.103), channel_id=1, source_target_pairs={{0,8},{1,9},{2,10},{3,11},{4,12},{5,13},{6,14},{7,15},{8,0},{9,1},... | collective-permute-start | bytes 786440 | tf_op jit(solution)/shard_map/ppermute | solution.py:237
  86.4 24.0 %collective-permute-start.6 = (f16[1024,128]{1,0:T(8,128)(2,1)S(1)}, f16[1024,128]{1,0:T(8,128)(2,1)S(1)}, u32[]{:S(2)}, u32[]{:S(2)}) collective-permute-start(f16[1024,128]{1,0:T(8,128)(2,1)S(1)} %bitcast.104), channel_id=1, source_target_pairs={{0,136},{1,121},{2,106},{3,91},{4,76},{5,61},{6,46},{7,31},{8,0},{... | collective-permute-start | bytes 786440 | tf_op jit(solution)/shard_map/ppermute | solution.py:237
  89.2 2.8 %copy-start.2 = (bf16[16,12,128,128]{3,2,1,0:T(8,128)(2,1)S(1)}, bf16[16,12,128,128]{3,2,1,0:T(8,128)(2,1)}, u32[]{:S(2)}) copy-start(bf16[16,12,128,128]{3,2,1,0:T(8,128)(2,1)} %copy-done) | copy-start | bytes 18874372
  94.8 0.7 copy-start.6
  99.0 23.0 %all-to-all-start.3 = ((f32[32,3,128]{2,1,0:T(4,128)}), f32[32,3,128]{2,1,0:T(4,128)S(1)}, u32[]{:S(2)}, u32[]{:S(2)}) async-start(f32[32,3,128]{2,1,0:T(4,128)} %broadcast_in_dim.30), calls=%async_computation.3 | async-start | bytes 131072 | tf_op jit(solution)/shard_map/all_to_all | solution.py:268
  108.3 13.9 %collective-permute-start.10 = (f16[1024,128]{1,0:T(8,128)(2,1)}, f16[1024,128]{1,0:T(8,128)(2,1)S(1)}, u32[]{:S(2)}, u32[]{:S(2)}) collective-permute-start(f16[1024,128]{1,0:T(8,128)(2,1)} %bitcast.32), channel_id=1, source_target_pairs={{0,8},{1,25},{2,42},{3,59},{4,76},{5,93},{6,110},{7,127},{8,128},{... | collective-permute-start | bytes 786440 | tf_op jit(solution)/shard_map/ppermute | solution.py:237
  109.7 12.5 %collective-permute-start.9 = (f16[1024,128]{1,0:T(8,128)(2,1)S(1)}, f16[1024,128]{1,0:T(8,128)(2,1)S(1)}, u32[]{:S(2)}, u32[]{:S(2)}) collective-permute-start(f16[1024,128]{1,0:T(8,128)(2,1)S(1)} %bitcast.124), channel_id=1, source_target_pairs={{0,0},{1,17},{2,34},{3,51},{4,68},{5,85},{6,102},{7,119},{8,136},{... | collective-permute-start | bytes 786440 | tf_op jit(solution)/shard_map/ppermute | solution.py:237
  110.5 2.8 %copy-start.3 = (bf16[16,12,128,128]{3,2,1,0:T(8,128)(2,1)S(1)}, bf16[16,12,128,128]{3,2,1,0:T(8,128)(2,1)}, u32[]{:S(2)}) copy-start(bf16[16,12,128,128]{3,2,1,0:T(8,128)(2,1)} %copy-done) | copy-start | bytes 18874372
  115.6 10.2 %collective-permute-start.7 = (f16[1024,128]{1,0:T(8,128)(2,1)S(1)}, f16[1024,128]{1,0:T(8,128)(2,1)S(1)}, u32[]{:S(2)}, u32[]{:S(2)}) collective-permute-start(f16[1024,128]{1,0:T(8,128)(2,1)S(1)} %bitcast.118), channel_id=1, source_target_pairs={{0,8},{1,9},{2,10},{3,11},{4,12},{5,13},{6,14},{7,15},{8,0},{9,1},... | collective-permute-start | bytes 786440 | tf_op jit(solution)/shard_map/ppermute | solution.py:237
  158.8 5.2 %collective-permute-start.11 = (f16[1024,128]{1,0:T(8,128)(2,1)S(1)}, f16[1024,128]{1,0:T(8,128)(2,1)S(1)}, u32[]{:S(2)}, u32[]{:S(2)}) collective-permute-start(f16[1024,128]{1,0:T(8,128)(2,1)S(1)} %bitcast.111), channel_id=1, source_target_pairs={{0,8},{1,9},{2,10},{3,11},{4,12},{5,13},{6,14},{7,15},{8,0},{9,1},... | collective-permute-start | bytes 786440 | tf_op jit(solution)/shard_map/ppermute | solution.py:237
  165.2 16.6 %all-to-all-start.6 = ((f32[32,3,128]{2,1,0:T(4,128)}), f32[32,3,128]{2,1,0:T(4,128)S(1)}, u32[]{:S(2)}, u32[]{:S(2)}) async-start(f32[32,3,128]{2,1,0:T(4,128)} %broadcast_in_dim.33), calls=%async_computation.6 | async-start | bytes 131072 | tf_op jit(solution)/shard_map/all_to_all | solution.py:268

commit v4 on v3

v4 whole, which is shorter than its diff:
```python
import functools

import jax
import jax.numpy as jnp
from jax import lax
from jax.experimental import pallas as pl
from jax.experimental.pallas import tpu as pltpu
from jax.sharding import PartitionSpec as P

EPS = 1e-06
TINY = 1e-30
WIRE = jnp.float16
SEGMENT_SCALE = 1024.0
PEAK_EXPONENT = 14.0
CODE_ROWS = 16
ROWS_PER_STEP = 2
VMEM_LIMIT = 24 * 2**20
LOADING_VMEM_LIMIT = 53 * 2**20


def whole_vmem():
    return pl.BlockSpec(memory_space=pltpu.VMEM)


def whole_smem():
    return pl.BlockSpec(memory_space=pltpu.SMEM)


def low_part(value, high):
    return (value - high.astype(jnp.float32)).astype(jnp.bfloat16)


def code_of(squares, rows):
    return jnp.floor(jnp.log2(SEGMENT_SCALE * lax.rsqrt(squares * (1.0 / rows) + TINY)))


def forward_rows(begin, offsets, tiles, halves, out, factor):
    blocks, width, columns = halves.shape
    columns = columns // 2
    kept = tiles.shape[1]

    @pl.loop(0, blocks // 2 // ROWS_PER_STEP)
    def _(step):
        for local in range(ROWS_PER_STEP):
            at = step * ROWS_PER_STEP + local
            row = begin + at
            total = jnp.zeros((width, 2 * columns), jnp.float32)
            for k in range(0, kept, 2):
                first = halves[lax.rem(row + offsets[k], blocks)]
                second = halves[lax.rem(row + offsets[k + 1], blocks)]
                left = jnp.concatenate([tiles[row, k], tiles[row, k + 1]], axis=1)
                right = jnp.concatenate([first, second], axis=0)
                total += jnp.dot(left, right, preferred_element_type=jnp.float32)
            result = total[:, :columns] + total[:, columns:]
            out[pl.ds(pl.multiple_of(at * width, width), width)] = (
                result if factor is None else result * factor
            )


def forward_first_kernel(offsets, half, tiles, own_half, other_half, out, halves):
    each, width, columns = own_half.shape
    start = half[0] * each
    squares = jnp.zeros((1, columns), jnp.float32)
    for block in range(each):
        for source, base in ((own_half, start), (other_half, each - start)):
            value = source[block]
            squares += jnp.sum(value * value, axis=0, keepdims=True)
            high = value.astype(jnp.bfloat16)
            halves[base + block] = jnp.concatenate([high, low_part(value, high)], axis=1)
    code = code_of(squares, 2 * each * width)
    out[each * width :] = jnp.broadcast_to(code, (CODE_ROWS, columns))
    forward_rows(each - start, offsets, tiles, halves, out, jnp.exp2(code))


def forward_second_kernel(offsets, half, tiles, halves, out):
    forward_rows(half[0] * (halves.shape[0] // 2), offsets, tiles, halves, out, None)


def backward_rows(row, offsets, tiles, value, squares, total):
    blocks, columns, width = total.shape
    squares[...] += jnp.sum(value * value, axis=0, keepdims=True)
    turned = value.T
    high = turned.astype(jnp.bfloat16)
    left = jnp.concatenate([high, low_part(turned, high)], axis=0)
    for k in range(0, tiles.shape[1], 2):
        right = jnp.concatenate([tiles[row, k], tiles[row, k + 1]], axis=1)
        part = jnp.dot(left, right, preferred_element_type=jnp.float32)
        part = part[:columns] + part[columns:]
        total[lax.rem(row + offsets[k], blocks)] += part[:, :width]
        total[lax.rem(row + offsets[k + 1], blocks)] += part[:, width:]


def backward_result(start, squares, total, given, out):
    blocks, columns, width = total.shape
    each = blocks // 2
    code = code_of(squares, blocks * width)
    scale = jnp.exp2(code)
    for block in range(blocks):
        place = lax.rem(start + block, blocks)
        value = total[place] if given is None else total[place] + given[place]
        at = block % each * width
        out[block // each, at : at + width] = value.T * scale
    for part in range(2):
        out[part, each * width :] = jnp.broadcast_to(code, (CODE_ROWS, columns))


def backward_loading_kernel(offsets, half, source, near, out, tiles, squares, total, arrived):
    blocks = total.shape[0]
    start = half[0] * (blocks // 2)
    steps = blocks // ROWS_PER_STEP

    def load(step):
        part = pl.ds(step * ROWS_PER_STEP, ROWS_PER_STEP)
        return pltpu.make_async_copy(source.at[part], tiles.at[part], arrived.at[step])

    for step in range(steps):
        load(step).start()
    total[...] = jnp.zeros_like(total)
    squares[...] = jnp.zeros_like(squares)

    @pl.loop(0, steps)
    def _(step):
        load(step).wait()
        for local in range(ROWS_PER_STEP):
            row = step * ROWS_PER_STEP + local
            backward_rows(row, offsets, tiles, near[row], squares, total)

    backward_result(start, squares[...], total, None, out)


def backward_first_kernel(offsets, half, tiles, near, total, squares):
    each = near.shape[0]
    total[...] = jnp.zeros_like(total)
    squares[...] = jnp.zeros_like(squares)

    @pl.loop(0, each // ROWS_PER_STEP)
    def _(step):
        for local in range(ROWS_PER_STEP):
            at = step * ROWS_PER_STEP + local
            row = half[0] * each + at
            backward_rows(row, offsets, tiles, near[at], squares, total)


def backward_second_kernel(offsets, half, tiles, near, given, given_squares, out, squares, total):
    each = near.shape[0]
    total[...] = jnp.zeros_like(total)
    squares[...] = given_squares[...]

    @pl.loop(0, each // ROWS_PER_STEP)
    def _(step):
        for local in range(ROWS_PER_STEP):
            at = step * ROWS_PER_STEP + local
            row = (1 - half[0]) * each + at
            backward_rows(row, offsets, tiles, near[at], squares, total)

    backward_result(half[0] * each, squares[...], total, given, out)


def gram_kernel(start, first, second, out):
    count, width, columns = start.shape

    def total(function):
        sums = jnp.zeros((width, columns), jnp.float32)
        for block in range(count):
            sums += function(start[block], first[block], second[block])
        return jnp.sum(sums, axis=0, keepdims=True)

    weight = total(lambda s, u, v: s * s)
    usable = weight > 0
    safe = jnp.where(usable, weight, 1.0)
    a = jnp.where(usable, total(lambda s, u, v: s * u) / safe, 0.0)
    b = jnp.where(usable, total(lambda s, u, v: s * (v - a * u)) / safe, 0.0)
    out[...] = jnp.zeros_like(out)
    out[0:1] = a
    out[1:2] = b
    out[2:3] = weight
    out[3:4] = total(lambda s, u, v: (u - a * s) * (u - a * s))
    out[4:5] = total(lambda s, u, v: (u - a * s) * (v - a * u - b * s))
    out[5:6] = total(lambda s, u, v: (v - a * u - b * s) * (v - a * u - b * s))


def scalar_kernel(count, found, out):
    a, b, weight, uu, uv, vv = (found[:, k, :] for k in range(6))

    def mean(value):
        return jnp.sum(value, axis=0, keepdims=True) * (1.0 / count)

    norm = jnp.sqrt(mean(weight) + EPS)
    inverse = 1.0 / norm
    alpha_one = mean(a * weight) * inverse * inverse
    delta = a - alpha_one
    beta_one = jnp.sqrt(mean(uu + delta * delta * weight) * inverse * inverse + EPS)
    k = inverse / beta_one
    shift = b + delta * a - beta_one * beta_one
    alpha_two = k * k * mean(uv + delta * uu + delta * shift * weight)
    along = delta - alpha_two
    rest = shift - alpha_two * delta
    square = mean(vv + 2.0 * along * uv + along * along * uu + rest * rest * weight)
    beta_two = jnp.sqrt(k * k * square + EPS)
    out[...] = jnp.zeros_like(out)
    out[0:1] = alpha_one
    out[1:2] = alpha_two
    out[2:3] = beta_one
    out[3:4] = beta_two
    out[4:5] = (k * alpha_one * alpha_two - beta_one * inverse) / beta_two
    out[5:6] = -k * (alpha_one + alpha_two) / beta_two
    out[6:7] = k / beta_two


def small_call(kernel, name, *values):
    columns = values[0].shape[-1]
    return pl.pallas_call(
        kernel,
        out_shape=jax.ShapeDtypeStruct((8, columns), jnp.float32),
        in_specs=[whole_vmem()] * len(values),
        out_specs=whole_vmem(),
        compiler_params=pltpu.CompilerParams(vmem_limit_bytes=VMEM_LIMIT),
        cost_estimate=pl.CostEstimate(flops=0, bytes_accessed=2**16, transcendentals=0),
        name=name,
    )(*values)


def call(kernel, name, out_shape, scratch, offsets, half, tiles, *values):
    loading = kernel is backward_loading_kernel
    tiles_spec = pl.BlockSpec(memory_space=pl.ANY) if loading else whole_vmem()
    return pl.pallas_call(
        kernel,
        out_shape=out_shape,
        in_specs=[whole_smem(), whole_smem(), tiles_spec] + [whole_vmem()] * len(values),
        out_specs=tuple(whole_vmem() for _ in out_shape),
        scratch_shapes=scratch or [],
        compiler_params=pltpu.CompilerParams(vmem_limit_bytes=LOADING_VMEM_LIMIT if loading else VMEM_LIMIT),
        cost_estimate=pl.CostEstimate(flops=0, bytes_accessed=2**16, transcendentals=0),
        name=name,
    )(offsets, half, tiles, *values)


def forward_product(tiles, offsets, half, own_half, other_half):
    blocks, _, width, _ = tiles.shape
    columns = own_half.shape[-1]
    each = blocks // 2
    shape = (each, width, columns)
    message = jax.ShapeDtypeStruct((each * width + CODE_ROWS, columns), jnp.float32)
    part = jax.ShapeDtypeStruct((each * width, columns), jnp.float32)
    other, halves = call(
        forward_first_kernel,
        "forward_first",
        (message, pltpu.VMEM((blocks, width, 2 * columns), jnp.bfloat16)),
        None,
        offsets, half, tiles, own_half.reshape(shape), other_half.reshape(shape),
    )
    (own,) = call(forward_second_kernel, "forward_second", (part,), None, offsets, half, tiles, halves)
    return other.astype(WIRE), own


def messages_shape(blocks, width, columns):
    return (2, blocks // 2 * width + CODE_ROWS, columns)


def two_messages(value):
    return value[0].astype(WIRE), value[1].astype(WIRE)


def backward_loading(tiles, offsets, half, near):
    blocks, _, width, _ = tiles.shape
    columns = near.shape[-1]
    shape = (blocks, width, columns)
    out, kept = call(
        backward_loading_kernel,
        "backward_loading",
        (
            pltpu.VMEM(messages_shape(blocks, width, columns), jnp.float32),
            pltpu.VMEM(tiles.shape, tiles.dtype),
        ),
        [
            pltpu.VMEM((1, columns), jnp.float32),
            pltpu.VMEM((blocks, columns, width), jnp.float32),
            pltpu.SemaphoreType.DMA((blocks // ROWS_PER_STEP,)),
        ],
        offsets, half, tiles, near.reshape(shape),
    )
    return two_messages(out), kept


def backward_product(tiles, offsets, half, own_half, other_half):
    blocks, _, width, _ = tiles.shape
    columns = own_half.shape[-1]
    shape = (blocks // 2, width, columns)
    total = (blocks, columns, width)
    given, squares = call(
        backward_first_kernel,
        "backward_first",
        (jax.ShapeDtypeStruct(total, jnp.float32), jax.ShapeDtypeStruct((1, columns), jnp.float32)),
        None,
        offsets, half, tiles, own_half.reshape(shape),
    )
    (out,) = call(
        backward_second_kernel,
        "backward_second",
        (jax.ShapeDtypeStruct(messages_shape(blocks, width, columns), jnp.float32),),
        [pltpu.VMEM((1, columns), jnp.float32), pltpu.VMEM(total, jnp.float32)],
        offsets, half, tiles, other_half.reshape(shape), given, squares,
    )
    return two_messages(out)


AXES = ("row", "half", "line")


def permute(value, place):
    rows = lax.axis_size("row")
    cols = lax.axis_size("half") * lax.axis_size("line")
    pairs = []
    for r in range(rows):
        for c in range(cols):
            to_row, to_col = place(r, c, c ^ (cols // 2))
            pairs.append((r * cols + c, to_row % rows * cols + to_col))
    return lax.ppermute(value, AXES, pairs)


def swap(value):
    return permute(value, lambda r, c, o: (r, o))


def fetch(value):
    own = permute(value, lambda r, c, o: (r - c, c))
    return own, permute(value, lambda r, c, o: (r - o, o))


def give_back(own, other):
    same = permute(own, lambda r, c, o: (r + c, c))
    return same, permute(other, lambda r, c, o: (r + c, o))


def encode(value):
    peak = jnp.max(jnp.abs(value), axis=-2, keepdims=True)
    code = PEAK_EXPONENT - jnp.floor(jnp.log2(jnp.maximum(peak, TINY)))
    codes = jnp.broadcast_to(code, value.shape[:-2] + (CODE_ROWS, value.shape[-1]))
    return jnp.concatenate([(value * jnp.exp2(code)).astype(WIRE), codes.astype(WIRE)], axis=-2)


def decode(message):
    rows = message.shape[-2] - CODE_ROWS
    value = message[..., :rows, :].astype(jnp.float32)
    return value * jnp.exp2(-message[..., rows : rows + 1, :].astype(jnp.float32))


def sum_line(partial):
    count = lax.axis_size("line")
    rows, columns = partial.shape
    parts = encode(partial.reshape(count, rows // count, columns))
    parts = lax.all_to_all(parts, "line", 0, 0)
    share = encode(jnp.sum(decode(parts), axis=0))
    return lax.all_to_all(jnp.broadcast_to(share[None], parts.shape), "line", 0, 0)


def segment_values(own):
    rows = lax.axis_size("row")
    copies = jnp.broadcast_to(own[None], (2 * rows,) + own.shape)
    return lax.all_to_all(copies, ("row", "half"), 0, 0)


def body(start_block, tiles, band_offsets):
    half = lax.axis_index("half")
    rows, height, columns = lax.axis_size("row"), *start_block.shape
    parts = lax.axis_size("line")
    offsets = band_offsets[0, 0]
    place = half[None].astype(jnp.int32)
    start_half = lax.dynamic_slice_in_dim(start_block, half * (height // 2), height // 2, 0)
    start_half = start_half.reshape(parts, height // 2 // parts, columns)

    def partial_sum(kept, far, back):
        other, own = forward_product(kept, offsets, place, decode(far[0]), decode(far[1]))
        given = swap(other)
        return own + decode(given) + decode(back[0]) + decode(back[1])

    def ordered(own, other):
        first = jnp.where(half == 0, own, other)
        second = jnp.where(half == 0, other, own)
        return jnp.concatenate([first, second], axis=0).reshape(height, columns)

    far = fetch(encode(start_half))
    back, kept = backward_loading(tiles[0, 0], offsets, place, start_block)
    first = sum_line(partial_sum(kept, far, give_back(*back)))

    first_rest = swap(first)
    far = fetch(first)
    first_half, first_rest = decode(first), decode(first_rest)
    back = backward_product(kept, offsets, place, first_half, first_rest)
    second = sum_line(partial_sum(kept, far, give_back(*back)))

    second_rest = swap(second)
    second_half = decode(second)
    found = segment_values(small_call(gram_kernel, "gram", start_half, first_half, second_half))
    scalars = small_call(functools.partial(scalar_kernel, height * rows), "scalars", found)
    scalars, second_rest = lax.optimization_barrier((scalars, second_rest))
    q_third = (
        scalars[4] * start_block
        + scalars[5] * ordered(first_half, first_rest)
        + scalars[6] * ordered(second_half, decode(second_rest))
    )
    return (scalars[0:2], scalars[2:4], q_third)


def solution(mesh):
    rows, cols = mesh.devices.shape
    parted = jax.sharding.Mesh(mesh.devices.reshape(rows, 2, cols // 2), AXES)
    split = ("half", "line")
    placed = (P("row", None), P("row", split, None, None, None, None), P("row", split, None))
    return jax.shard_map(
        body, mesh=parted, in_specs=placed, out_specs=(P(), P(), P("row", None)), check_vma=False
    )
```

time: 185 us -> 157 us (0.85)
  starting transfers between devices: 51.3 us -> 37.8 us
  local copies, waits for them, and re-layouts: 14.6 us -> 4.41 us
  blocking collectives: 67.1 us -> 63.1 us
  waiting for transfers between devices: 19.9 us -> 16.8 us
  Pallas kernels: 21.7 us -> 24.2 us
    all_to_all x3 -> x1, starting transfers between devices: 26 us -> 11.3 us  [segment_values(): return lax.all_to_all(copies, ('row', 'half'), 0, 0)]
    unnamed x14 -> x8, local copies, waits for them, and re-layouts: 11.7 us -> 2.8 us
    all_to_all x2, blocking collectives: 43.5 us -> 39 us  [sum_line(): parts = lax.all_to_all(parts, 'line', 0, 0)]
    reduce_sum x14 -> x2, other arithmetic: 3.71 us -> 0.12 us  [sum_line(): share = encode(jnp.sum(decode(parts), axis=0))]
    ppermute x12, waiting for transfers between devices: 13.8 us -> 10.7 us  [permute(): return lax.ppermute(value, AXES, pairs)]
    all_to_all x3 -> x1, waiting for transfers between devices: 6.07 us -> 6.09 us  [segment_values(): return lax.all_to_all(copies, ('row', 'half'), 0, 0)]
  transfers between devices with their start and end apart: 15 -> 13, of which waited for: 4 -> 4; matrix products, arithmetic and copies ran while one was open for 2% -> 2% of each run, Pallas kernels for 12% -> 16%
where the time goes in v4:
time: 157 us; the launch traced here: 156 us
  blocking collectives  63.1 us (40%)
  starting transfers between devices  37.8 us (24%)
  Pallas kernels  24.2 us (15%)
  waiting for transfers between devices  16.8 us (11%)
  other arithmetic  8.4 us (5%)
  local copies, waits for them, and re-layouts  4.41 us (3%)
    all_to_all x2, blocking collectives, sum_line(): parts = lax.all_to_all(parts, 'line', 0, 0)  39 us
    ppermute x12, starting transfers between devices, permute(): return lax.ppermute(value, AXES, pairs)  26.5 us
    all_to_all x2, blocking collectives, sum_line(): lax.all_to_all(jnp.broadcast_to(share[None], parts.shape), 'line', 0, 0)  24.1 us
    pallas_call x7, Pallas kernels, call(): pl.pallas_call(kernel, out_shape=out_shape, in_specs=[whole_smem(), whole...  23.5 us
    all_to_all x1, starting transfers between devices, segment_values(): return lax.all_to_all(copies, ('row', 'half'), 0, 0)  11.3 us
    ppermute x12, waiting for transfers between devices, permute(): return lax.ppermute(value, AXES, pairs)  10.7 us
    all_to_all x1, waiting for transfers between devices, segment_values(): return lax.all_to_all(copies, ('row', 'half'), 0, 0)  6.09 us
  transfers between devices with their start and end apart: 13, of which 4 were waited for; matrix products, arithmetic and copies ran while one was open for 2% of the time, Pallas kernels for 16%

profile of v4, /device:TPU:1, one launch (start us, length us, event | category | flops | bytes accessed | tf_op | source)
XLA Modules:
  0.0 156.0 jit_solution(1214563504413407783)
XLA Ops:
  0.6 1.1 abs_reduce_fusion.2
  1.9 0.7 collective-permute-start
  2.6 6.0 %collective-permute-start.1 = (f16[8,144,128]{2,1,0:T(8,128)(2,1)S(1)}, f16[8,144,128]{2,1,0:T(8,128)(2,1)S(1)}, u32[]{:S(2)}, u32[]{:S(2)}) collective-permute-start(f16[8,144,128]{2,1,0:T(8,128)(2,1)S(1)} %pad_maximum_fusion.2), channel_id=1, source_target_pairs={{0,136},{1,121},{2,106},{3,91},{4,76},{5,61},{6,46},{7,31},{8,0},{... | collective-permute-start | bytes 884744 | tf_op jit(solution)/shard_map/ppermute | solution.py:318
  8.7 7.9 %backward_loading.1 = (f32[2,1040,128]{2,1,0:T(8,128)S(1)}, bf16[16,12,128,128]{3,2,1,0:T(8,128)(2,1)S(1)}) custom-call(s32[12]{0:T(128)} %bitcast.68, s32[1]{0:T(128)} %bitcast.2.half, bf16[16,12,128,128]{3,2,1,0:T(8,128)(2,1)} %bitcast.76, f32[16,128,128]{2,1,0:T(8,128)} %bitcast.75), custom_call_target="tpu_custom_call" | custom-call | bytes 65536 | tf_op jit(solution)/shard_map/backward_loading/pallas_call | solution.py:226
  17.1 0.7 collective-permute-start.3
  17.9 2.3 %forward_first.2 = (f32[1040,128]{1,0:T(8,128)S(1)}, bf16[16,128,256]{2,1,0:T(8,128)(2,1)S(1)}) custom-call(s32[12]{0:T(128)S(1)} %bitcast.69, s32[1]{0:T(128)} %bitcast.2.half, bf16[16,12,128,128]{3,2,1,0:T(8,128)(2,1)S(1)} %get-tuple-element.13.tiles, f32[8,128,128]{2,1,0:T(8,128)S(1)} %convert_multiply_fusion.7.own_half, ...), custom_call_target="tpu_custom_call" | custom-call | bytes 65536 | tf_op jit(solution)/shard_map/forward_first/pallas_call | solution.py:226
  20.3 5.2 %collective-permute-start.2 = (f16[1040,128]{1,0:T(8,128)(2,1)S(1)}, f16[1040,128]{1,0:T(8,128)(2,1)S(1)}, u32[]{:S(2)}, u32[]{:S(2)}) collective-permute-start(f16[1040,128]{1,0:T(8,128)(2,1)S(1)} %convert_element_type.159), channel_id=1, source_target_pairs={{0,8},{1,9},{2,10},{3,11},{4,12},{5,13},{6,14},{7,15},{8,0},{9,1},... | collective-permute-start | bytes 798728 | tf_op jit(solution)/shard_map/ppermute | solution.py:318
  25.9 2.1 %forward_second.2 = f32[1024,128]{1,0:T(8,128)S(1)} custom-call(s32[12]{0:T(128)S(1)} %bitcast.70, s32[1]{0:T(128)} %bitcast.2.half, bf16[16,12,128,128]{3,2,1,0:T(8,128)(2,1)S(1)} %get-tuple-element.13.tiles, bf16[16,128,256]{2,1,0:T(8,128)(2,1)S(1)} %get-tuple-element.14.halves), custom_call_target="tpu_custom_call" | custom-call | bytes 65536 | tf_op jit(solution)/shard_map/forward_second/pallas_call | solution.py:226
  28.0 4.6 %collective-permute-done.2 = f16[1040,128]{1,0:T(8,128)(2,1)S(1)} collective-permute-done((f16[1040,128]{1,0:T(8,128)(2,1)S(1)}, f16[1040,128]{1,0:T(8,128)(2,1)S(1)}, u32[]{:S(2)}, u32[]{:S(2)}) %collective-permute-start.2) | collective-permute-done | bytes 266272 | tf_op jit(solution)/shard_map/ppermute | solution.py:318
  33.1 22.9 %all_to_all.25 = f16[8,144,128]{2,1,0:T(8,128)(2,1)S(1)} all-to-all(f16[8,144,128]{2,1,0:T(8,128)(2,1)S(1)} %pad_maximum_fusion.3), channel_id=1, replica_groups=mesh['row'=16,'half'=2,'line'=8] {'line'}, dimensions={0} | all-to-all | bytes 589824 | tf_op jit(solution)/shard_map/all_to_all | solution.py:352
  56.2 12.1 %all_to_all.26 = f16[8,144,128]{2,1,0:T(8,128)(2,1)S(1)} all-to-all(f16[8,144,128]{2,1,0:T(8,128)(2,1)S(1)} %broadcast_in_dim.22), channel_id=1, replica_groups=mesh['row'=16,'half'=2,'line'=8] {'line'}, dimensions={0} | all-to-all | bytes 589824 | tf_op jit(solution)/shard_map/all_to_all | solution.py:354
  68.3 2.4 %collective-permute-start.8 = (f16[8,144,128]{2,1,0:T(8,128)(2,1)S(1)}, f16[8,144,128]{2,1,0:T(8,128)(2,1)S(1)}, u32[]{:S(2)}, u32[]{:S(2)}) collective-permute-start(f16[8,144,128]{2,1,0:T(8,128)(2,1)S(1)} %all_to_all.26), channel_id=1, source_target_pairs={{0,8},{1,9},{2,10},{3,11},{4,12},{5,13},{6,14},{7,15},{8,0},{9,1},... | collective-permute-start | bytes 884744 | tf_op jit(solution)/shard_map/ppermute | solution.py:318
  70.7 0.7 collective-permute-start.5
  71.4 4.0 %collective-permute-start.6 = (f16[8,144,128]{2,1,0:T(8,128)(2,1)S(1)}, f16[8,144,128]{2,1,0:T(8,128)(2,1)S(1)}, u32[]{:S(2)}, u32[]{:S(2)}) collective-permute-start(f16[8,144,128]{2,1,0:T(8,128)(2,1)S(1)} %all_to_all.26), channel_id=1, source_target_pairs={{0,136},{1,121},{2,106},{3,91},{4,76},{5,61},{6,46},{7,31},{8,0},{... | collective-permute-start | bytes 884744 | tf_op jit(solution)/shard_map/ppermute | solution.py:318
  75.5 1.0 broadcast_select_fusion.1
  76.5 2.8 %copy-done.1 = bf16[16,12,128,128]{3,2,1,0:T(8,128)(2,1)S(1)} copy-done((bf16[16,12,128,128]{3,2,1,0:T(8,128)(2,1)S(1)}, bf16[16,12,128,128]{3,2,1,0:T(8,128)(2,1)}, u32[]{:S(2)}) %copy-start.1) | copy-done | bytes 6291480
  79.3 3.1 %backward_first.1 = (f32[16,128,128]{2,1,0:T(8,128)S(1)}, f32[1,128]{1,0:T(1,128)S(1)}) custom-call(s32[12]{0:T(128)S(1)} %bitcast.71, s32[1]{0:T(128)} %bitcast.2.half, bf16[16,12,128,128]{3,2,1,0:T(8,128)(2,1)S(1)} %copy-done.1, f32[8,128,128]{2,1,0:T(8,128)S(1)} %get-tuple-element.34.near.first), custom_call_target="tpu_custom_call" | custom-call | bytes 65536 | tf_op jit(solution)/shard_map/backward_first/pallas_call | solution.py:226
  82.4 3.5 %backward_second.1 = f32[2,1040,128]{2,1,0:T(8,128)S(1)} custom-call(s32[12]{0:T(128)S(1)} %bitcast.72, s32[1]{0:T(128)} %bitcast.2.half, bf16[16,12,128,128]{3,2,1,0:T(8,128)(2,1)S(1)} %copy-done.1, f32[8,128,128]{2,1,0:T(8,128)S(1)} %get-tuple-element.33.near, f32[16,128,128]{2,1,0:T(8,128)S(1)} %get-tuple-element.19.given, ...), custom_call_target="tpu_custom_call" | custom-call | bytes 65536 | tf_op jit(solution)/shard_map/backward_second/pallas_call | solution.py:226
  86.2 0.9 collective-permute-start.10
  87.9 2.5 %forward_first.3 = (f32[1040,128]{1,0:T(8,128)S(1)}, bf16[16,128,256]{2,1,0:T(8,128)(2,1)S(1)}) custom-call(s32[12]{0:T(128)S(1)} %bitcast.73, s32[1]{0:T(128)} %bitcast.2.half, bf16[16,12,128,128]{3,2,1,0:T(8,128)(2,1)S(1)} %copy-done.1, f32[8,128,128]{2,1,0:T(8,128)S(1)} %convert_multiply_fusion.4.own_half, ...), custom_call_target="tpu_custom_call" | custom-call | bytes 65536 | tf_op jit(solution)/shard_map/forward_first/pallas_call | solution.py:226
  90.4 2.2 %forward_second.3 = f32[1024,128]{1,0:T(8,128)S(1)} custom-call(s32[12]{0:T(128)S(1)} %bitcast.74, s32[1]{0:T(128)} %bitcast.2.half, bf16[16,12,128,128]{3,2,1,0:T(8,128)(2,1)S(1)} %copy-done.1, bf16[16,128,256]{2,1,0:T(8,128)(2,1)S(1)} %get-tuple-element.17.halves), custom_call_target="tpu_custom_call" | custom-call | bytes 65536 | tf_op jit(solution)/shard_map/forward_second/pallas_call | solution.py:226
  92.6 4.6 %collective-permute-start.7 = (f16[1040,128]{1,0:T(8,128)(2,1)S(1)}, f16[1040,128]{1,0:T(8,128)(2,1)S(1)}, u32[]{:S(2)}, u32[]{:S(2)}) collective-permute-start(f16[1040,128]{1,0:T(8,128)(2,1)S(1)} %convert_element_type.180), channel_id=1, source_target_pairs={{0,8},{1,9},{2,10},{3,11},{4,12},{5,13},{6,14},{7,15},{8,0},{9,1},... | collective-permute-start | bytes 798728 | tf_op jit(solution)/shard_map/ppermute | solution.py:318
  97.3 5.8 %collective-permute-done.7 = f16[1040,128]{1,0:T(8,128)(2,1)S(1)} collective-permute-done((f16[1040,128]{1,0:T(8,128)(2,1)S(1)}, f16[1040,128]{1,0:T(8,128)(2,1)S(1)}, u32[]{:S(2)}, u32[]{:S(2)}) %collective-permute-start.7) | collective-permute-done | bytes 266272 | tf_op jit(solution)/shard_map/ppermute | solution.py:318
  103.6 16.1 %all_to_all.27 = f16[8,144,128]{2,1,0:T(8,128)(2,1)S(1)} all-to-all(f16[8,144,128]{2,1,0:T(8,128)(2,1)S(1)} %pad_maximum_fusion.4), channel_id=1, replica_groups=mesh['row'=16,'half'=2,'line'=8] {'line'}, dimensions={0} | all-to-all | bytes 589824 | tf_op jit(solution)/shard_map/all_to_all | solution.py:352
  120.0 12.1 %all_to_all.28 = f16[8,144,128]{2,1,0:T(8,128)(2,1)S(1)} all-to-all(f16[8,144,128]{2,1,0:T(8,128)(2,1)S(1)} %broadcast_in_dim.25), channel_id=1, replica_groups=mesh['row'=16,'half'=2,'line'=8] {'line'}, dimensions={0} | all-to-all | bytes 589824 | tf_op jit(solution)/shard_map/all_to_all | solution.py:354
  132.9 0.7 broadcast_in_dim.26
  133.6 11.3 %all-to-all-start.4 = ((f32[32,8,128]{2,1,0:T(8,128)}), f32[32,8,128]{2,1,0:T(8,128)S(1)}, u32[]{:S(2)}, u32[]{:S(2)}) async-start(f32[32,8,128]{2,1,0:T(8,128)} %broadcast_in_dim.26), calls=%async_computation.4 | async-start | bytes 262144 | tf_op jit(solution)/shard_map/all_to_all | solution.py:360
  144.9 1.2 pad_maximum_fusion
  146.1 6.1 %all-to-all-done.4.found = f32[32,8,128]{2,1,0:T(8,128)S(1)} async-done(((f32[32,8,128]{2,1,0:T(8,128)}), f32[32,8,128]{2,1,0:T(8,128)S(1)}, u32[]{:S(2)}, u32[]{:S(2)}) %all-to-all-start.4) | async-done | bytes 131104 | tf_op jit(solution)/shard_map/all_to_all | solution.py:360
  152.9 0.7 multiply_exponential_fusion.2
  153.6 1.1 fusion.3
  154.8 1.2 fusion
  (81 shorter events, 5.4 us)
Async XLA Ops:
  1.8 16.1 %copy-start.2 = (s32[1,1,12]{2,1,0:T(1,128)S(1)}, s32[1,1,12]{2,1,0:T(1,128)}, u32[]{:S(2)}) copy-start(s32[1,1,12]{2,1,0:T(1,128)} %param.5) | copy-start | bytes 148
  1.9 15.8 %collective-permute-start = (f16[8,144,128]{2,1,0:T(8,128)(2,1)S(1)}, f16[8,144,128]{2,1,0:T(8,128)(2,1)S(1)}, u32[]{:S(2)}, u32[]{:S(2)}) collective-permute-start(f16[8,144,128]{2,1,0:T(8,128)(2,1)S(1)} %pad_maximum_fusion.2), channel_id=1, source_target_pairs={{0,0},{1,241},{2,226},{3,211},{4,196},{5,181},{6,166},{7,151},{8,1... | collective-permute-start | bytes 884744 | tf_op jit(solution)/shard_map/ppermute | solution.py:318
  2.6 15.2 %collective-permute-start.1 = (f16[8,144,128]{2,1,0:T(8,128)(2,1)S(1)}, f16[8,144,128]{2,1,0:T(8,128)(2,1)S(1)}, u32[]{:S(2)}, u32[]{:S(2)}) collective-permute-start(f16[8,144,128]{2,1,0:T(8,128)(2,1)S(1)} %pad_maximum_fusion.2), channel_id=1, source_target_pairs={{0,136},{1,121},{2,106},{3,91},{4,76},{5,61},{6,46},{7,31},{8,0},{... | collective-permute-start | bytes 884744 | tf_op jit(solution)/shard_map/ppermute | solution.py:318
  16.5 11.4 %copy-start = (bf16[16,12,128,128]{3,2,1,0:T(8,128)(2,1)}, bf16[16,12,128,128]{3,2,1,0:T(8,128)(2,1)S(1)}, u32[]{:S(2)}) copy-start(bf16[16,12,128,128]{3,2,1,0:T(8,128)(2,1)S(1)} %get-tuple-element.13.tiles) | copy-start | bytes 18874372
  16.7 9.1 %collective-permute-start.4 = (f16[1040,128]{1,0:T(8,128)(2,1)S(1)}, f16[1040,128]{1,0:T(8,128)(2,1)S(1)}, u32[]{:S(2)}, u32[]{:S(2)}) collective-permute-start(f16[1040,128]{1,0:T(8,128)(2,1)S(1)} %get-tuple-element.32), channel_id=1, source_target_pairs={{0,8},{1,25},{2,42},{3,59},{4,76},{5,93},{6,110},{7,127},{8,128},{... | collective-permute-start | bytes 798728 | tf_op jit(solution)/shard_map/ppermute | solution.py:318
  17.1 8.8 %collective-permute-start.3 = (f16[1040,128]{1,0:T(8,128)(2,1)S(1)}, f16[1040,128]{1,0:T(8,128)(2,1)S(1)}, u32[]{:S(2)}, u32[]{:S(2)}) collective-permute-start(f16[1040,128]{1,0:T(8,128)(2,1)S(1)} %get-tuple-element.31), channel_id=1, source_target_pairs={{0,0},{1,17},{2,34},{3,51},{4,68},{5,85},{6,102},{7,119},{8,136},{... | collective-permute-start | bytes 798728 | tf_op jit(solution)/shard_map/ppermute | solution.py:318
  20.3 12.2 %collective-permute-start.2 = (f16[1040,128]{1,0:T(8,128)(2,1)S(1)}, f16[1040,128]{1,0:T(8,128)(2,1)S(1)}, u32[]{:S(2)}, u32[]{:S(2)}) collective-permute-start(f16[1040,128]{1,0:T(8,128)(2,1)S(1)} %convert_element_type.159), channel_id=1, source_target_pairs={{0,8},{1,9},{2,10},{3,11},{4,12},{5,13},{6,14},{7,15},{8,0},{9,1},... | collective-permute-start | bytes 798728 | tf_op jit(solution)/shard_map/ppermute | solution.py:318
  68.3 7.1 %collective-permute-start.8 = (f16[8,144,128]{2,1,0:T(8,128)(2,1)S(1)}, f16[8,144,128]{2,1,0:T(8,128)(2,1)S(1)}, u32[]{:S(2)}, u32[]{:S(2)}) collective-permute-start(f16[8,144,128]{2,1,0:T(8,128)(2,1)S(1)} %all_to_all.26), channel_id=1, source_target_pairs={{0,8},{1,9},{2,10},{3,11},{4,12},{5,13},{6,14},{7,15},{8,0},{9,1},... | collective-permute-start | bytes 884744 | tf_op jit(solution)/shard_map/ppermute | solution.py:318
  70.7 17.0 %collective-permute-start.5 = (f16[8,144,128]{2,1,0:T(8,128)(2,1)S(1)}, f16[8,144,128]{2,1,0:T(8,128)(2,1)S(1)}, u32[]{:S(2)}, u32[]{:S(2)}) collective-permute-start(f16[8,144,128]{2,1,0:T(8,128)(2,1)S(1)} %all_to_all.26), channel_id=1, source_target_pairs={{0,0},{1,241},{2,226},{3,211},{4,196},{5,181},{6,166},{7,151},{8,1... | collective-permute-start | bytes 884744 | tf_op jit(solution)/shard_map/ppermute | solution.py:318
  71.4 16.4 %collective-permute-start.6 = (f16[8,144,128]{2,1,0:T(8,128)(2,1)S(1)}, f16[8,144,128]{2,1,0:T(8,128)(2,1)S(1)}, u32[]{:S(2)}, u32[]{:S(2)}) collective-permute-start(f16[8,144,128]{2,1,0:T(8,128)(2,1)S(1)} %all_to_all.26), channel_id=1, source_target_pairs={{0,136},{1,121},{2,106},{3,91},{4,76},{5,61},{6,46},{7,31},{8,0},{... | collective-permute-start | bytes 884744 | tf_op jit(solution)/shard_map/ppermute | solution.py:318
  76.5 2.8 %copy-start.1 = (bf16[16,12,128,128]{3,2,1,0:T(8,128)(2,1)S(1)}, bf16[16,12,128,128]{3,2,1,0:T(8,128)(2,1)}, u32[]{:S(2)}) copy-start(bf16[16,12,128,128]{3,2,1,0:T(8,128)(2,1)} %copy-done) | copy-start | bytes 18874372
  86.2 11.1 %collective-permute-start.10 = (f16[1040,128]{1,0:T(8,128)(2,1)S(1)}, f16[1040,128]{1,0:T(8,128)(2,1)S(1)}, u32[]{:S(2)}, u32[]{:S(2)}) collective-permute-start(f16[1040,128]{1,0:T(8,128)(2,1)S(1)} %get-tuple-element.30), channel_id=1, source_target_pairs={{0,8},{1,25},{2,42},{3,59},{4,76},{5,93},{6,110},{7,127},{8,128},{... | collective-permute-start | bytes 798728 | tf_op jit(solution)/shard_map/ppermute | solution.py:318
  87.1 10.2 %collective-permute-start.9 = (f16[1040,128]{1,0:T(8,128)(2,1)S(1)}, f16[1040,128]{1,0:T(8,128)(2,1)S(1)}, u32[]{:S(2)}, u32[]{:S(2)}) collective-permute-start(f16[1040,128]{1,0:T(8,128)(2,1)S(1)} %get-tuple-element.29), channel_id=1, source_target_pairs={{0,0},{1,17},{2,34},{3,51},{4,68},{5,85},{6,102},{7,119},{8,136},{... | collective-permute-start | bytes 798728 | tf_op jit(solution)/shard_map/ppermute | solution.py:318
  92.6 10.4 %collective-permute-start.7 = (f16[1040,128]{1,0:T(8,128)(2,1)S(1)}, f16[1040,128]{1,0:T(8,128)(2,1)S(1)}, u32[]{:S(2)}, u32[]{:S(2)}) collective-permute-start(f16[1040,128]{1,0:T(8,128)(2,1)S(1)} %convert_element_type.180), channel_id=1, source_target_pairs={{0,8},{1,9},{2,10},{3,11},{4,12},{5,13},{6,14},{7,15},{8,0},{9,1},... | collective-permute-start | bytes 798728 | tf_op jit(solution)/shard_map/ppermute | solution.py:318
  103.3 51.5 %copy-start.3 = (f32[2048,128]{1,0:T(8,128)S(1)}, f32[2048,128]{1,0:T(8,128)}, u32[]{:S(2)}) copy-start(f32[2048,128]{1,0:T(8,128)} %param.3) | copy-start | bytes 3145732
  132.0 20.3 %collective-permute-start.11 = (f16[8,144,128]{2,1,0:T(8,128)(2,1)S(1)}, f16[8,144,128]{2,1,0:T(8,128)(2,1)}, u32[]{:S(2)}, u32[]{:S(2)}) collective-permute-start(f16[8,144,128]{2,1,0:T(8,128)(2,1)S(1)} %all_to_all.28), channel_id=1, source_target_pairs={{0,8},{1,9},{2,10},{3,11},{4,12},{5,13},{6,14},{7,15},{8,0},{9,1},... | collective-permute-start | bytes 884744 | tf_op jit(solution)/shard_map/ppermute | solution.py:318
  133.6 18.6 %all-to-all-start.4 = ((f32[32,8,128]{2,1,0:T(8,128)}), f32[32,8,128]{2,1,0:T(8,128)S(1)}, u32[]{:S(2)}, u32[]{:S(2)}) async-start(f32[32,8,128]{2,1,0:T(8,128)} %broadcast_in_dim.26), calls=%async_computation.4 | async-start | bytes 262144 | tf_op jit(solution)/shard_map/all_to_all | solution.py:360

commit v5 on v4

v5 whole, which is shorter than its diff:
```python
import functools

import jax
import jax.numpy as jnp
from jax import lax
from jax.experimental import pallas as pl
from jax.experimental.pallas import tpu as pltpu
from jax.sharding import PartitionSpec as P

EPS = 1e-06
TINY = 1e-30
WIRE = jnp.float16
SEGMENT_SCALE = 1024.0
PEAK_EXPONENT = 14.0
CODE_ROWS = 16
ROWS_PER_STEP = 8
VMEM_LIMIT = 24 * 2**20
LOADING_VMEM_LIMIT = 53 * 2**20


def whole_vmem():
    return pl.BlockSpec(memory_space=pltpu.VMEM)


def whole_smem():
    return pl.BlockSpec(memory_space=pltpu.SMEM)


def low_part(value, high):
    return (value - high.astype(jnp.float32)).astype(jnp.bfloat16)


def code_of(squares, rows):
    return jnp.floor(jnp.log2(SEGMENT_SCALE * lax.rsqrt(squares * (1.0 / rows) + TINY)))


def forward_rows(begin, offsets, tiles, halves, out, factor):
    blocks, width, columns = halves.shape
    columns = columns // 2
    kept = tiles.shape[1]

    @pl.loop(0, blocks // 2 // ROWS_PER_STEP)
    def _(step):
        for local in range(ROWS_PER_STEP):
            at = step * ROWS_PER_STEP + local
            row = begin + at
            total = jnp.zeros((width, 2 * columns), jnp.float32)
            for k in range(0, kept, 2):
                first = halves[(row + offsets[k]) & (blocks - 1)]
                second = halves[(row + offsets[k + 1]) & (blocks - 1)]
                left = jnp.concatenate([tiles[row, k], tiles[row, k + 1]], axis=1)
                right = jnp.concatenate([first, second], axis=0)
                total += jnp.dot(left, right, preferred_element_type=jnp.float32)
            result = total[:, :columns] + total[:, columns:]
            out[pl.ds(pl.multiple_of(at * width, width), width)] = (
                result if factor is None else result * factor
            )


def forward_first_kernel(offsets, half, tiles, own_half, other_half, out, halves):
    each, width, columns = own_half.shape
    start = half[0] * each
    squares = jnp.zeros((1, columns), jnp.float32)
    for block in range(each):
        for source, base in ((own_half, start), (other_half, each - start)):
            value = source[block]
            squares += jnp.sum(value * value, axis=0, keepdims=True)
            high = value.astype(jnp.bfloat16)
            halves[base + block] = jnp.concatenate([high, low_part(value, high)], axis=1)
    code = code_of(squares, 2 * each * width)
    out[each * width :] = jnp.broadcast_to(code, (CODE_ROWS, columns))
    forward_rows(each - start, offsets, tiles, halves, out, jnp.exp2(code))


def forward_second_kernel(offsets, half, tiles, halves, out):
    forward_rows(half[0] * (halves.shape[0] // 2), offsets, tiles, halves, out, None)


def turn_rows(block, value, squares, turned):
    squares[...] += jnp.sum(value * value, axis=0, keepdims=True)
    value = value.T
    high = value.astype(jnp.bfloat16)
    turned[block] = jnp.concatenate([high, low_part(value, high)], axis=0)


def backward_block(block, kinds, offsets, tiles, turned):
    blocks, columns, width = turned.shape
    total = jnp.zeros((columns, width), jnp.float32)
    for k in kinds:
        first = (block + blocks - offsets[k]) & (blocks - 1)
        second = (block + blocks - offsets[k + 1]) & (blocks - 1)
        left = jnp.concatenate([turned[first], turned[second]], axis=1)
        right = jnp.concatenate([tiles[first, k], tiles[second, k + 1]], axis=0)
        total += jnp.dot(left, right, preferred_element_type=jnp.float32)
    return total


def backward_rows(start, kinds, offsets, tiles, squares, turned, given, out):
    blocks, columns, width = turned.shape
    columns = columns // 2
    each = blocks // 2
    code = code_of(squares[...], blocks * width)
    scale = jnp.exp2(code)
    for part in range(2):
        out[part, each * width :] = jnp.broadcast_to(code, (CODE_ROWS, columns))

        @pl.loop(0, each // ROWS_PER_STEP)
        def _(step):
            for local in range(ROWS_PER_STEP):
                at = step * ROWS_PER_STEP + local
                block = (start + part * each + at) & (blocks - 1)
                total = backward_block(block, kinds, offsets, tiles, turned)
                if given is not None:
                    total += given[block]
                result = (total[:columns] + total[columns:]).T * scale
                out[part, pl.ds(pl.multiple_of(at * width, width), width)] = result


def backward_loading_kernel(offsets, half, source, near, out, tiles, squares, turned, given, arrived):
    blocks = near.shape[0]
    steps = arrived.shape[0]
    each = tiles.shape[1] // steps

    def load(step):
        part = pl.ds(step * each, each)
        return pltpu.make_async_copy(source.at[:, part], tiles.at[:, part], arrived.at[step])

    for step in range(steps):
        load(step).start()
    squares[...] = jnp.zeros_like(squares)
    for block in range(blocks):
        turn_rows(block, near[block], squares, turned)
    for step in range(steps):
        load(step).wait()
        kinds = range(step * each, (step + 1) * each, 2)
        if step == steps - 1:
            backward_rows(
                half[0] * (blocks // 2), kinds, offsets, tiles, squares, turned, given, out
            )
            continue

        @pl.loop(0, blocks // ROWS_PER_STEP)
        def _(at):
            for local in range(ROWS_PER_STEP):
                block = at * ROWS_PER_STEP + local
                total = backward_block(block, kinds, offsets, tiles, turned)
                given[block] = total if step == 0 else given[block] + total


def backward_kernel(offsets, half, tiles, own_half, other_half, out, squares, turned):
    each = own_half.shape[0]
    start = half[0] * each
    squares[...] = jnp.zeros_like(squares)
    for block in range(each):
        turn_rows(start + block, own_half[block], squares, turned)
        turn_rows(each - start + block, other_half[block], squares, turned)
    kinds = range(0, tiles.shape[1], 2)
    backward_rows(start, kinds, offsets, tiles, squares, turned, None, out)


def gram_kernel(start, first, second, out):
    count, width, columns = start.shape

    def total(function):
        sums = jnp.zeros((width, columns), jnp.float32)
        for block in range(count):
            sums += function(start[block], first[block], second[block])
        return jnp.sum(sums, axis=0, keepdims=True)

    weight = total(lambda s, u, v: s * s)
    usable = weight > 0
    safe = jnp.where(usable, weight, 1.0)
    a = jnp.where(usable, total(lambda s, u, v: s * u) / safe, 0.0)
    b = jnp.where(usable, total(lambda s, u, v: s * (v - a * u)) / safe, 0.0)
    uu = total(lambda s, u, v: (u - a * s) * (u - a * s))
    uv = total(lambda s, u, v: (u - a * s) * (v - a * u - b * s))
    vv = total(lambda s, u, v: (v - a * u - b * s) * (v - a * u - b * s))
    values = jnp.concatenate([a, b, weight, uu, uv, vv, uu, uu], axis=0)
    for copy in range(out.shape[0]):
        out[copy] = values


def last_kernel(count, half, found, start, first_own, first_other, second_own, second_other, coefficients, out):
    a, b, weight, uu, uv, vv = (found[:, k, :] for k in range(6))

    def mean(value):
        return jnp.sum(value, axis=0, keepdims=True) * (1.0 / count)

    norm = jnp.sqrt(mean(weight) + EPS)
    inverse = 1.0 / norm
    alpha_one = mean(a * weight) * inverse * inverse
    delta = a - alpha_one
    beta_one = jnp.sqrt(mean(uu + delta * delta * weight) * inverse * inverse + EPS)
    k = inverse / beta_one
    shift = b + delta * a - beta_one * beta_one
    alpha_two = k * k * mean(uv + delta * uu + delta * shift * weight)
    along = delta - alpha_two
    rest = shift - alpha_two * delta
    square = mean(vv + 2.0 * along * uv + along * along * uu + rest * rest * weight)
    beta_two = jnp.sqrt(k * k * square + EPS)
    coefficients[0:1] = alpha_one
    coefficients[1:2] = alpha_two
    coefficients[2:3] = beta_one
    coefficients[3:4] = beta_two
    of_start = (k * alpha_one * alpha_two - beta_one * inverse) / beta_two
    of_first = -k * (alpha_one + alpha_two) / beta_two
    of_second = k / beta_two
    each = first_own.shape[0]
    begin = half[0] * each
    for first, second, base in (
        (first_own, second_own, begin),
        (first_other, second_other, each - begin),
    ):
        for block in range(each):
            out[base + block] = (
                of_start * start[base + block] + of_first * first[block] + of_second * second[block]
            )


def small_call(kernel, name, out_shape, *values, first=None):
    specs = [whole_vmem()] * len(values)
    if first is not None:
        specs = [whole_smem()] + specs
        values = (first,) + values
    return pl.pallas_call(
        kernel,
        out_shape=out_shape,
        in_specs=specs,
        out_specs=tuple(whole_vmem() for _ in out_shape),
        compiler_params=pltpu.CompilerParams(vmem_limit_bytes=VMEM_LIMIT),
        cost_estimate=pl.CostEstimate(flops=0, bytes_accessed=2**16, transcendentals=0),
        name=name,
    )(*values)


def call(kernel, name, out_shape, scratch, offsets, half, tiles, *values):
    loading = kernel is backward_loading_kernel
    beside = kernel is forward_second_kernel
    return pl.pallas_call(
        kernel,
        out_shape=out_shape,
        in_specs=[whole_smem(), whole_smem(), pl.BlockSpec(memory_space=pl.ANY) if loading else whole_vmem()]
        + [whole_vmem()] * len(values),
        out_specs=tuple(whole_vmem() for _ in out_shape),
        scratch_shapes=scratch,
        compiler_params=pltpu.CompilerParams(
            vmem_limit_bytes=LOADING_VMEM_LIMIT if loading else VMEM_LIMIT
        ),
        cost_estimate=pl.CostEstimate(
            flops=2**30 if beside else 0,
            bytes_accessed=2**20 if beside else 2**16,
            transcendentals=0,
        ),
        name=name,
    )(offsets, half, tiles, *values)


def forward_product(tiles, offsets, half, own_half, other_half):
    blocks, _, width, _ = tiles.shape
    columns = own_half.shape[-1]
    each = blocks // 2
    shape = (each, width, columns)
    message = jax.ShapeDtypeStruct((each * width + CODE_ROWS, columns), jnp.float32)
    part = jax.ShapeDtypeStruct((each * width, columns), jnp.float32)
    other, halves = call(
        forward_first_kernel,
        "forward_first",
        (message, pltpu.VMEM((blocks, width, 2 * columns), jnp.bfloat16)),
        [],
        offsets, half, tiles, own_half.reshape(shape), other_half.reshape(shape),
    )
    (own,) = call(forward_second_kernel, "forward_second", (part,), [], offsets, half, tiles, halves)
    return other, own


def messages_shape(blocks, width, columns):
    return (2, blocks // 2 * width + CODE_ROWS, columns)


def backward_scratch(blocks, width, columns):
    return [
        pltpu.VMEM((1, columns), jnp.float32),
        pltpu.VMEM((blocks, 2 * columns, width), jnp.bfloat16),
    ]


def backward_loading(tiles, offsets, half, near):
    blocks, _, width, _ = tiles.shape
    columns = near.shape[-1]
    out, kept = call(
        backward_loading_kernel,
        "backward_loading",
        (
            pltpu.VMEM(messages_shape(blocks, width, columns), jnp.float32),
            pltpu.VMEM(tiles.shape, tiles.dtype),
        ),
        backward_scratch(blocks, width, columns)
        + [pltpu.VMEM((blocks, 2 * columns, width), jnp.float32), pltpu.SemaphoreType.DMA((3,))],
        offsets, half, tiles, near.reshape(blocks, width, columns),
    )
    return (out[0].astype(WIRE), out[1].astype(WIRE)), kept


def backward_product(tiles, offsets, half, own_half, other_half):
    blocks, _, width, _ = tiles.shape
    columns = own_half.shape[-1]
    shape = (blocks // 2, width, columns)
    (out,) = call(
        backward_kernel,
        "backward",
        (jax.ShapeDtypeStruct(messages_shape(blocks, width, columns), jnp.float32),),
        backward_scratch(blocks, width, columns),
        offsets, half, tiles, own_half.reshape(shape), other_half.reshape(shape),
    )
    return out[0].astype(WIRE), out[1].astype(WIRE)


AXES = ("row", "half", "line")


def permute(value, place):
    rows = lax.axis_size("row")
    cols = lax.axis_size("half") * lax.axis_size("line")
    pairs = []
    for r in range(rows):
        for c in range(cols):
            to_row, to_col = place(r, c, c ^ (cols // 2))
            pairs.append((r * cols + c, to_row % rows * cols + to_col))
    return lax.ppermute(value, AXES, pairs)


def swap(value):
    return permute(value, lambda r, c, o: (r, o))


def fetch(value):
    own = permute(value, lambda r, c, o: (r - c, c))
    return own, permute(value, lambda r, c, o: (r - o, o))


def give_back(own, other):
    same = permute(own, lambda r, c, o: (r + c, c))
    return same, permute(other, lambda r, c, o: (r + c, o))


def pack(value, code):
    codes = jnp.broadcast_to(code, value.shape[:-2] + (CODE_ROWS, value.shape[-1]))
    return jnp.concatenate([(value * jnp.exp2(code)).astype(WIRE), codes.astype(WIRE)], axis=-2)


def code_in(message):
    rows = message.shape[-2] - CODE_ROWS
    return message[..., rows : rows + 1, :].astype(jnp.float32)


def decode(message):
    rows = message.shape[-2] - CODE_ROWS
    return message[..., :rows, :].astype(jnp.float32) * jnp.exp2(-code_in(message))


def encode(value):
    peak = jnp.max(jnp.abs(value), axis=-2, keepdims=True)
    return pack(value, PEAK_EXPONENT - jnp.floor(jnp.log2(jnp.maximum(peak, TINY))))


def sum_line(partial, code):
    count = lax.axis_size("line")
    rows, columns = partial.shape
    parts = pack(partial.reshape(count, rows // count, columns), code)
    parts = lax.all_to_all(parts, "line", 0, 0)
    code = jnp.min(code_in(parts), axis=0) - (count - 1).bit_length()
    share = pack(jnp.sum(decode(parts), axis=0), code)
    return lax.all_to_all(jnp.broadcast_to(share[None], parts.shape), "line", 0, 0)


def body(start_block, tiles, band_offsets):
    half = lax.axis_index("half")
    rows, height, columns = lax.axis_size("row"), *start_block.shape
    parts = lax.axis_size("line")
    blocks = tiles.shape[2]
    offsets = band_offsets[0, 0]
    place = half[None].astype(jnp.int32)
    start_half = lax.dynamic_slice_in_dim(start_block, half * (height // 2), height // 2, 0)
    start_half = start_half.reshape(parts, height // 2 // parts, columns)

    def apply(kept, far, back):
        other, own = forward_product(kept, offsets, place, decode(far[0]), decode(far[1]))
        given = swap(other.astype(WIRE))
        own, *back = lax.optimization_barrier((own, *back))
        arrived = own + decode(back[0]) + decode(back[1])
        code = jnp.minimum(code_in(other), code_in(given))
        code = jnp.minimum(code, jnp.minimum(code_in(back[0]), code_in(back[1]))) - 2.0
        return sum_line(arrived + decode(given), code)

    far = fetch(encode(start_half))
    back, kept = backward_loading(tiles[0, 0], offsets, place, start_block)
    first = apply(kept, far, give_back(*back))

    first_other = swap(first)
    far = fetch(first)
    first, first_other = decode(first), decode(first_other)
    back = backward_product(kept, offsets, place, first, first_other)
    second = apply(kept, far, give_back(*back))

    second_other = swap(second)
    second = decode(second)
    (found,) = small_call(
        gram_kernel,
        "gram",
        (jax.ShapeDtypeStruct((2 * rows, 8, columns), jnp.float32),),
        start_half, first, second,
    )
    found = lax.all_to_all(found, ("row", "half"), 0, 0)
    found, second_other = lax.optimization_barrier((found, second_other))
    in_blocks = [
        value.reshape(-1, height // blocks, columns)
        for value in (start_block, first, first_other, second, decode(second_other))
    ]
    coefficients, q_third = small_call(
        functools.partial(last_kernel, height * rows),
        "last",
        (
            jax.ShapeDtypeStruct((4, columns), jnp.float32),
            jax.ShapeDtypeStruct((blocks, height // blocks, columns), jnp.float32),
        ),
        found, *in_blocks, first=place,
    )
    return (coefficients[0:2], coefficients[2:4], q_third.reshape(height, columns))


def solution(mesh):
    rows, cols = mesh.devices.shape
    parted = jax.sharding.Mesh(mesh.devices.reshape(rows, 2, cols // 2), AXES)
    split = ("half", "line")
    placed = (P("row", None), P("row", split, None, None, None, None), P("row", split, None))
    return jax.shard_map(
        body, mesh=parted, in_specs=placed, out_specs=(P(), P(), P("row", None)), check_vma=False
    )
```

time: 157 us -> 150 us (0.955)
  blocking collectives: 63.1 us -> 89.6 us
  starting transfers between devices: 37.8 us -> 24.2 us
  waiting for transfers between devices: 16.8 us -> 10.6 us
  other arithmetic: 8.4 us -> 2.8 us
  Pallas kernels: 24.2 us -> 20.5 us
  local copies, waits for them, and re-layouts: 4.41 us -> 0.93 us
    all_to_all x0 -> x1, blocking collectives: none -> 15.1 us  [body(): found = lax.all_to_all(found, ('row', 'half'), 0, 0)]
    all_to_all x1 -> x0, starting transfers between devices: 11.3 us -> none  [segment_values(): return lax.all_to_all(copies, ('row', 'half'), 0, 0)]
    all_to_all x2, blocking collectives: 39 us -> 48.4 us  [sum_line(): parts = lax.all_to_all(parts, 'line', 0, 0)]
    all_to_all x1 -> x0, waiting for transfers between devices: 6.09 us -> none  [segment_values(): return lax.all_to_all(copies, ('row', 'half'), 0, 0)]
    pallas_call x7 -> x6, Pallas kernels: 23.5 us -> 18.8 us  [call(): pl.pallas_call(kernel, out_shape=out_shape, in_specs=[whole_smem(), whole...]
    unnamed x8 -> x4, local copies, waits for them, and re-layouts: 2.8 us -> 0.01 us
    ppermute x12, starting transfers between devices: 26.5 us -> 24.2 us  [permute(): return lax.ppermute(value, AXES, pairs)]
    select_n x2 -> x0, other arithmetic: 2.12 us -> none  [ordered(): first = jnp.where(half == 0, own, other)]
  transfers between devices with their start and end apart: 13 -> 12, of which waited for: 4 -> 3; matrix products, arithmetic and copies ran while one was open for 2% -> 1% of each run, Pallas kernels for 16% -> 13%
where the time goes in v5:
time: 150 us
  blocking collectives  89.6 us (60%)
  starting transfers between devices  24.2 us (16%)
  Pallas kernels  20.5 us (14%)
  waiting for transfers between devices  10.6 us (7%)
  other arithmetic  2.8 us (2%)
    all_to_all x2, blocking collectives, sum_line(): parts = lax.all_to_all(parts, 'line', 0, 0)  48.4 us
    all_to_all x2, blocking collectives, sum_line(): lax.all_to_all(jnp.broadcast_to(share[None], parts.shape), 'line', 0, 0)  26.1 us
    ppermute x12, starting transfers between devices, permute(): return lax.ppermute(value, AXES, pairs)  24.2 us
    pallas_call x6, Pallas kernels, call(): pl.pallas_call(kernel, out_shape=out_shape, in_specs=[whole_smem(), whole...  18.8 us
    all_to_all x1, blocking collectives, body(): found = lax.all_to_all(found, ('row', 'half'), 0, 0)  15.1 us
    ppermute x12, waiting for transfers between devices, permute(): return lax.ppermute(value, AXES, pairs)  10.6 us
  transfers between devices with their start and end apart: 12, of which 3 were waited for; matrix products, arithmetic and copies ran while one was open for 1% of the time, Pallas kernels for 13%

profile of v5, /device:TPU:1, one launch (start us, length us, event | category | flops | bytes accessed | tf_op | source)
XLA Modules:
  0.0 149.8 jit_solution(8357071524896513782)
XLA Ops:
  0.6 1.1 abs_reduce_fusion
  1.9 4.7 %collective-permute-start.1 = (f16[8,144,128]{2,1,0:T(8,128)(2,1)S(1)}, f16[8,144,128]{2,1,0:T(8,128)(2,1)S(1)}, u32[]{:S(2)}, u32[]{:S(2)}) collective-permute-start(f16[8,144,128]{2,1,0:T(8,128)(2,1)S(1)} %pad_maximum_fusion), channel_id=1, source_target_pairs={{0,136},{1,121},{2,106},{3,91},{4,76},{5,61},{6,46},{7,31},{8,0},{... | collective-permute-start | bytes 884744 | tf_op jit(solution)/shard_map/ppermute | solution.py:329
  6.7 0.7 collective-permute-start
  7.4 7.1 %backward_loading.1 = (f32[2,1040,128]{2,1,0:T(8,128)S(1)}, bf16[16,12,128,128]{3,2,1,0:T(8,128)(2,1)S(1)}) custom-call(s32[12]{0:T(128)} %bitcast.51, s32[1]{0:T(128)} %bitcast.half, bf16[16,12,128,128]{3,2,1,0:T(8,128)(2,1)} %bitcast.57, f32[16,128,128]{2,1,0:T(8,128)} %bitcast.48), custom_call_target="tpu_custom_call" | custom-call | bytes 65536 | tf_op jit(solution)/shard_map/backward_loading/pallas_call | solution.py:239
  14.6 1.8 %collective-permute-start.3 = (f16[1040,128]{1,0:T(8,128)(2,1)S(1)}, f16[1040,128]{1,0:T(8,128)(2,1)S(1)}, u32[]{:S(2)}, u32[]{:S(2)}) collective-permute-start(f16[1040,128]{1,0:T(8,128)(2,1)S(1)} %get-tuple-element.43), channel_id=1, source_target_pairs={{0,8},{1,25},{2,42},{3,59},{4,76},{5,93},{6,110},{7,127},{8,128},{... | collective-permute-start | bytes 798728 | tf_op jit(solution)/shard_map/ppermute | solution.py:329
  16.5 0.7 collective-permute-start.2
  17.3 1.9 %forward_first.2 = (f32[1040,128]{1,0:T(8,128)S(1)}, bf16[16,128,256]{2,1,0:T(8,128)(2,1)S(1)}) custom-call(s32[12]{0:T(128)S(1)} %bitcast.52, s32[1]{0:T(128)} %bitcast.half, bf16[16,12,128,128]{3,2,1,0:T(8,128)(2,1)S(1)} %get-tuple-element.19.tiles, f32[8,128,128]{2,1,0:T(8,128)S(1)} %convert_multiply_fusion.7.own_half, ...), custom_call_target="tpu_custom_call" | custom-call | bytes 65536 | tf_op jit(solution)/shard_map/forward_first/pallas_call | solution.py:239
  19.3 4.6 %collective-permute-start.4 = (f16[1040,128]{1,0:T(8,128)(2,1)S(1)}, f16[1040,128]{1,0:T(8,128)(2,1)S(1)}, u32[]{:S(2)}, u32[]{:S(2)}) collective-permute-start(f16[1040,128]{1,0:T(8,128)(2,1)S(1)} %convert_element_type.181), channel_id=1, source_target_pairs={{0,8},{1,9},{2,10},{3,11},{4,12},{5,13},{6,14},{7,15},{8,0},{9,1},... | collective-permute-start | bytes 798728 | tf_op jit(solution)/shard_map/ppermute | solution.py:329
  23.8 1.7 %forward_second.2 = f32[1024,128]{1,0:T(8,128)S(1)} custom-call(s32[12]{0:T(128)S(1)} %bitcast.53, s32[1]{0:T(128)} %bitcast.half, bf16[16,12,128,128]{3,2,1,0:T(8,128)(2,1)S(1)} %get-tuple-element.19.tiles, bf16[16,128,256]{2,1,0:T(8,128)(2,1)S(1)} %get-tuple-element.20.halves), custom_call_target="tpu_custom_call" | custom-call | flops 1073741824 | bytes 1048576 | tf_op jit(solution)/shard_map/forward_second/pallas_call | solution.py:239
  25.6 4.4 %collective-permute-done.4 = f16[1040,128]{1,0:T(8,128)(2,1)S(1)} collective-permute-done((f16[1040,128]{1,0:T(8,128)(2,1)S(1)}, f16[1040,128]{1,0:T(8,128)(2,1)S(1)}, u32[]{:S(2)}, u32[]{:S(2)}) %collective-permute-start.4) | collective-permute-done | bytes 266272 | tf_op jit(solution)/shard_map/ppermute | solution.py:329
  30.0 0.2 multiply_add_fusion.1
  30.3 24.1 %all_to_all.25 = f16[8,144,128]{2,1,0:T(8,128)(2,1)S(1)} all-to-all(f16[8,144,128]{2,1,0:T(8,128)(2,1)S(1)} %pad_maximum_fusion.1), channel_id=1, replica_groups=mesh['row'=16,'half'=2,'line'=8] {'line'}, dimensions={0} | all-to-all | bytes 589824 | tf_op jit(solution)/shard_map/all_to_all | solution.py:370
  54.7 12.6 %all_to_all.26 = f16[8,144,128]{2,1,0:T(8,128)(2,1)S(1)} all-to-all(f16[8,144,128]{2,1,0:T(8,128)(2,1)S(1)} %broadcast_in_dim.20), channel_id=1, replica_groups=mesh['row'=16,'half'=2,'line'=8] {'line'}, dimensions={0} | all-to-all | bytes 589824 | tf_op jit(solution)/shard_map/all_to_all | solution.py:373
  67.3 1.0 collective-permute-start.7
  68.3 1.8 %collective-permute-start.6 = (f16[8,144,128]{2,1,0:T(8,128)(2,1)S(1)}, f16[8,144,128]{2,1,0:T(8,128)(2,1)S(1)}, u32[]{:S(2)}, u32[]{:S(2)}) collective-permute-start(f16[8,144,128]{2,1,0:T(8,128)(2,1)S(1)} %all_to_all.26), channel_id=1, source_target_pairs={{0,136},{1,121},{2,106},{3,91},{4,76},{5,61},{6,46},{7,31},{8,0},{... | collective-permute-start | bytes 884744 | tf_op jit(solution)/shard_map/ppermute | solution.py:329
  70.1 0.8 collective-permute-start.5
  71.0 1.9 %collective-permute-done.7 = f16[8,144,128]{2,1,0:T(8,128)(2,1)S(1)} collective-permute-done((f16[8,144,128]{2,1,0:T(8,128)(2,1)S(1)}, f16[8,144,128]{2,1,0:T(8,128)(2,1)S(1)}, u32[]{:S(2)}, u32[]{:S(2)}) %collective-permute-start.7) | collective-permute-done | bytes 294944 | tf_op jit(solution)/shard_map/ppermute | solution.py:329
  72.9 4.5 %backward.1 = f32[2,1040,128]{2,1,0:T(8,128)S(1)} custom-call(s32[12]{0:T(128)S(1)} %bitcast.54, s32[1]{0:T(128)} %bitcast.half, bf16[16,12,128,128]{3,2,1,0:T(8,128)(2,1)S(1)} %get-tuple-element.19.tiles, f32[8,128,128]{2,1,0:T(8,128)S(1)} %convert_multiply_fusion.5.own_half.first.first_own, f32[8,128,128]{2,1,0:T(8,128)S(1)} %convert_multiply_fusion.2.other_half.first_other), custom_call_target="tpu_custom_call" | custom-call | bytes 65536 | tf_op jit(solution)/shard_map/backward/pallas_call | solution.py:239
  77.6 1.1 collective-permute-start.9
  78.7 0.7 collective-permute-start.8
  79.5 1.9 %forward_first.3 = (f32[1040,128]{1,0:T(8,128)S(1)}, bf16[16,128,256]{2,1,0:T(8,128)(2,1)S(1)}) custom-call(s32[12]{0:T(128)S(1)} %bitcast.55, s32[1]{0:T(128)} %bitcast.half, bf16[16,12,128,128]{3,2,1,0:T(8,128)(2,1)S(1)} %get-tuple-element.19.tiles, f32[8,128,128]{2,1,0:T(8,128)S(1)} %convert_multiply_fusion.4.own_half, ...), custom_call_target="tpu_custom_call" | custom-call | bytes 65536 | tf_op jit(solution)/shard_map/forward_first/pallas_call | solution.py:239
  81.5 5.6 %collective-permute-start.10 = (f16[1040,128]{1,0:T(8,128)(2,1)S(1)}, f16[1040,128]{1,0:T(8,128)(2,1)S(1)}, u32[]{:S(2)}, u32[]{:S(2)}) collective-permute-start(f16[1040,128]{1,0:T(8,128)(2,1)S(1)} %convert_element_type.205), channel_id=1, source_target_pairs={{0,8},{1,9},{2,10},{3,11},{4,12},{5,13},{6,14},{7,15},{8,0},{9,1},... | collective-permute-start | bytes 798728 | tf_op jit(solution)/shard_map/ppermute | solution.py:329
  87.0 1.7 %forward_second.3 = f32[1024,128]{1,0:T(8,128)S(1)} custom-call(s32[12]{0:T(128)S(1)} %bitcast.56, s32[1]{0:T(128)} %bitcast.half, bf16[16,12,128,128]{3,2,1,0:T(8,128)(2,1)S(1)} %get-tuple-element.19.tiles, bf16[16,128,256]{2,1,0:T(8,128)(2,1)S(1)} %get-tuple-element.26.halves), custom_call_target="tpu_custom_call" | custom-call | flops 1073741824 | bytes 1048576 | tf_op jit(solution)/shard_map/forward_second/pallas_call | solution.py:239
  88.8 4.4 %collective-permute-done.10 = f16[1040,128]{1,0:T(8,128)(2,1)S(1)} collective-permute-done((f16[1040,128]{1,0:T(8,128)(2,1)S(1)}, f16[1040,128]{1,0:T(8,128)(2,1)S(1)}, u32[]{:S(2)}, u32[]{:S(2)}) %collective-permute-start.10) | collective-permute-done | bytes 266272 | tf_op jit(solution)/shard_map/ppermute | solution.py:329
  93.2 0.2 multiply_add_fusion
  93.6 24.3 %all_to_all.27 = f16[8,144,128]{2,1,0:T(8,128)(2,1)S(1)} all-to-all(f16[8,144,128]{2,1,0:T(8,128)(2,1)S(1)} %pad_maximum_fusion.2), channel_id=1, replica_groups=mesh['row'=16,'half'=2,'line'=8] {'line'}, dimensions={0} | all-to-all | bytes 589824 | tf_op jit(solution)/shard_map/all_to_all | solution.py:370
  118.0 13.4 %all_to_all.28 = f16[8,144,128]{2,1,0:T(8,128)(2,1)S(1)} all-to-all(f16[8,144,128]{2,1,0:T(8,128)(2,1)S(1)} %broadcast_in_dim.23), channel_id=1, replica_groups=mesh['row'=16,'half'=2,'line'=8] {'line'}, dimensions={0} | all-to-all | bytes 589824 | tf_op jit(solution)/shard_map/all_to_all | solution.py:373
  131.5 0.8 collective-permute-start.11
  132.3 0.4 gram.1
  132.7 15.1 %all_to_all.29.found = f32[32,8,128]{2,1,0:T(8,128)S(1)} all-to-all(f32[32,8,128]{2,1,0:T(8,128)S(1)} %gram.1), channel_id=1, replica_groups=mesh['row'=16,'half'=2,'line'=8] {'row','half'}, dimensions={0} | all-to-all | bytes 262144 | tf_op jit(solution)/shard_map/all_to_all | solution.py:413
  147.9 1.3 last.1
  149.2 0.6 fusion.24
  (63 shorter events, 1.7 us)
Async XLA Ops:
  1.8 15.5 %copy-start.1 = (s32[1,1,12]{2,1,0:T(1,128)S(1)}, s32[1,1,12]{2,1,0:T(1,128)}, u32[]{:S(2)}) copy-start(s32[1,1,12]{2,1,0:T(1,128)} %param.5) | copy-start | bytes 148
  1.9 15.2 %collective-permute-start.1 = (f16[8,144,128]{2,1,0:T(8,128)(2,1)S(1)}, f16[8,144,128]{2,1,0:T(8,128)(2,1)S(1)}, u32[]{:S(2)}, u32[]{:S(2)}) collective-permute-start(f16[8,144,128]{2,1,0:T(8,128)(2,1)S(1)} %pad_maximum_fusion), channel_id=1, source_target_pairs={{0,136},{1,121},{2,106},{3,91},{4,76},{5,61},{6,46},{7,31},{8,0},{... | collective-permute-start | bytes 884744 | tf_op jit(solution)/shard_map/ppermute | solution.py:329
  6.7 10.6 %collective-permute-start = (f16[8,144,128]{2,1,0:T(8,128)(2,1)S(1)}, f16[8,144,128]{2,1,0:T(8,128)(2,1)S(1)}, u32[]{:S(2)}, u32[]{:S(2)}) collective-permute-start(f16[8,144,128]{2,1,0:T(8,128)(2,1)S(1)} %pad_maximum_fusion), channel_id=1, source_target_pairs={{0,0},{1,241},{2,226},{3,211},{4,196},{5,181},{6,166},{7,151},{8,1... | collective-permute-start | bytes 884744 | tf_op jit(solution)/shard_map/ppermute | solution.py:329
  14.6 10.9 %collective-permute-start.3 = (f16[1040,128]{1,0:T(8,128)(2,1)S(1)}, f16[1040,128]{1,0:T(8,128)(2,1)S(1)}, u32[]{:S(2)}, u32[]{:S(2)}) collective-permute-start(f16[1040,128]{1,0:T(8,128)(2,1)S(1)} %get-tuple-element.43), channel_id=1, source_target_pairs={{0,8},{1,25},{2,42},{3,59},{4,76},{5,93},{6,110},{7,127},{8,128},{... | collective-permute-start | bytes 798728 | tf_op jit(solution)/shard_map/ppermute | solution.py:329
  16.5 9.1 %collective-permute-start.2 = (f16[1040,128]{1,0:T(8,128)(2,1)S(1)}, f16[1040,128]{1,0:T(8,128)(2,1)S(1)}, u32[]{:S(2)}, u32[]{:S(2)}) collective-permute-start(f16[1040,128]{1,0:T(8,128)(2,1)S(1)} %get-tuple-element.44), channel_id=1, source_target_pairs={{0,0},{1,17},{2,34},{3,51},{4,68},{5,85},{6,102},{7,119},{8,136},{... | collective-permute-start | bytes 798728 | tf_op jit(solution)/shard_map/ppermute | solution.py:329
  19.3 10.7 %collective-permute-start.4 = (f16[1040,128]{1,0:T(8,128)(2,1)S(1)}, f16[1040,128]{1,0:T(8,128)(2,1)S(1)}, u32[]{:S(2)}, u32[]{:S(2)}) collective-permute-start(f16[1040,128]{1,0:T(8,128)(2,1)S(1)} %convert_element_type.181), channel_id=1, source_target_pairs={{0,8},{1,9},{2,10},{3,11},{4,12},{5,13},{6,14},{7,15},{8,0},{9,1},... | collective-permute-start | bytes 798728 | tf_op jit(solution)/shard_map/ppermute | solution.py:329
  67.3 5.6 %collective-permute-start.7 = (f16[8,144,128]{2,1,0:T(8,128)(2,1)S(1)}, f16[8,144,128]{2,1,0:T(8,128)(2,1)S(1)}, u32[]{:S(2)}, u32[]{:S(2)}) collective-permute-start(f16[8,144,128]{2,1,0:T(8,128)(2,1)S(1)} %all_to_all.26), channel_id=1, source_target_pairs={{0,8},{1,9},{2,10},{3,11},{4,12},{5,13},{6,14},{7,15},{8,0},{9,1},... | collective-permute-start | bytes 884744 | tf_op jit(solution)/shard_map/ppermute | solution.py:329
  68.3 11.0 %collective-permute-start.6 = (f16[8,144,128]{2,1,0:T(8,128)(2,1)S(1)}, f16[8,144,128]{2,1,0:T(8,128)(2,1)S(1)}, u32[]{:S(2)}, u32[]{:S(2)}) collective-permute-start(f16[8,144,128]{2,1,0:T(8,128)(2,1)S(1)} %all_to_all.26), channel_id=1, source_target_pairs={{0,136},{1,121},{2,106},{3,91},{4,76},{5,61},{6,46},{7,31},{8,0},{... | collective-permute-start | bytes 884744 | tf_op jit(solution)/shard_map/ppermute | solution.py:329
  70.1 9.3 %collective-permute-start.5 = (f16[8,144,128]{2,1,0:T(8,128)(2,1)S(1)}, f16[8,144,128]{2,1,0:T(8,128)(2,1)S(1)}, u32[]{:S(2)}, u32[]{:S(2)}) collective-permute-start(f16[8,144,128]{2,1,0:T(8,128)(2,1)S(1)} %all_to_all.26), channel_id=1, source_target_pairs={{0,0},{1,241},{2,226},{3,211},{4,196},{5,181},{6,166},{7,151},{8,1... | collective-permute-start | bytes 884744 | tf_op jit(solution)/shard_map/ppermute | solution.py:329
  77.6 11.2 %collective-permute-start.9 = (f16[1040,128]{1,0:T(8,128)(2,1)S(1)}, f16[1040,128]{1,0:T(8,128)(2,1)S(1)}, u32[]{:S(2)}, u32[]{:S(2)}) collective-permute-start(f16[1040,128]{1,0:T(8,128)(2,1)S(1)} %get-tuple-element.41), channel_id=1, source_target_pairs={{0,8},{1,25},{2,42},{3,59},{4,76},{5,93},{6,110},{7,127},{8,128},{... | collective-permute-start | bytes 798728 | tf_op jit(solution)/shard_map/ppermute | solution.py:329
  78.7 10.1 %collective-permute-start.8 = (f16[1040,128]{1,0:T(8,128)(2,1)S(1)}, f16[1040,128]{1,0:T(8,128)(2,1)S(1)}, u32[]{:S(2)}, u32[]{:S(2)}) collective-permute-start(f16[1040,128]{1,0:T(8,128)(2,1)S(1)} %get-tuple-element.42), channel_id=1, source_target_pairs={{0,0},{1,17},{2,34},{3,51},{4,68},{5,85},{6,102},{7,119},{8,136},{... | collective-permute-start | bytes 798728 | tf_op jit(solution)/shard_map/ppermute | solution.py:329
  81.5 11.7 %collective-permute-start.10 = (f16[1040,128]{1,0:T(8,128)(2,1)S(1)}, f16[1040,128]{1,0:T(8,128)(2,1)S(1)}, u32[]{:S(2)}, u32[]{:S(2)}) collective-permute-start(f16[1040,128]{1,0:T(8,128)(2,1)S(1)} %convert_element_type.205), channel_id=1, source_target_pairs={{0,8},{1,9},{2,10},{3,11},{4,12},{5,13},{6,14},{7,15},{8,0},{9,1},... | collective-permute-start | bytes 798728 | tf_op jit(solution)/shard_map/ppermute | solution.py:329
  88.8 59.2 %copy-start = (f32[2048,128]{1,0:T(8,128)S(1)}, f32[2048,128]{1,0:T(8,128)}, u32[]{:S(2)}) copy-start(f32[2048,128]{1,0:T(8,128)} %param.3) | copy-start | bytes 3145732
  131.5 16.4 %collective-permute-start.11 = (f16[8,144,128]{2,1,0:T(8,128)(2,1)S(1)}, f16[8,144,128]{2,1,0:T(8,128)(2,1)S(1)}, u32[]{:S(2)}, u32[]{:S(2)}) collective-permute-start(f16[8,144,128]{2,1,0:T(8,128)(2,1)S(1)} %all_to_all.28), channel_id=1, source_target_pairs={{0,8},{1,9},{2,10},{3,11},{4,12},{5,13},{6,14},{7,15},{8,0},{9,1},... | collective-permute-start | bytes 884744 | tf_op jit(solution)/shard_map/ppermute | solution.py:329

commit v6 on v5

--- a/solution.py
+++ b/solution.py
@@ -11,8 +11,7 @@
 TINY = 1e-30
 WIRE = jnp.float16
 SEGMENT_SCALE = 1024.0
-PEAK_EXPONENT = 14.0
-CODE_ROWS = 16
+CODE_ROWS = 8
 ROWS_PER_STEP = 8
 VMEM_LIMIT = 24 * 2**20
 LOADING_VMEM_LIMIT = 53 * 2**20
@@ -34,9 +33,14 @@
     return jnp.floor(jnp.log2(SEGMENT_SCALE * lax.rsqrt(squares * (1.0 / rows) + TINY)))
 
 
+def merged(total, columns, axis):
+    if total.shape[axis] == columns:
+        return total
+    return sum(jnp.split(total, 2, axis=axis))
+
+
 def forward_rows(begin, offsets, tiles, halves, out, factor):
-    blocks, width, columns = halves.shape
-    columns = columns // 2
+    blocks, width = halves.shape[:2]
     kept = tiles.shape[1]
 
     @pl.loop(0, blocks // 2 // ROWS_PER_STEP)
@@ -44,17 +48,29 @@
         for local in range(ROWS_PER_STEP):
             at = step * ROWS_PER_STEP + local
             row = begin + at
-            total = jnp.zeros((width, 2 * columns), jnp.float32)
+            total = jnp.zeros((width, halves.shape[2]), jnp.float32)
             for k in range(0, kept, 2):
                 first = halves[(row + offsets[k]) & (blocks - 1)]
                 second = halves[(row + offsets[k + 1]) & (blocks - 1)]
                 left = jnp.concatenate([tiles[row, k], tiles[row, k + 1]], axis=1)
                 right = jnp.concatenate([first, second], axis=0)
                 total += jnp.dot(left, right, preferred_element_type=jnp.float32)
-            result = total[:, :columns] + total[:, columns:]
+            result = merged(total, out.shape[1], 1)
             out[pl.ds(pl.multiple_of(at * width, width), width)] = (
                 result if factor is None else result * factor
             )
+
+
+def forward_start_kernel(offsets, half, tiles, far, out):
+    blocks, width, columns = far.shape
+    squares = jnp.zeros((1, columns), jnp.float32)
+    for block in range(blocks):
+        value = far[block].astype(jnp.float32)
+        squares += jnp.sum(value * value, axis=0, keepdims=True)
+    code = code_of(squares, blocks * width)
+    out[blocks // 2 * width :] = jnp.broadcast_to(code, (CODE_ROWS, columns))
+    begin = (1 - half[0]) * (blocks // 2)
+    forward_rows(begin, offsets, tiles, far, out, jnp.exp2(code))
 
 
 def forward_first_kernel(offsets, half, tiles, own_half, other_half, out, halves):
@@ -80,7 +96,10 @@
     squares[...] += jnp.sum(value * value, axis=0, keepdims=True)
     value = value.T
     high = value.astype(jnp.bfloat16)
-    turned[block] = jnp.concatenate([high, low_part(value, high)], axis=0)
+    if turned.shape[1] == high.shape[0]:
+        turned[block] = high
+    else:
+        turned[block] = jnp.concatenate([high, low_part(value, high)], axis=0)
 
 
 def backward_block(block, kinds, offsets, tiles, turned):
@@ -96,8 +115,8 @@
 
 
 def backward_rows(start, kinds, offsets, tiles, squares, turned, given, out):
-    blocks, columns, width = turned.shape
-    columns = columns // 2
+    blocks, _, width = turned.shape
+    columns = squares.shape[1]
     each = blocks // 2
     code = code_of(squares[...], blocks * width)
     scale = jnp.exp2(code)
@@ -112,7 +131,7 @@
                 total = backward_block(block, kinds, offsets, tiles, turned)
                 if given is not None:
                     total += given[block]
-                result = (total[:columns] + total[columns:]).T * scale
+                result = merged(total, columns, 0).T * scale
                 out[part, pl.ds(pl.multiple_of(at * width, width), width)] = result
 
 
@@ -180,7 +199,7 @@
         out[copy] = values
 
 
-def last_kernel(count, half, found, start, first_own, first_other, second_own, second_other, coefficients, out):
+def last_kernel(count, half, found, start, first_own, first_other, second_own, second_other, alphas, betas, out):
     a, b, weight, uu, uv, vv = (found[:, k, :] for k in range(6))
 
     def mean(value):
@@ -198,10 +217,8 @@
     rest = shift - alpha_two * delta
     square = mean(vv + 2.0 * along * uv + along * along * uu + rest * rest * weight)
     beta_two = jnp.sqrt(k * k * square + EPS)
-    coefficients[0:1] = alpha_one
-    coefficients[1:2] = alpha_two
-    coefficients[2:3] = beta_one
-    coefficients[3:4] = beta_two
+    alphas[...] = jnp.concatenate([alpha_one, alpha_two], axis=0)
+    betas[...] = jnp.concatenate([beta_one, beta_two], axis=0)
     of_start = (k * alpha_one * alpha_two - beta_one * inverse) / beta_two
     of_first = -k * (alpha_one + alpha_two) / beta_two
     of_second = k / beta_two
@@ -255,20 +272,25 @@
     )(offsets, half, tiles, *values)
 
 
-def forward_product(tiles, offsets, half, own_half, other_half):
+def forward_product(tiles, offsets, half, far):
     blocks, _, width, _ = tiles.shape
-    columns = own_half.shape[-1]
+    columns = far[0].shape[-1]
     each = blocks // 2
-    shape = (each, width, columns)
     message = jax.ShapeDtypeStruct((each * width + CODE_ROWS, columns), jnp.float32)
     part = jax.ShapeDtypeStruct((each * width, columns), jnp.float32)
-    other, halves = call(
-        forward_first_kernel,
-        "forward_first",
-        (message, pltpu.VMEM((blocks, width, 2 * columns), jnp.bfloat16)),
-        [],
-        offsets, half, tiles, own_half.reshape(shape), other_half.reshape(shape),
-    )
+    if len(far) == 1:
+        halves = far[0].reshape(blocks, width, columns)
+        (other,) = call(
+            forward_start_kernel, "forward_start", (message,), [], offsets, half, tiles, halves
+        )
+    else:
+        other, halves = call(
+            forward_first_kernel,
+            "forward_first",
+            (message, pltpu.VMEM((blocks, width, 2 * columns), jnp.bfloat16)),
+            [],
+            offsets, half, tiles, *(value.reshape(each, width, columns) for value in far),
+        )
     (own,) = call(forward_second_kernel, "forward_second", (part,), [], offsets, half, tiles, halves)
     return other, own
 
@@ -277,10 +299,10 @@
     return (2, blocks // 2 * width + CODE_ROWS, columns)
 
 
-def backward_scratch(blocks, width, columns):
+def backward_scratch(blocks, width, columns, halves):
     return [
         pltpu.VMEM((1, columns), jnp.float32),
-        pltpu.VMEM((blocks, 2 * columns, width), jnp.bfloat16),
+        pltpu.VMEM((blocks, halves * columns, width), jnp.bfloat16),
     ]
 
 
@@ -294,8 +316,8 @@
             pltpu.VMEM(messages_shape(blocks, width, columns), jnp.float32),
             pltpu.VMEM(tiles.shape, tiles.dtype),
         ),
-        backward_scratch(blocks, width, columns)
-        + [pltpu.VMEM((blocks, 2 * columns, width), jnp.float32), pltpu.SemaphoreType.DMA((3,))],
+        backward_scratch(blocks, width, columns, 1)
+        + [pltpu.VMEM((blocks, columns, width), jnp.float32), pltpu.SemaphoreType.DMA((3,))],
         offsets, half, tiles, near.reshape(blocks, width, columns),
     )
     return (out[0].astype(WIRE), out[1].astype(WIRE)), kept
@@ -309,7 +331,7 @@
         backward_kernel,
         "backward",
         (jax.ShapeDtypeStruct(messages_shape(blocks, width, columns), jnp.float32),),
-        backward_scratch(blocks, width, columns),
+        backward_scratch(blocks, width, columns, 2),
         offsets, half, tiles, own_half.reshape(shape), other_half.reshape(shape),
     )
     return out[0].astype(WIRE), out[1].astype(WIRE)
@@ -338,6 +360,10 @@
     return own, permute(value, lambda r, c, o: (r - o, o))
 
 
+def fetch_whole(value):
+    return permute(value, lambda r, c, o: (r - o, o))
+
+
 def give_back(own, other):
     same = permute(own, lambda r, c, o: (r + c, c))
     return same, permute(other, lambda r, c, o: (r + c, o))
@@ -356,11 +382,6 @@
 def decode(message):
     rows = message.shape[-2] - CODE_ROWS
     return message[..., :rows, :].astype(jnp.float32) * jnp.exp2(-code_in(message))
-
-
-def encode(value):
-    peak = jnp.max(jnp.abs(value), axis=-2, keepdims=True)
-    return pack(value, PEAK_EXPONENT - jnp.floor(jnp.log2(jnp.maximum(peak, TINY))))
 
 
 def sum_line(partial, code):
@@ -384,7 +405,7 @@
     start_half = start_half.reshape(parts, height // 2 // parts, columns)
 
     def apply(kept, far, back):
-        other, own = forward_product(kept, offsets, place, decode(far[0]), decode(far[1]))
+        other, own = forward_product(kept, offsets, place, far)
         given = swap(other.astype(WIRE))
         own, *back = lax.optimization_barrier((own, *back))
         arrived = own + decode(back[0]) + decode(back[1])
@@ -392,12 +413,12 @@
         code = jnp.minimum(code, jnp.minimum(code_in(back[0]), code_in(back[1]))) - 2.0
         return sum_line(arrived + decode(given), code)
 
-    far = fetch(encode(start_half))
+    far = (fetch_whole(start_block.astype(jnp.bfloat16)),)
     back, kept = backward_loading(tiles[0, 0], offsets, place, start_block)
     first = apply(kept, far, give_back(*back))
 
     first_other = swap(first)
-    far = fetch(first)
+    far = tuple(decode(message) for message in fetch(first))
     first, first_other = decode(first), decode(first_other)
     back = backward_product(kept, offsets, place, first, first_other)
     second = apply(kept, far, give_back(*back))
@@ -416,16 +437,17 @@
         value.reshape(-1, height // blocks, columns)
         for value in (start_block, first, first_other, second, decode(second_other))
     ]
-    coefficients, q_third = small_call(
+    alphas, betas, q_third = small_call(
         functools.partial(last_kernel, height * rows),
         "last",
         (
-            jax.ShapeDtypeStruct((4, columns), jnp.float32),
+            jax.ShapeDtypeStruct((2, columns), jnp.float32),
+            jax.ShapeDtypeStruct((2, columns), jnp.float32),
             jax.ShapeDtypeStruct((blocks, height // blocks, columns), jnp.float32),
         ),
         found, *in_blocks, first=place,
     )
-    return (coefficients[0:2], coefficients[2:4], q_third.reshape(height, columns))
+    return (alphas, betas, q_third.reshape(height, columns))
 
 
 def solution(mesh):

time: 150 us -> 144 us (0.960)
  blocking collectives: 89.6 us -> 75 us
  waiting for transfers between devices: 10.6 us -> 21.5 us
  Pallas kernels: 20.5 us -> 18.3 us
    all_to_all x2 -> x1, blocking collectives: 26.1 us -> 11.9 us  [sum_line(): lax.all_to_all(jnp.broadcast_to(share[None], parts.shape), 'line', 0, 0)]
    all_to_all x0 -> x1, waiting for transfers between devices: none -> 9.36 us  [sum_line(): lax.all_to_all(jnp.broadcast_to(share[None], parts.shape), 'line', 0, 0)]
    ppermute x12 -> x11, starting transfers between devices: 24.2 us -> 20 us  [permute(): return lax.ppermute(value, AXES, pairs)]
    all_to_all x2, blocking collectives: 48.4 us -> 44.3 us  [sum_line(): parts = lax.all_to_all(parts, 'line', 0, 0)]
    all_to_all x1, blocking collectives: 15.1 us -> 18.8 us  [body(): found = lax.all_to_all(found, ('row', 'half'), 0, 0)]
    all_to_all x0 -> x1, starting transfers between devices: none -> 3.42 us  [sum_line(): lax.all_to_all(jnp.broadcast_to(share[None], parts.shape), 'line', 0, 0)]
    pallas_call x6, Pallas kernels: 18.8 us -> 16.6 us  [call(): pl.pallas_call(kernel, out_shape=out_shape, in_specs=[whole_smem(), whole...]
    ppermute x12 -> x11, waiting for transfers between devices: 10.6 us -> 12.1 us  [permute(): return lax.ppermute(value, AXES, pairs)]
  transfers between devices with their start and end apart: 12 -> 12, of which waited for: 3 -> 6; matrix products, arithmetic and copies ran while one was open for 1% -> 1% of each run, Pallas kernels for 13% -> 12%
where the time goes in v6:
time: 144 us; the launch traced here: 143 us
  blocking collectives  75 us (52%)
  starting transfers between devices  23.5 us (16%)
  waiting for transfers between devices  21.5 us (15%)
  Pallas kernels  18.3 us (13%)
  other arithmetic  2.74 us (2%)
    all_to_all x2, blocking collectives, sum_line(): parts = lax.all_to_all(parts, 'line', 0, 0)  44.3 us
    ppermute x11, starting transfers between devices, permute(): return lax.ppermute(value, AXES, pairs)  20 us
    all_to_all x1, blocking collectives, body(): found = lax.all_to_all(found, ('row', 'half'), 0, 0)  18.8 us
    pallas_call x6, Pallas kernels, call(): pl.pallas_call(kernel, out_shape=out_shape, in_specs=[whole_smem(), whole...  16.6 us
    ppermute x11, waiting for transfers between devices, permute(): return lax.ppermute(value, AXES, pairs)  12.1 us
    all_to_all x1, blocking collectives, sum_line(): lax.all_to_all(jnp.broadcast_to(share[None], parts.shape), 'line', 0, 0)  11.9 us
    all_to_all x1, waiting for transfers between devices, sum_line(): lax.all_to_all(jnp.broadcast_to(share[None], parts.shape), 'line', 0, 0)  9.36 us
    all_to_all x1, starting transfers between devices, sum_line(): lax.all_to_all(jnp.broadcast_to(share[None], parts.shape), 'line', 0, 0)  3.42 us
  transfers between devices with their start and end apart: 12, of which 6 were waited for; matrix products, arithmetic and copies ran while one was open for 1% of the time, Pallas kernels for 12%

profile of v6, /device:TPU:1, one launch (start us, length us, event | category | flops | bytes accessed | tf_op | source)
XLA Modules:
  0.0 143.1 jit_solution(6615834421422170981)
XLA Ops:
  0.6 1.3 convert_element_type.153
  1.9 4.7 %collective-permute-start = (bf16[2048,128]{1,0:T(8,128)(2,1)S(1)}, bf16[2048,128]{1,0:T(8,128)(2,1)S(1)}, u32[]{:S(2)}, u32[]{:S(2)}) collective-permute-start(bf16[2048,128]{1,0:T(8,128)(2,1)S(1)} %convert_element_type.153), channel_id=1, source_target_pairs={{0,136},{1,121},{2,106},{3,91},{4,76},{5,61},{6,46},{7,31},{8,0},{... | collective-permute-start | bytes 1572872 | tf_op jit(solution)/shard_map/ppermute | solution.py:351
  6.7 5.5 %backward_loading.1 = (f32[2,1032,128]{2,1,0:T(8,128)S(1)}, bf16[16,12,128,128]{3,2,1,0:T(8,128)(2,1)S(1)}) custom-call(s32[12]{0:T(128)} %bitcast.50, s32[1]{0:T(128)} %bitcast.half, bf16[16,12,128,128]{3,2,1,0:T(8,128)(2,1)} %bitcast.56, f32[16,128,128]{2,1,0:T(8,128)} %bitcast.45), custom_call_target="tpu_custom_call" | custom-call | bytes 65536 | tf_op jit(solution)/shard_map/backward_loading/pallas_call | solution.py:256
  12.4 0.7 collective-permute-start.1
  13.0 1.8 %collective-permute-start.2 = (f16[1032,128]{1,0:T(8,128)(2,1)S(1)}, f16[1032,128]{1,0:T(8,128)(2,1)S(1)}, u32[]{:S(2)}, u32[]{:S(2)}) collective-permute-start(f16[1032,128]{1,0:T(8,128)(2,1)S(1)} %get-tuple-element.39), channel_id=1, source_target_pairs={{0,8},{1,25},{2,42},{3,59},{4,76},{5,93},{6,110},{7,127},{8,128},{... | collective-permute-start | bytes 792584 | tf_op jit(solution)/shard_map/ppermute | solution.py:351
  14.9 2.4 %collective-permute-done = bf16[2048,128]{1,0:T(8,128)(2,1)S(1)} collective-permute-done((bf16[2048,128]{1,0:T(8,128)(2,1)S(1)}, bf16[2048,128]{1,0:T(8,128)(2,1)S(1)}, u32[]{:S(2)}, u32[]{:S(2)}) %collective-permute-start) | collective-permute-done | bytes 524320 | tf_op jit(solution)/shard_map/ppermute | solution.py:351
  17.3 1.7 %forward_start.1 = f32[1032,128]{1,0:T(8,128)S(1)} custom-call(s32[12]{0:T(128)S(1)} %bitcast.51, s32[1]{0:T(128)} %bitcast.half, bf16[16,12,128,128]{3,2,1,0:T(8,128)(2,1)S(1)} %get-tuple-element.18.tiles, bf16[16,128,128]{2,1,0:T(8,128)(2,1)S(1)} %bitcast.48), custom_call_target="tpu_custom_call" | custom-call | bytes 65536 | tf_op jit(solution)/shard_map/forward_start/pallas_call | solution.py:256
  19.0 2.1 %collective-permute-start.3 = (f16[1032,128]{1,0:T(8,128)(2,1)S(1)}, f16[1032,128]{1,0:T(8,128)(2,1)S(1)}, u32[]{:S(2)}, u32[]{:S(2)}) collective-permute-start(f16[1032,128]{1,0:T(8,128)(2,1)S(1)} %convert_element_type.160), channel_id=1, source_target_pairs={{0,8},{1,9},{2,10},{3,11},{4,12},{5,13},{6,14},{7,15},{8,0},{9,1},... | collective-permute-start | bytes 792584 | tf_op jit(solution)/shard_map/ppermute | solution.py:351
  21.1 1.6 %forward_second.2 = f32[1024,128]{1,0:T(8,128)S(1)} custom-call(s32[12]{0:T(128)S(1)} %bitcast.52, s32[1]{0:T(128)} %bitcast.half, bf16[16,12,128,128]{3,2,1,0:T(8,128)(2,1)S(1)} %get-tuple-element.18.tiles, bf16[16,128,128]{2,1,0:T(8,128)(2,1)S(1)} %bitcast.49), custom_call_target="tpu_custom_call" | custom-call | flops 1073741824 | bytes 1048576 | tf_op jit(solution)/shard_map/forward_second/pallas_call | solution.py:256
  22.7 1.3 collective-permute-done.2
  23.9 4.7 %collective-permute-done.3 = f16[1032,128]{1,0:T(8,128)(2,1)S(1)} collective-permute-done((f16[1032,128]{1,0:T(8,128)(2,1)S(1)}, f16[1032,128]{1,0:T(8,128)(2,1)S(1)}, u32[]{:S(2)}, u32[]{:S(2)}) %collective-permute-start.3) | collective-permute-done | bytes 264224 | tf_op jit(solution)/shard_map/ppermute | solution.py:351
  28.7 0.2 multiply_add_fusion.1
  29.0 18.8 %all_to_all.25 = f16[8,136,128]{2,1,0:T(8,128)(2,1)S(1)} all-to-all(f16[8,136,128]{2,1,0:T(8,128)(2,1)S(1)} %pad_maximum_fusion), channel_id=1, replica_groups=mesh['row'=16,'half'=2,'line'=8] {'line'}, dimensions={0} | all-to-all | bytes 557056 | tf_op jit(solution)/shard_map/all_to_all | solution.py:391
  48.0 11.9 %all_to_all.26 = f16[8,136,128]{2,1,0:T(8,128)(2,1)S(1)} all-to-all(f16[8,136,128]{2,1,0:T(8,128)(2,1)S(1)} %broadcast_in_dim.17), channel_id=1, replica_groups=mesh['row'=16,'half'=2,'line'=8] {'line'}, dimensions={0} | all-to-all | bytes 557056 | tf_op jit(solution)/shard_map/all_to_all | solution.py:394
  59.9 0.7 collective-permute-start.6
  60.6 0.7 collective-permute-start.4
  61.3 5.0 %collective-permute-start.5 = (f16[8,136,128]{2,1,0:T(8,128)(2,1)S(1)}, f16[8,136,128]{2,1,0:T(8,128)(2,1)S(1)}, u32[]{:S(2)}, u32[]{:S(2)}) collective-permute-start(f16[8,136,128]{2,1,0:T(8,128)(2,1)S(1)} %all_to_all.26), channel_id=1, source_target_pairs={{0,136},{1,121},{2,106},{3,91},{4,76},{5,61},{6,46},{7,31},{8,0},{... | collective-permute-start | bytes 835592 | tf_op jit(solution)/shard_map/ppermute | solution.py:351
  66.4 4.5 %backward.1 = f32[2,1032,128]{2,1,0:T(8,128)S(1)} custom-call(s32[12]{0:T(128)S(1)} %bitcast.53, s32[1]{0:T(128)} %bitcast.half, bf16[16,12,128,128]{3,2,1,0:T(8,128)(2,1)S(1)} %get-tuple-element.18.tiles, f32[8,128,128]{2,1,0:T(8,128)S(1)} %convert_multiply_fusion.5.own_half.first.first_own, f32[8,128,128]{2,1,0:T(8,128)S(1)} %convert_multiply_fusion.2.other_half.first_other), custom_call_target="tpu_custom_call" | custom-call | bytes 65536 | tf_op jit(solution)/shard_map/backward/pallas_call | solution.py:256
  71.2 0.7 collective-permute-start.7
  71.9 2.8 %collective-permute-start.8 = (f16[1032,128]{1,0:T(8,128)(2,1)S(1)}, f16[1032,128]{1,0:T(8,128)(2,1)S(1)}, u32[]{:S(2)}, u32[]{:S(2)}) collective-permute-start(f16[1032,128]{1,0:T(8,128)(2,1)S(1)} %get-tuple-element.37), channel_id=1, source_target_pairs={{0,8},{1,25},{2,42},{3,59},{4,76},{5,93},{6,110},{7,127},{8,128},{... | collective-permute-start | bytes 792584 | tf_op jit(solution)/shard_map/ppermute | solution.py:351
  74.8 1.8 %forward_first.1 = (f32[1032,128]{1,0:T(8,128)S(1)}, bf16[16,128,256]{2,1,0:T(8,128)(2,1)S(1)}) custom-call(s32[12]{0:T(128)S(1)} %bitcast.54, s32[1]{0:T(128)} %bitcast.half, bf16[16,12,128,128]{3,2,1,0:T(8,128)(2,1)S(1)} %get-tuple-element.18.tiles, f32[8,128,128]{2,1,0:T(8,128)S(1)} %convert_multiply_fusion.4.own_half, ...), custom_call_target="tpu_custom_call" | custom-call | bytes 65536 | tf_op jit(solution)/shard_map/forward_first/pallas_call | solution.py:256
  76.7 1.6 %forward_second.3 = f32[1024,128]{1,0:T(8,128)S(1)} custom-call(s32[12]{0:T(128)S(1)} %bitcast.55, s32[1]{0:T(128)} %bitcast.half, bf16[16,12,128,128]{3,2,1,0:T(8,128)(2,1)S(1)} %get-tuple-element.18.tiles, bf16[16,128,256]{2,1,0:T(8,128)(2,1)S(1)} %get-tuple-element.23.halves), custom_call_target="tpu_custom_call" | custom-call | flops 1073741824 | bytes 1048576 | tf_op jit(solution)/shard_map/forward_second/pallas_call | solution.py:256
  78.3 1.3 collective-permute-done.8
  79.6 2.4 %collective-permute-done.9 = f16[1032,128]{1,0:T(8,128)(2,1)S(1)} collective-permute-done((f16[1032,128]{1,0:T(8,128)(2,1)S(1)}, f16[1032,128]{1,0:T(8,128)(2,1)S(1)}, u32[]{:S(2)}, u32[]{:S(2)}) %collective-permute-start.9) | collective-permute-done | bytes 264224 | tf_op jit(solution)/shard_map/ppermute | solution.py:351
  82.4 25.5 %all_to_all.27 = f16[8,136,128]{2,1,0:T(8,128)(2,1)S(1)} all-to-all(f16[8,136,128]{2,1,0:T(8,128)(2,1)S(1)} %pad_maximum_fusion.1), channel_id=1, replica_groups=mesh['row'=16,'half'=2,'line'=8] {'line'}, dimensions={0} | all-to-all | bytes 557056 | tf_op jit(solution)/shard_map/all_to_all | solution.py:391
  108.0 0.7 broadcast_in_dim.20
  108.8 3.4 %all-to-all-start.3 = ((f16[8,136,128]{2,1,0:T(8,128)(2,1)}), f16[8,136,128]{2,1,0:T(8,128)(2,1)S(1)}, u32[]{:S(2)}, u32[]{:S(2)}) async-start(f16[8,136,128]{2,1,0:T(8,128)(2,1)} %broadcast_in_dim.20), calls=%async_computation.3 | async-start | bytes 557056 | tf_op jit(solution)/shard_map/all_to_all | solution.py:394
  112.3 9.4 %all-to-all-done.3 = f16[8,136,128]{2,1,0:T(8,128)(2,1)S(1)} async-done(((f16[8,136,128]{2,1,0:T(8,128)(2,1)}), f16[8,136,128]{2,1,0:T(8,128)(2,1)S(1)}, u32[]{:S(2)}, u32[]{:S(2)}) %all-to-all-start.3) | async-done | bytes 278560 | tf_op jit(solution)/shard_map/all_to_all | solution.py:394
  121.6 0.8 collective-permute-start.10
  122.5 0.4 gram.1
  122.9 18.8 %all_to_all.28.found = f32[32,8,128]{2,1,0:T(8,128)S(1)} all-to-all(f32[32,8,128]{2,1,0:T(8,128)S(1)} %gram.1), channel_id=1, replica_groups=mesh['row'=16,'half'=2,'line'=8] {'row','half'}, dimensions={0} | all-to-all | bytes 262144 | tf_op jit(solution)/shard_map/all_to_all | solution.py:434
  141.8 1.3 last.1
  (54 shorter events, 1.7 us)
Async XLA Ops:
  0.6 16.7 %copy-start.1 = (s32[1,1,12]{2,1,0:T(1,128)S(1)}, s32[1,1,12]{2,1,0:T(1,128)}, u32[]{:S(2)}) copy-start(s32[1,1,12]{2,1,0:T(1,128)} %param.5) | copy-start | bytes 148
  1.9 15.4 %collective-permute-start = (bf16[2048,128]{1,0:T(8,128)(2,1)S(1)}, bf16[2048,128]{1,0:T(8,128)(2,1)S(1)}, u32[]{:S(2)}, u32[]{:S(2)}) collective-permute-start(bf16[2048,128]{1,0:T(8,128)(2,1)S(1)} %convert_element_type.153), channel_id=1, source_target_pairs={{0,136},{1,121},{2,106},{3,91},{4,76},{5,61},{6,46},{7,31},{8,0},{... | collective-permute-start | bytes 1572872 | tf_op jit(solution)/shard_map/ppermute | solution.py:351
  12.4 10.3 %collective-permute-start.1 = (f16[1032,128]{1,0:T(8,128)(2,1)S(1)}, f16[1032,128]{1,0:T(8,128)(2,1)S(1)}, u32[]{:S(2)}, u32[]{:S(2)}) collective-permute-start(f16[1032,128]{1,0:T(8,128)(2,1)S(1)} %get-tuple-element.40), channel_id=1, source_target_pairs={{0,0},{1,17},{2,34},{3,51},{4,68},{5,85},{6,102},{7,119},{8,136},{... | collective-permute-start | bytes 792584 | tf_op jit(solution)/shard_map/ppermute | solution.py:351
  13.0 10.9 %collective-permute-start.2 = (f16[1032,128]{1,0:T(8,128)(2,1)S(1)}, f16[1032,128]{1,0:T(8,128)(2,1)S(1)}, u32[]{:S(2)}, u32[]{:S(2)}) collective-permute-start(f16[1032,128]{1,0:T(8,128)(2,1)S(1)} %get-tuple-element.39), channel_id=1, source_target_pairs={{0,8},{1,25},{2,42},{3,59},{4,76},{5,93},{6,110},{7,127},{8,128},{... | collective-permute-start | bytes 792584 | tf_op jit(solution)/shard_map/ppermute | solution.py:351
  19.0 9.6 %collective-permute-start.3 = (f16[1032,128]{1,0:T(8,128)(2,1)S(1)}, f16[1032,128]{1,0:T(8,128)(2,1)S(1)}, u32[]{:S(2)}, u32[]{:S(2)}) collective-permute-start(f16[1032,128]{1,0:T(8,128)(2,1)S(1)} %convert_element_type.160), channel_id=1, source_target_pairs={{0,8},{1,9},{2,10},{3,11},{4,12},{5,13},{6,14},{7,15},{8,0},{9,1},... | collective-permute-start | bytes 792584 | tf_op jit(solution)/shard_map/ppermute | solution.py:351
  59.9 6.4 %collective-permute-start.6 = (f16[8,136,128]{2,1,0:T(8,128)(2,1)S(1)}, f16[8,136,128]{2,1,0:T(8,128)(2,1)S(1)}, u32[]{:S(2)}, u32[]{:S(2)}) collective-permute-start(f16[8,136,128]{2,1,0:T(8,128)(2,1)S(1)} %all_to_all.26), channel_id=1, source_target_pairs={{0,8},{1,9},{2,10},{3,11},{4,12},{5,13},{6,14},{7,15},{8,0},{9,1},... | collective-permute-start | bytes 835592 | tf_op jit(solution)/shard_map/ppermute | solution.py:351
  60.6 14.0 %collective-permute-start.4 = (f16[8,136,128]{2,1,0:T(8,128)(2,1)S(1)}, f16[8,136,128]{2,1,0:T(8,128)(2,1)S(1)}, u32[]{:S(2)}, u32[]{:S(2)}) collective-permute-start(f16[8,136,128]{2,1,0:T(8,128)(2,1)S(1)} %all_to_all.26), channel_id=1, source_target_pairs={{0,0},{1,241},{2,226},{3,211},{4,196},{5,181},{6,166},{7,151},{8,1... | collective-permute-start | bytes 835592 | tf_op jit(solution)/shard_map/ppermute | solution.py:351
  61.3 13.4 %collective-permute-start.5 = (f16[8,136,128]{2,1,0:T(8,128)(2,1)S(1)}, f16[8,136,128]{2,1,0:T(8,128)(2,1)S(1)}, u32[]{:S(2)}, u32[]{:S(2)}) collective-permute-start(f16[8,136,128]{2,1,0:T(8,128)(2,1)S(1)} %all_to_all.26), channel_id=1, source_target_pairs={{0,136},{1,121},{2,106},{3,91},{4,76},{5,61},{6,46},{7,31},{8,0},{... | collective-permute-start | bytes 835592 | tf_op jit(solution)/shard_map/ppermute | solution.py:351
  71.2 7.1 %collective-permute-start.7 = (f16[1032,128]{1,0:T(8,128)(2,1)S(1)}, f16[1032,128]{1,0:T(8,128)(2,1)S(1)}, u32[]{:S(2)}, u32[]{:S(2)}) collective-permute-start(f16[1032,128]{1,0:T(8,128)(2,1)S(1)} %get-tuple-element.38), channel_id=1, source_target_pairs={{0,0},{1,17},{2,34},{3,51},{4,68},{5,85},{6,102},{7,119},{8,136},{... | collective-permute-start | bytes 792584 | tf_op jit(solution)/shard_map/ppermute | solution.py:351
  71.9 7.7 %collective-permute-start.8 = (f16[1032,128]{1,0:T(8,128)(2,1)S(1)}, f16[1032,128]{1,0:T(8,128)(2,1)S(1)}, u32[]{:S(2)}, u32[]{:S(2)}) collective-permute-start(f16[1032,128]{1,0:T(8,128)(2,1)S(1)} %get-tuple-element.37), channel_id=1, source_target_pairs={{0,8},{1,25},{2,42},{3,59},{4,76},{5,93},{6,110},{7,127},{8,128},{... | collective-permute-start | bytes 792584 | tf_op jit(solution)/shard_map/ppermute | solution.py:351
  76.6 5.4 %collective-permute-start.9 = (f16[1032,128]{1,0:T(8,128)(2,1)S(1)}, f16[1032,128]{1,0:T(8,128)(2,1)S(1)}, u32[]{:S(2)}, u32[]{:S(2)}) collective-permute-start(f16[1032,128]{1,0:T(8,128)(2,1)S(1)} %convert_element_type.184), channel_id=1, source_target_pairs={{0,8},{1,9},{2,10},{3,11},{4,12},{5,13},{6,14},{7,15},{8,0},{9,1},... | collective-permute-start | bytes 792584 | tf_op jit(solution)/shard_map/ppermute | solution.py:351
  76.7 35.5 %copy-start = (f32[2048,128]{1,0:T(8,128)S(1)}, f32[2048,128]{1,0:T(8,128)}, u32[]{:S(2)}) copy-start(f32[2048,128]{1,0:T(8,128)} %param.3) | copy-start | bytes 3145732
  108.8 12.8 %all-to-all-start.3 = ((f16[8,136,128]{2,1,0:T(8,128)(2,1)}), f16[8,136,128]{2,1,0:T(8,128)(2,1)S(1)}, u32[]{:S(2)}, u32[]{:S(2)}) async-start(f16[8,136,128]{2,1,0:T(8,128)(2,1)} %broadcast_in_dim.20), calls=%async_computation.3 | async-start | bytes 557056 | tf_op jit(solution)/shard_map/all_to_all | solution.py:394
  121.6 20.1 %collective-permute-start.10 = (f16[8,136,128]{2,1,0:T(8,128)(2,1)S(1)}, f16[8,136,128]{2,1,0:T(8,128)(2,1)S(1)}, u32[]{:S(2)}, u32[]{:S(2)}) collective-permute-start(f16[8,136,128]{2,1,0:T(8,128)(2,1)S(1)} %all-to-all-done.3), channel_id=1, source_target_pairs={{0,8},{1,9},{2,10},{3,11},{4,12},{5,13},{6,14},{7,15},{8,0},{9,1},... | collective-permute-start | bytes 835592 | tf_op jit(solution)/shard_map/ppermute | solution.py:351

commit v7 on v6

--- a/solution.py
+++ b/solution.py
@@ -148,7 +148,7 @@
         load(step).start()
     squares[...] = jnp.zeros_like(squares)
     for block in range(blocks):
-        turn_rows(block, near[block], squares, turned)
+        turn_rows(block, near[block].astype(jnp.float32), squares, turned)
     for step in range(steps):
         load(step).wait()
         kinds = range(step * each, (step + 1) * each, 2)
@@ -177,13 +177,14 @@
     backward_rows(start, kinds, offsets, tiles, squares, turned, None, out)
 
 
-def gram_kernel(start, first, second, out):
-    count, width, columns = start.shape
+def gram_kernel(half, start, first, second, out):
+    count, width, columns = first.shape
+    begin = half[0] * count
 
     def total(function):
         sums = jnp.zeros((width, columns), jnp.float32)
         for block in range(count):
-            sums += function(start[block], first[block], second[block])
+            sums += function(start[begin + block], first[block], second[block])
         return jnp.sum(sums, axis=0, keepdims=True)
 
     weight = total(lambda s, u, v: s * s)
@@ -401,9 +402,6 @@
     blocks = tiles.shape[2]
     offsets = band_offsets[0, 0]
     place = half[None].astype(jnp.int32)
-    start_half = lax.dynamic_slice_in_dim(start_block, half * (height // 2), height // 2, 0)
-    start_half = start_half.reshape(parts, height // 2 // parts, columns)
-
     def apply(kept, far, back):
         other, own = forward_product(kept, offsets, place, far)
         given = swap(other.astype(WIRE))
@@ -413,8 +411,9 @@
         code = jnp.minimum(code, jnp.minimum(code_in(back[0]), code_in(back[1]))) - 2.0
         return sum_line(arrived + decode(given), code)
 
-    far = (fetch_whole(start_block.astype(jnp.bfloat16)),)
-    back, kept = backward_loading(tiles[0, 0], offsets, place, start_block)
+    rounded = start_block.astype(jnp.bfloat16)
+    far = (fetch_whole(rounded),)
+    back, kept = backward_loading(tiles[0, 0], offsets, place, rounded)
     first = apply(kept, far, give_back(*back))
 
     first_other = swap(first)
@@ -429,7 +428,7 @@
         gram_kernel,
         "gram",
         (jax.ShapeDtypeStruct((2 * rows, 8, columns), jnp.float32),),
-        start_half, first, second,
+        start_block.reshape(blocks, height // blocks, columns), first, second, first=place,
     )
     found = lax.all_to_all(found, ("row", "half"), 0, 0)
     found, second_other = lax.optimization_barrier((found, second_other))

time: 144 us -> 143 us (level)
  blocking collectives: 75 us -> 87.8 us
  waiting for transfers between devices: 21.5 us -> 12.1 us
  starting transfers between devices: 23.5 us -> 20.7 us
    all_to_all x1 -> x2, blocking collectives: 11.9 us -> 25 us  [sum_line(): lax.all_to_all(jnp.broadcast_to(share[None], parts.shape), 'line', 0, 0)]
    all_to_all x1 -> x0, waiting for transfers between devices: 9.36 us -> none  [sum_line(): lax.all_to_all(jnp.broadcast_to(share[None], parts.shape), 'line', 0, 0)]
    all_to_all x1 -> x0, starting transfers between devices: 3.42 us -> none  [sum_line(): lax.all_to_all(jnp.broadcast_to(share[None], parts.shape), 'line', 0, 0)]
  transfers between devices with their start and end apart: 12 -> 11, of which waited for: 6 -> 5; matrix products, arithmetic and copies ran while one was open for 1% -> 0% of each run, Pallas kernels for 12% -> 12%
where the time goes in v7:
time: 143 us
  blocking collectives  87.8 us (61%)
  starting transfers between devices  20.7 us (14%)
  Pallas kernels  18.2 us (13%)
  waiting for transfers between devices  12.1 us (8%)
  other arithmetic  2.73 us (2%)
    all_to_all x2, blocking collectives, sum_line(): parts = lax.all_to_all(parts, 'line', 0, 0)  45.2 us
    all_to_all x2, blocking collectives, sum_line(): lax.all_to_all(jnp.broadcast_to(share[None], parts.shape), 'line', 0, 0)  25 us
    ppermute x11, starting transfers between devices, permute(): return lax.ppermute(value, AXES, pairs)  20.7 us
    all_to_all x1, blocking collectives, body(): found = lax.all_to_all(found, ('row', 'half'), 0, 0)  17.6 us
    pallas_call x6, Pallas kernels, call(): pl.pallas_call(kernel, out_shape=out_shape, in_specs=[whole_smem(), whole...  16.5 us
    ppermute x11, waiting for transfers between devices, permute(): return lax.ppermute(value, AXES, pairs)  12.1 us
  transfers between devices with their start and end apart: 11, of which 5 were waited for; matrix products, arithmetic and copies ran while one was open for 0% of the time, Pallas kernels for 12%

profile of v7, /device:TPU:1, one launch (start us, length us, event | category | flops | bytes accessed | tf_op | source)
XLA Modules:
  0.0 142.9 jit_solution(7181730314608901664)
XLA Ops:
  0.6 1.3 convert_element_type.153
  1.9 4.7 %collective-permute-start = (bf16[2048,128]{1,0:T(8,128)(2,1)S(1)}, bf16[2048,128]{1,0:T(8,128)(2,1)S(1)}, u32[]{:S(2)}, u32[]{:S(2)}) collective-permute-start(bf16[2048,128]{1,0:T(8,128)(2,1)S(1)} %convert_element_type.153), channel_id=1, source_target_pairs={{0,136},{1,121},{2,106},{3,91},{4,76},{5,61},{6,46},{7,31},{8,0},{... | collective-permute-start | bytes 1572872 | tf_op jit(solution)/shard_map/ppermute | solution.py:352
  6.7 5.3 %backward_loading.1 = (f32[2,1032,128]{2,1,0:T(8,128)S(1)}, bf16[16,12,128,128]{3,2,1,0:T(8,128)(2,1)S(1)}) custom-call(s32[12]{0:T(128)} %bitcast.49, s32[1]{0:T(128)} %bitcast.half, bf16[16,12,128,128]{3,2,1,0:T(8,128)(2,1)} %bitcast.55, bf16[16,128,128]{2,1,0:T(8,128)(2,1)} %bitcast.56), custom_call_target="tpu_custom_call" | custom-call | bytes 65536 | tf_op jit(solution)/shard_map/backward_loading/pallas_call | solution.py:257
  12.2 0.7 collective-permute-start.1
  12.9 2.3 %collective-permute-start.2 = (f16[1032,128]{1,0:T(8,128)(2,1)S(1)}, f16[1032,128]{1,0:T(8,128)(2,1)S(1)}, u32[]{:S(2)}, u32[]{:S(2)}) collective-permute-start(f16[1032,128]{1,0:T(8,128)(2,1)S(1)} %get-tuple-element.39), channel_id=1, source_target_pairs={{0,8},{1,25},{2,42},{3,59},{4,76},{5,93},{6,110},{7,127},{8,128},{... | collective-permute-start | bytes 792584 | tf_op jit(solution)/shard_map/ppermute | solution.py:352
  15.2 2.2 %collective-permute-done = bf16[2048,128]{1,0:T(8,128)(2,1)S(1)} collective-permute-done((bf16[2048,128]{1,0:T(8,128)(2,1)S(1)}, bf16[2048,128]{1,0:T(8,128)(2,1)S(1)}, u32[]{:S(2)}, u32[]{:S(2)}) %collective-permute-start) | collective-permute-done | bytes 524320 | tf_op jit(solution)/shard_map/ppermute | solution.py:352
  17.3 1.7 %forward_start.1 = f32[1032,128]{1,0:T(8,128)S(1)} custom-call(s32[12]{0:T(128)S(1)} %bitcast.50, s32[1]{0:T(128)} %bitcast.half, bf16[16,12,128,128]{3,2,1,0:T(8,128)(2,1)S(1)} %get-tuple-element.18.tiles, bf16[16,128,128]{2,1,0:T(8,128)(2,1)S(1)} %bitcast.47), custom_call_target="tpu_custom_call" | custom-call | bytes 65536 | tf_op jit(solution)/shard_map/forward_start/pallas_call | solution.py:257
  19.0 2.1 %collective-permute-start.3 = (f16[1032,128]{1,0:T(8,128)(2,1)S(1)}, f16[1032,128]{1,0:T(8,128)(2,1)S(1)}, u32[]{:S(2)}, u32[]{:S(2)}) collective-permute-start(f16[1032,128]{1,0:T(8,128)(2,1)S(1)} %convert_element_type.160), channel_id=1, source_target_pairs={{0,8},{1,9},{2,10},{3,11},{4,12},{5,13},{6,14},{7,15},{8,0},{9,1},... | collective-permute-start | bytes 792584 | tf_op jit(solution)/shard_map/ppermute | solution.py:352
  21.1 1.6 %forward_second.2 = f32[1024,128]{1,0:T(8,128)S(1)} custom-call(s32[12]{0:T(128)S(1)} %bitcast.51, s32[1]{0:T(128)} %bitcast.half, bf16[16,12,128,128]{3,2,1,0:T(8,128)(2,1)S(1)} %get-tuple-element.18.tiles, bf16[16,128,128]{2,1,0:T(8,128)(2,1)S(1)} %bitcast.48), custom_call_target="tpu_custom_call" | custom-call | flops 1073741824 | bytes 1048576 | tf_op jit(solution)/shard_map/forward_second/pallas_call | solution.py:257
  22.7 1.3 collective-permute-done.2
  23.9 4.7 %collective-permute-done.3 = f16[1032,128]{1,0:T(8,128)(2,1)S(1)} collective-permute-done((f16[1032,128]{1,0:T(8,128)(2,1)S(1)}, f16[1032,128]{1,0:T(8,128)(2,1)S(1)}, u32[]{:S(2)}, u32[]{:S(2)}) %collective-permute-start.3) | collective-permute-done | bytes 264224 | tf_op jit(solution)/shard_map/ppermute | solution.py:352
  28.7 0.2 multiply_add_fusion.1
  29.0 18.6 %all_to_all.25 = f16[8,136,128]{2,1,0:T(8,128)(2,1)S(1)} all-to-all(f16[8,136,128]{2,1,0:T(8,128)(2,1)S(1)} %pad_maximum_fusion), channel_id=1, replica_groups=mesh['row'=16,'half'=2,'line'=8] {'line'}, dimensions={0} | all-to-all | bytes 557056 | tf_op jit(solution)/shard_map/all_to_all | solution.py:392
  47.8 11.9 %all_to_all.26 = f16[8,136,128]{2,1,0:T(8,128)(2,1)S(1)} all-to-all(f16[8,136,128]{2,1,0:T(8,128)(2,1)S(1)} %broadcast_in_dim.17), channel_id=1, replica_groups=mesh['row'=16,'half'=2,'line'=8] {'line'}, dimensions={0} | all-to-all | bytes 557056 | tf_op jit(solution)/shard_map/all_to_all | solution.py:395
  59.7 0.9 collective-permute-start.6
  60.6 0.7 collective-permute-start.4
  61.3 4.7 %collective-permute-start.5 = (f16[8,136,128]{2,1,0:T(8,128)(2,1)S(1)}, f16[8,136,128]{2,1,0:T(8,128)(2,1)S(1)}, u32[]{:S(2)}, u32[]{:S(2)}) collective-permute-start(f16[8,136,128]{2,1,0:T(8,128)(2,1)S(1)} %all_to_all.26), channel_id=1, source_target_pairs={{0,136},{1,121},{2,106},{3,91},{4,76},{5,61},{6,46},{7,31},{8,0},{... | collective-permute-start | bytes 835592 | tf_op jit(solution)/shard_map/ppermute | solution.py:352
  66.2 4.5 %backward.1 = f32[2,1032,128]{2,1,0:T(8,128)S(1)} custom-call(s32[12]{0:T(128)S(1)} %bitcast.52, s32[1]{0:T(128)} %bitcast.half, bf16[16,12,128,128]{3,2,1,0:T(8,128)(2,1)S(1)} %get-tuple-element.18.tiles, f32[8,128,128]{2,1,0:T(8,128)S(1)} %convert_multiply_fusion.5.own_half.first.first_own, f32[8,128,128]{2,1,0:T(8,128)S(1)} %convert_multiply_fusion.2.other_half.first_other), custom_call_target="tpu_custom_call" | custom-call | bytes 65536 | tf_op jit(solution)/shard_map/backward/pallas_call | solution.py:257
  70.9 0.7 collective-permute-start.7
  71.6 2.8 %collective-permute-start.8 = (f16[1032,128]{1,0:T(8,128)(2,1)S(1)}, f16[1032,128]{1,0:T(8,128)(2,1)S(1)}, u32[]{:S(2)}, u32[]{:S(2)}) collective-permute-start(f16[1032,128]{1,0:T(8,128)(2,1)S(1)} %get-tuple-element.37), channel_id=1, source_target_pairs={{0,8},{1,25},{2,42},{3,59},{4,76},{5,93},{6,110},{7,127},{8,128},{... | collective-permute-start | bytes 792584 | tf_op jit(solution)/shard_map/ppermute | solution.py:352
  74.6 1.8 %forward_first.1 = (f32[1032,128]{1,0:T(8,128)S(1)}, bf16[16,128,256]{2,1,0:T(8,128)(2,1)S(1)}) custom-call(s32[12]{0:T(128)S(1)} %bitcast.53, s32[1]{0:T(128)} %bitcast.half, bf16[16,12,128,128]{3,2,1,0:T(8,128)(2,1)S(1)} %get-tuple-element.18.tiles, f32[8,128,128]{2,1,0:T(8,128)S(1)} %convert_multiply_fusion.4.own_half, ...), custom_call_target="tpu_custom_call" | custom-call | bytes 65536 | tf_op jit(solution)/shard_map/forward_first/pallas_call | solution.py:257
  76.5 0.1 collective-permute-start.9
  76.6 1.6 %forward_second.3 = f32[1024,128]{1,0:T(8,128)S(1)} custom-call(s32[12]{0:T(128)S(1)} %bitcast.54, s32[1]{0:T(128)} %bitcast.half, bf16[16,12,128,128]{3,2,1,0:T(8,128)(2,1)S(1)} %get-tuple-element.18.tiles, bf16[16,128,256]{2,1,0:T(8,128)(2,1)S(1)} %get-tuple-element.23.halves), custom_call_target="tpu_custom_call" | custom-call | flops 1073741824 | bytes 1048576 | tf_op jit(solution)/shard_map/forward_second/pallas_call | solution.py:257
  78.2 1.4 collective-permute-done.8
  79.6 2.6 %collective-permute-done.9 = f16[1032,128]{1,0:T(8,128)(2,1)S(1)} collective-permute-done((f16[1032,128]{1,0:T(8,128)(2,1)S(1)}, f16[1032,128]{1,0:T(8,128)(2,1)S(1)}, u32[]{:S(2)}, u32[]{:S(2)}) %collective-permute-start.9) | collective-permute-done | bytes 264224 | tf_op jit(solution)/shard_map/ppermute | solution.py:352
  82.2 0.2 multiply_add_fusion
  82.5 26.6 %all_to_all.27 = f16[8,136,128]{2,1,0:T(8,128)(2,1)S(1)} all-to-all(f16[8,136,128]{2,1,0:T(8,128)(2,1)S(1)} %pad_maximum_fusion.1), channel_id=1, replica_groups=mesh['row'=16,'half'=2,'line'=8] {'line'}, dimensions={0} | all-to-all | bytes 557056 | tf_op jit(solution)/shard_map/all_to_all | solution.py:392
  109.3 13.1 %all_to_all.28 = f16[8,136,128]{2,1,0:T(8,128)(2,1)S(1)} all-to-all(f16[8,136,128]{2,1,0:T(8,128)(2,1)S(1)} %broadcast_in_dim.20), channel_id=1, replica_groups=mesh['row'=16,'half'=2,'line'=8] {'line'}, dimensions={0} | all-to-all | bytes 557056 | tf_op jit(solution)/shard_map/all_to_all | solution.py:395
  122.5 1.0 collective-permute-start.10
  123.5 0.4 gram.1
  123.9 17.6 %all_to_all.29.found = f32[32,8,128]{2,1,0:T(8,128)S(1)} all-to-all(f32[32,8,128]{2,1,0:T(8,128)S(1)} %gram.1), channel_id=1, replica_groups=mesh['row'=16,'half'=2,'line'=8] {'row','half'}, dimensions={0} | all-to-all | bytes 262144 | tf_op jit(solution)/shard_map/all_to_all | solution.py:433
  141.6 1.3 last.1
  (54 shorter events, 1.4 us)
Async XLA Ops:
  0.6 16.7 %copy-start.1 = (s32[1,1,12]{2,1,0:T(1,128)S(1)}, s32[1,1,12]{2,1,0:T(1,128)}, u32[]{:S(2)}) copy-start(s32[1,1,12]{2,1,0:T(1,128)} %param.5) | copy-start | bytes 148
  1.9 4.8 %copy-start.2 = (bf16[2048,128]{1,0:T(8,128)(2,1)}, bf16[2048,128]{1,0:T(8,128)(2,1)S(1)}, u32[]{:S(2)}) copy-start(bf16[2048,128]{1,0:T(8,128)(2,1)S(1)} %convert_element_type.153) | copy-start | bytes 1572868
  1.9 15.4 %collective-permute-start = (bf16[2048,128]{1,0:T(8,128)(2,1)S(1)}, bf16[2048,128]{1,0:T(8,128)(2,1)S(1)}, u32[]{:S(2)}, u32[]{:S(2)}) collective-permute-start(bf16[2048,128]{1,0:T(8,128)(2,1)S(1)} %convert_element_type.153), channel_id=1, source_target_pairs={{0,136},{1,121},{2,106},{3,91},{4,76},{5,61},{6,46},{7,31},{8,0},{... | collective-permute-start | bytes 1572872 | tf_op jit(solution)/shard_map/ppermute | solution.py:352
  12.2 10.5 %collective-permute-start.1 = (f16[1032,128]{1,0:T(8,128)(2,1)S(1)}, f16[1032,128]{1,0:T(8,128)(2,1)S(1)}, u32[]{:S(2)}, u32[]{:S(2)}) collective-permute-start(f16[1032,128]{1,0:T(8,128)(2,1)S(1)} %get-tuple-element.40), channel_id=1, source_target_pairs={{0,0},{1,17},{2,34},{3,51},{4,68},{5,85},{6,102},{7,119},{8,136},{... | collective-permute-start | bytes 792584 | tf_op jit(solution)/shard_map/ppermute | solution.py:352
  12.9 11.1 %collective-permute-start.2 = (f16[1032,128]{1,0:T(8,128)(2,1)S(1)}, f16[1032,128]{1,0:T(8,128)(2,1)S(1)}, u32[]{:S(2)}, u32[]{:S(2)}) collective-permute-start(f16[1032,128]{1,0:T(8,128)(2,1)S(1)} %get-tuple-element.39), channel_id=1, source_target_pairs={{0,8},{1,25},{2,42},{3,59},{4,76},{5,93},{6,110},{7,127},{8,128},{... | collective-permute-start | bytes 792584 | tf_op jit(solution)/shard_map/ppermute | solution.py:352
  19.0 9.6 %collective-permute-start.3 = (f16[1032,128]{1,0:T(8,128)(2,1)S(1)}, f16[1032,128]{1,0:T(8,128)(2,1)S(1)}, u32[]{:S(2)}, u32[]{:S(2)}) collective-permute-start(f16[1032,128]{1,0:T(8,128)(2,1)S(1)} %convert_element_type.160), channel_id=1, source_target_pairs={{0,8},{1,9},{2,10},{3,11},{4,12},{5,13},{6,14},{7,15},{8,0},{9,1},... | collective-permute-start | bytes 792584 | tf_op jit(solution)/shard_map/ppermute | solution.py:352
  59.7 6.4 %collective-permute-start.6 = (f16[8,136,128]{2,1,0:T(8,128)(2,1)S(1)}, f16[8,136,128]{2,1,0:T(8,128)(2,1)S(1)}, u32[]{:S(2)}, u32[]{:S(2)}) collective-permute-start(f16[8,136,128]{2,1,0:T(8,128)(2,1)S(1)} %all_to_all.26), channel_id=1, source_target_pairs={{0,8},{1,9},{2,10},{3,11},{4,12},{5,13},{6,14},{7,15},{8,0},{9,1},... | collective-permute-start | bytes 835592 | tf_op jit(solution)/shard_map/ppermute | solution.py:352
  60.6 13.8 %collective-permute-start.4 = (f16[8,136,128]{2,1,0:T(8,128)(2,1)S(1)}, f16[8,136,128]{2,1,0:T(8,128)(2,1)S(1)}, u32[]{:S(2)}, u32[]{:S(2)}) collective-permute-start(f16[8,136,128]{2,1,0:T(8,128)(2,1)S(1)} %all_to_all.26), channel_id=1, source_target_pairs={{0,0},{1,241},{2,226},{3,211},{4,196},{5,181},{6,166},{7,151},{8,1... | collective-permute-start | bytes 835592 | tf_op jit(solution)/shard_map/ppermute | solution.py:352
  61.3 13.2 %collective-permute-start.5 = (f16[8,136,128]{2,1,0:T(8,128)(2,1)S(1)}, f16[8,136,128]{2,1,0:T(8,128)(2,1)S(1)}, u32[]{:S(2)}, u32[]{:S(2)}) collective-permute-start(f16[8,136,128]{2,1,0:T(8,128)(2,1)S(1)} %all_to_all.26), channel_id=1, source_target_pairs={{0,136},{1,121},{2,106},{3,91},{4,76},{5,61},{6,46},{7,31},{8,0},{... | collective-permute-start | bytes 835592 | tf_op jit(solution)/shard_map/ppermute | solution.py:352
  70.9 7.3 %collective-permute-start.7 = (f16[1032,128]{1,0:T(8,128)(2,1)S(1)}, f16[1032,128]{1,0:T(8,128)(2,1)S(1)}, u32[]{:S(2)}, u32[]{:S(2)}) collective-permute-start(f16[1032,128]{1,0:T(8,128)(2,1)S(1)} %get-tuple-element.38), channel_id=1, source_target_pairs={{0,0},{1,17},{2,34},{3,51},{4,68},{5,85},{6,102},{7,119},{8,136},{... | collective-permute-start | bytes 792584 | tf_op jit(solution)/shard_map/ppermute | solution.py:352
  71.6 8.0 %collective-permute-start.8 = (f16[1032,128]{1,0:T(8,128)(2,1)S(1)}, f16[1032,128]{1,0:T(8,128)(2,1)S(1)}, u32[]{:S(2)}, u32[]{:S(2)}) collective-permute-start(f16[1032,128]{1,0:T(8,128)(2,1)S(1)} %get-tuple-element.37), channel_id=1, source_target_pairs={{0,8},{1,25},{2,42},{3,59},{4,76},{5,93},{6,110},{7,127},{8,128},{... | collective-permute-start | bytes 792584 | tf_op jit(solution)/shard_map/ppermute | solution.py:352
  76.5 5.7 %collective-permute-start.9 = (f16[1032,128]{1,0:T(8,128)(2,1)S(1)}, f16[1032,128]{1,0:T(8,128)(2,1)S(1)}, u32[]{:S(2)}, u32[]{:S(2)}) collective-permute-start(f16[1032,128]{1,0:T(8,128)(2,1)S(1)} %convert_element_type.184), channel_id=1, source_target_pairs={{0,8},{1,9},{2,10},{3,11},{4,12},{5,13},{6,14},{7,15},{8,0},{9,1},... | collective-permute-start | bytes 792584 | tf_op jit(solution)/shard_map/ppermute | solution.py:352
  76.6 46.9 %copy-start = (f32[2048,128]{1,0:T(8,128)S(1)}, f32[2048,128]{1,0:T(8,128)}, u32[]{:S(2)}) copy-start(f32[2048,128]{1,0:T(8,128)} %param.3) | copy-start | bytes 3145732
  122.5 19.1 %collective-permute-start.10 = (f16[8,136,128]{2,1,0:T(8,128)(2,1)S(1)}, f16[8,136,128]{2,1,0:T(8,128)(2,1)S(1)}, u32[]{:S(2)}, u32[]{:S(2)}) collective-permute-start(f16[8,136,128]{2,1,0:T(8,128)(2,1)S(1)} %all_to_all.28), channel_id=1, source_target_pairs={{0,8},{1,9},{2,10},{3,11},{4,12},{5,13},{6,14},{7,15},{8,0},{9,1},... | collective-permute-start | bytes 835592 | tf_op jit(solution)/shard_map/ppermute | solution.py:352

commit v8 on v7

--- a/solution.py
+++ b/solution.py
@@ -14,6 +14,8 @@
 CODE_ROWS = 8
 ROWS_PER_STEP = 8
 VMEM_LIMIT = 24 * 2**20
+ROUND_VMEM_LIMIT = 61 * 2**20
+ROUND_PARTS = 8
 LOADING_VMEM_LIMIT = 53 * 2**20
 
 
@@ -175,6 +177,38 @@
         turn_rows(each - start + block, other_half[block], squares, turned)
     kinds = range(0, tiles.shape[1], 2)
     backward_rows(start, kinds, offsets, tiles, squares, turned, None, out)
+
+
+def round_kernel(source, out, value, arrived):
+    parts = arrived.shape[0]
+    rows = out.shape[0] // parts
+
+    def load(part):
+        at = pl.ds(part * rows, rows)
+        return pltpu.make_async_copy(source.at[at], value.at[at], arrived.at[part])
+
+    for part in range(parts):
+        load(part).start()
+    for part in range(parts):
+        load(part).wait()
+        at = pl.ds(part * rows, rows)
+        out[at] = value[at].astype(out.dtype)
+
+
+def rounded_block(value):
+    return pl.pallas_call(
+        round_kernel,
+        out_shape=pltpu.VMEM(value.shape, jnp.bfloat16),
+        in_specs=[pl.BlockSpec(memory_space=pl.ANY)],
+        out_specs=whole_vmem(),
+        scratch_shapes=[
+            pltpu.VMEM(value.shape, value.dtype),
+            pltpu.SemaphoreType.DMA((ROUND_PARTS,)),
+        ],
+        compiler_params=pltpu.CompilerParams(vmem_limit_bytes=ROUND_VMEM_LIMIT),
+        cost_estimate=pl.CostEstimate(flops=0, bytes_accessed=2**16, transcendentals=0),
+        name="round",
+    )(value)
 
 
 def gram_kernel(half, start, first, second, out):
@@ -411,7 +445,7 @@
         code = jnp.minimum(code, jnp.minimum(code_in(back[0]), code_in(back[1]))) - 2.0
         return sum_line(arrived + decode(given), code)
 
-    rounded = start_block.astype(jnp.bfloat16)
+    rounded = rounded_block(start_block)
     far = (fetch_whole(rounded),)
     back, kept = backward_loading(tiles[0, 0], offsets, place, rounded)
     first = apply(kept, far, give_back(*back))

time: 143 us -> 143 us (level)
  no operation moved by 1% of the time
where the time goes in v8:
time: 143 us
  blocking collectives  87.7 us (61%)
  starting transfers between devices  20.9 us (15%)
  Pallas kernels  19.6 us (14%)
  waiting for transfers between devices  12.1 us (8%)
  other arithmetic  1.44 us (1%)
    all_to_all x2, blocking collectives, sum_line(): parts = lax.all_to_all(parts, 'line', 0, 0)  45 us
    all_to_all x2, blocking collectives, sum_line(): lax.all_to_all(jnp.broadcast_to(share[None], parts.shape), 'line', 0, 0)  25 us
    ppermute x11, starting transfers between devices, permute(): return lax.ppermute(value, AXES, pairs)  20.9 us
    all_to_all x1, blocking collectives, body(): found = lax.all_to_all(found, ('row', 'half'), 0, 0)  17.7 us
    pallas_call x6, Pallas kernels, call(): pl.pallas_call(kernel, out_shape=out_shape, in_specs=[whole_smem(), whole...  16.5 us
    ppermute x11, waiting for transfers between devices, permute(): return lax.ppermute(value, AXES, pairs)  12.1 us
  transfers between devices with their start and end apart: 11, of which 5 were waited for; matrix products, arithmetic and copies ran while one was open for 0% of the time, Pallas kernels for 12%

profile of v8, /device:TPU:1, one launch (start us, length us, event | category | flops | bytes accessed | tf_op | source)
XLA Modules:
  0.0 143.1 jit_solution(8387715827739647652)
XLA Ops:
  0.6 1.4 round.1
  2.0 4.7 %collective-permute-start = (bf16[2048,128]{1,0:T(8,128)(2,1)S(1)}, bf16[2048,128]{1,0:T(8,128)(2,1)S(1)}, u32[]{:S(2)}, u32[]{:S(2)}) collective-permute-start(bf16[2048,128]{1,0:T(8,128)(2,1)S(1)} %round.1), channel_id=1, source_target_pairs={{0,136},{1,121},{2,106},{3,91},{4,76},{5,61},{6,46},{7,31},{8,0},{... | collective-permute-start | bytes 1572872 | tf_op jit(solution)/shard_map/ppermute | solution.py:386
  6.8 5.3 %backward_loading.1 = (f32[2,1032,128]{2,1,0:T(8,128)S(1)}, bf16[16,12,128,128]{3,2,1,0:T(8,128)(2,1)S(1)}) custom-call(s32[12]{0:T(128)} %bitcast.50, s32[1]{0:T(128)} %bitcast.half, bf16[16,12,128,128]{3,2,1,0:T(8,128)(2,1)} %bitcast.56, bf16[16,128,128]{2,1,0:T(8,128)(2,1)} %bitcast.47), custom_call_target="tpu_custom_call" | custom-call | bytes 65536 | tf_op jit(solution)/shard_map/backward_loading/pallas_call | solution.py:291
  12.3 0.7 collective-permute-start.1
  13.0 2.3 %collective-permute-start.2 = (f16[1032,128]{1,0:T(8,128)(2,1)S(1)}, f16[1032,128]{1,0:T(8,128)(2,1)S(1)}, u32[]{:S(2)}, u32[]{:S(2)}) collective-permute-start(f16[1032,128]{1,0:T(8,128)(2,1)S(1)} %get-tuple-element.39), channel_id=1, source_target_pairs={{0,8},{1,25},{2,42},{3,59},{4,76},{5,93},{6,110},{7,127},{8,128},{... | collective-permute-start | bytes 792584 | tf_op jit(solution)/shard_map/ppermute | solution.py:386
  15.3 2.2 %collective-permute-done = bf16[2048,128]{1,0:T(8,128)(2,1)S(1)} collective-permute-done((bf16[2048,128]{1,0:T(8,128)(2,1)S(1)}, bf16[2048,128]{1,0:T(8,128)(2,1)S(1)}, u32[]{:S(2)}, u32[]{:S(2)}) %collective-permute-start) | collective-permute-done | bytes 524320 | tf_op jit(solution)/shard_map/ppermute | solution.py:386
  17.4 1.7 %forward_start.1 = f32[1032,128]{1,0:T(8,128)S(1)} custom-call(s32[12]{0:T(128)S(1)} %bitcast.51, s32[1]{0:T(128)} %bitcast.half, bf16[16,12,128,128]{3,2,1,0:T(8,128)(2,1)S(1)} %get-tuple-element.18.tiles, bf16[16,128,128]{2,1,0:T(8,128)(2,1)S(1)} %bitcast.48), custom_call_target="tpu_custom_call" | custom-call | bytes 65536 | tf_op jit(solution)/shard_map/forward_start/pallas_call | solution.py:291
  19.1 2.1 %collective-permute-start.3 = (f16[1032,128]{1,0:T(8,128)(2,1)S(1)}, f16[1032,128]{1,0:T(8,128)(2,1)S(1)}, u32[]{:S(2)}, u32[]{:S(2)}) collective-permute-start(f16[1032,128]{1,0:T(8,128)(2,1)S(1)} %convert_element_type.156), channel_id=1, source_target_pairs={{0,8},{1,9},{2,10},{3,11},{4,12},{5,13},{6,14},{7,15},{8,0},{9,1},... | collective-permute-start | bytes 792584 | tf_op jit(solution)/shard_map/ppermute | solution.py:386
  21.2 1.6 %forward_second.2 = f32[1024,128]{1,0:T(8,128)S(1)} custom-call(s32[12]{0:T(128)S(1)} %bitcast.52, s32[1]{0:T(128)} %bitcast.half, bf16[16,12,128,128]{3,2,1,0:T(8,128)(2,1)S(1)} %get-tuple-element.18.tiles, bf16[16,128,128]{2,1,0:T(8,128)(2,1)S(1)} %bitcast.49), custom_call_target="tpu_custom_call" | custom-call | flops 1073741824 | bytes 1048576 | tf_op jit(solution)/shard_map/forward_second/pallas_call | solution.py:291
  22.8 1.3 collective-permute-done.2
  24.0 4.7 %collective-permute-done.3 = f16[1032,128]{1,0:T(8,128)(2,1)S(1)} collective-permute-done((f16[1032,128]{1,0:T(8,128)(2,1)S(1)}, f16[1032,128]{1,0:T(8,128)(2,1)S(1)}, u32[]{:S(2)}, u32[]{:S(2)}) %collective-permute-start.3) | collective-permute-done | bytes 264224 | tf_op jit(solution)/shard_map/ppermute | solution.py:386
  28.8 0.2 multiply_add_fusion.1
  29.1 18.6 %all_to_all.25 = f16[8,136,128]{2,1,0:T(8,128)(2,1)S(1)} all-to-all(f16[8,136,128]{2,1,0:T(8,128)(2,1)S(1)} %pad_maximum_fusion), channel_id=1, replica_groups=mesh['row'=16,'half'=2,'line'=8] {'line'}, dimensions={0} | all-to-all | bytes 557056 | tf_op jit(solution)/shard_map/all_to_all | solution.py:426
  47.9 11.9 %all_to_all.26 = f16[8,136,128]{2,1,0:T(8,128)(2,1)S(1)} all-to-all(f16[8,136,128]{2,1,0:T(8,128)(2,1)S(1)} %broadcast_in_dim.17), channel_id=1, replica_groups=mesh['row'=16,'half'=2,'line'=8] {'line'}, dimensions={0} | all-to-all | bytes 557056 | tf_op jit(solution)/shard_map/all_to_all | solution.py:429
  59.8 0.9 collective-permute-start.6
  60.7 0.7 collective-permute-start.4
  61.4 4.7 %collective-permute-start.5 = (f16[8,136,128]{2,1,0:T(8,128)(2,1)S(1)}, f16[8,136,128]{2,1,0:T(8,128)(2,1)S(1)}, u32[]{:S(2)}, u32[]{:S(2)}) collective-permute-start(f16[8,136,128]{2,1,0:T(8,128)(2,1)S(1)} %all_to_all.26), channel_id=1, source_target_pairs={{0,136},{1,121},{2,106},{3,91},{4,76},{5,61},{6,46},{7,31},{8,0},{... | collective-permute-start | bytes 835592 | tf_op jit(solution)/shard_map/ppermute | solution.py:386
  66.3 4.6 %backward.1 = f32[2,1032,128]{2,1,0:T(8,128)S(1)} custom-call(s32[12]{0:T(128)S(1)} %bitcast.53, s32[1]{0:T(128)} %bitcast.half, bf16[16,12,128,128]{3,2,1,0:T(8,128)(2,1)S(1)} %get-tuple-element.18.tiles, f32[8,128,128]{2,1,0:T(8,128)S(1)} %convert_multiply_fusion.5.own_half.first.first_own, f32[8,128,128]{2,1,0:T(8,128)S(1)} %convert_multiply_fusion.2.other_half.first_other), custom_call_target="tpu_custom_call" | custom-call | bytes 65536 | tf_op jit(solution)/shard_map/backward/pallas_call | solution.py:291
  71.0 0.7 collective-permute-start.7
  71.7 2.8 %collective-permute-start.8 = (f16[1032,128]{1,0:T(8,128)(2,1)S(1)}, f16[1032,128]{1,0:T(8,128)(2,1)S(1)}, u32[]{:S(2)}, u32[]{:S(2)}) collective-permute-start(f16[1032,128]{1,0:T(8,128)(2,1)S(1)} %get-tuple-element.37), channel_id=1, source_target_pairs={{0,8},{1,25},{2,42},{3,59},{4,76},{5,93},{6,110},{7,127},{8,128},{... | collective-permute-start | bytes 792584 | tf_op jit(solution)/shard_map/ppermute | solution.py:386
  74.7 1.8 %forward_first.1 = (f32[1032,128]{1,0:T(8,128)S(1)}, bf16[16,128,256]{2,1,0:T(8,128)(2,1)S(1)}) custom-call(s32[12]{0:T(128)S(1)} %bitcast.54, s32[1]{0:T(128)} %bitcast.half, bf16[16,12,128,128]{3,2,1,0:T(8,128)(2,1)S(1)} %get-tuple-element.18.tiles, f32[8,128,128]{2,1,0:T(8,128)S(1)} %convert_multiply_fusion.4.own_half, ...), custom_call_target="tpu_custom_call" | custom-call | bytes 65536 | tf_op jit(solution)/shard_map/forward_first/pallas_call | solution.py:291
  76.5 0.1 collective-permute-start.9
  76.7 1.6 %forward_second.3 = f32[1024,128]{1,0:T(8,128)S(1)} custom-call(s32[12]{0:T(128)S(1)} %bitcast.55, s32[1]{0:T(128)} %bitcast.half, bf16[16,12,128,128]{3,2,1,0:T(8,128)(2,1)S(1)} %get-tuple-element.18.tiles, bf16[16,128,256]{2,1,0:T(8,128)(2,1)S(1)} %get-tuple-element.23.halves), custom_call_target="tpu_custom_call" | custom-call | flops 1073741824 | bytes 1048576 | tf_op jit(solution)/shard_map/forward_second/pallas_call | solution.py:291
  78.3 1.4 collective-permute-done.8
  79.7 2.5 %collective-permute-done.9 = f16[1032,128]{1,0:T(8,128)(2,1)S(1)} collective-permute-done((f16[1032,128]{1,0:T(8,128)(2,1)S(1)}, f16[1032,128]{1,0:T(8,128)(2,1)S(1)}, u32[]{:S(2)}, u32[]{:S(2)}) %collective-permute-start.9) | collective-permute-done | bytes 264224 | tf_op jit(solution)/shard_map/ppermute | solution.py:386
  82.3 0.2 multiply_add_fusion
  82.6 26.5 %all_to_all.27 = f16[8,136,128]{2,1,0:T(8,128)(2,1)S(1)} all-to-all(f16[8,136,128]{2,1,0:T(8,128)(2,1)S(1)} %pad_maximum_fusion.1), channel_id=1, replica_groups=mesh['row'=16,'half'=2,'line'=8] {'line'}, dimensions={0} | all-to-all | bytes 557056 | tf_op jit(solution)/shard_map/all_to_all | solution.py:426
  109.3 13.1 %all_to_all.28 = f16[8,136,128]{2,1,0:T(8,128)(2,1)S(1)} all-to-all(f16[8,136,128]{2,1,0:T(8,128)(2,1)S(1)} %broadcast_in_dim.20), channel_id=1, replica_groups=mesh['row'=16,'half'=2,'line'=8] {'line'}, dimensions={0} | all-to-all | bytes 557056 | tf_op jit(solution)/shard_map/all_to_all | solution.py:429
  122.3 1.2 collective-permute-start.10
  123.6 0.4 gram.1
  124.0 17.7 %all_to_all.29.found = f32[32,8,128]{2,1,0:T(8,128)S(1)} all-to-all(f32[32,8,128]{2,1,0:T(8,128)S(1)} %gram.1), channel_id=1, replica_groups=mesh['row'=16,'half'=2,'line'=8] {'row','half'}, dimensions={0} | all-to-all | bytes 262144 | tf_op jit(solution)/shard_map/all_to_all | solution.py:467
  141.8 1.3 last.1
  (54 shorter events, 1.4 us)
Async XLA Ops:
  0.6 16.8 %copy-start.2 = (s32[1,1,12]{2,1,0:T(1,128)S(1)}, s32[1,1,12]{2,1,0:T(1,128)}, u32[]{:S(2)}) copy-start(s32[1,1,12]{2,1,0:T(1,128)} %param.5) | copy-start | bytes 148
  2.0 4.8 %copy-start.1 = (bf16[2048,128]{1,0:T(8,128)(2,1)}, bf16[2048,128]{1,0:T(8,128)(2,1)S(1)}, u32[]{:S(2)}) copy-start(bf16[2048,128]{1,0:T(8,128)(2,1)S(1)} %round.1) | copy-start | bytes 1572868
  2.0 15.4 %collective-permute-start = (bf16[2048,128]{1,0:T(8,128)(2,1)S(1)}, bf16[2048,128]{1,0:T(8,128)(2,1)S(1)}, u32[]{:S(2)}, u32[]{:S(2)}) collective-permute-start(bf16[2048,128]{1,0:T(8,128)(2,1)S(1)} %round.1), channel_id=1, source_target_pairs={{0,136},{1,121},{2,106},{3,91},{4,76},{5,61},{6,46},{7,31},{8,0},{... | collective-permute-start | bytes 1572872 | tf_op jit(solution)/shard_map/ppermute | solution.py:386
  12.3 10.5 %collective-permute-start.1 = (f16[1032,128]{1,0:T(8,128)(2,1)S(1)}, f16[1032,128]{1,0:T(8,128)(2,1)S(1)}, u32[]{:S(2)}, u32[]{:S(2)}) collective-permute-start(f16[1032,128]{1,0:T(8,128)(2,1)S(1)} %get-tuple-element.40), channel_id=1, source_target_pairs={{0,0},{1,17},{2,34},{3,51},{4,68},{5,85},{6,102},{7,119},{8,136},{... | collective-permute-start | bytes 792584 | tf_op jit(solution)/shard_map/ppermute | solution.py:386
  13.0 11.1 %collective-permute-start.2 = (f16[1032,128]{1,0:T(8,128)(2,1)S(1)}, f16[1032,128]{1,0:T(8,128)(2,1)S(1)}, u32[]{:S(2)}, u32[]{:S(2)}) collective-permute-start(f16[1032,128]{1,0:T(8,128)(2,1)S(1)} %get-tuple-element.39), channel_id=1, source_target_pairs={{0,8},{1,25},{2,42},{3,59},{4,76},{5,93},{6,110},{7,127},{8,128},{... | collective-permute-start | bytes 792584 | tf_op jit(solution)/shard_map/ppermute | solution.py:386
  19.1 9.6 %collective-permute-start.3 = (f16[1032,128]{1,0:T(8,128)(2,1)S(1)}, f16[1032,128]{1,0:T(8,128)(2,1)S(1)}, u32[]{:S(2)}, u32[]{:S(2)}) collective-permute-start(f16[1032,128]{1,0:T(8,128)(2,1)S(1)} %convert_element_type.156), channel_id=1, source_target_pairs={{0,8},{1,9},{2,10},{3,11},{4,12},{5,13},{6,14},{7,15},{8,0},{9,1},... | collective-permute-start | bytes 792584 | tf_op jit(solution)/shard_map/ppermute | solution.py:386
  59.8 6.4 %collective-permute-start.6 = (f16[8,136,128]{2,1,0:T(8,128)(2,1)S(1)}, f16[8,136,128]{2,1,0:T(8,128)(2,1)S(1)}, u32[]{:S(2)}, u32[]{:S(2)}) collective-permute-start(f16[8,136,128]{2,1,0:T(8,128)(2,1)S(1)} %all_to_all.26), channel_id=1, source_target_pairs={{0,8},{1,9},{2,10},{3,11},{4,12},{5,13},{6,14},{7,15},{8,0},{9,1},... | collective-permute-start | bytes 835592 | tf_op jit(solution)/shard_map/ppermute | solution.py:386
  60.7 13.8 %collective-permute-start.4 = (f16[8,136,128]{2,1,0:T(8,128)(2,1)S(1)}, f16[8,136,128]{2,1,0:T(8,128)(2,1)S(1)}, u32[]{:S(2)}, u32[]{:S(2)}) collective-permute-start(f16[8,136,128]{2,1,0:T(8,128)(2,1)S(1)} %all_to_all.26), channel_id=1, source_target_pairs={{0,0},{1,241},{2,226},{3,211},{4,196},{5,181},{6,166},{7,151},{8,1... | collective-permute-start | bytes 835592 | tf_op jit(solution)/shard_map/ppermute | solution.py:386
  61.4 13.2 %collective-permute-start.5 = (f16[8,136,128]{2,1,0:T(8,128)(2,1)S(1)}, f16[8,136,128]{2,1,0:T(8,128)(2,1)S(1)}, u32[]{:S(2)}, u32[]{:S(2)}) collective-permute-start(f16[8,136,128]{2,1,0:T(8,128)(2,1)S(1)} %all_to_all.26), channel_id=1, source_target_pairs={{0,136},{1,121},{2,106},{3,91},{4,76},{5,61},{6,46},{7,31},{8,0},{... | collective-permute-start | bytes 835592 | tf_op jit(solution)/shard_map/ppermute | solution.py:386
  71.0 7.3 %collective-permute-start.7 = (f16[1032,128]{1,0:T(8,128)(2,1)S(1)}, f16[1032,128]{1,0:T(8,128)(2,1)S(1)}, u32[]{:S(2)}, u32[]{:S(2)}) collective-permute-start(f16[1032,128]{1,0:T(8,128)(2,1)S(1)} %get-tuple-element.38), channel_id=1, source_target_pairs={{0,0},{1,17},{2,34},{3,51},{4,68},{5,85},{6,102},{7,119},{8,136},{... | collective-permute-start | bytes 792584 | tf_op jit(solution)/shard_map/ppermute | solution.py:386
  71.7 8.0 %collective-permute-start.8 = (f16[1032,128]{1,0:T(8,128)(2,1)S(1)}, f16[1032,128]{1,0:T(8,128)(2,1)S(1)}, u32[]{:S(2)}, u32[]{:S(2)}) collective-permute-start(f16[1032,128]{1,0:T(8,128)(2,1)S(1)} %get-tuple-element.37), channel_id=1, source_target_pairs={{0,8},{1,25},{2,42},{3,59},{4,76},{5,93},{6,110},{7,127},{8,128},{... | collective-permute-start | bytes 792584 | tf_op jit(solution)/shard_map/ppermute | solution.py:386
  76.5 5.7 %collective-permute-start.9 = (f16[1032,128]{1,0:T(8,128)(2,1)S(1)}, f16[1032,128]{1,0:T(8,128)(2,1)S(1)}, u32[]{:S(2)}, u32[]{:S(2)}) collective-permute-start(f16[1032,128]{1,0:T(8,128)(2,1)S(1)} %convert_element_type.180), channel_id=1, source_target_pairs={{0,8},{1,9},{2,10},{3,11},{4,12},{5,13},{6,14},{7,15},{8,0},{9,1},... | collective-permute-start | bytes 792584 | tf_op jit(solution)/shard_map/ppermute | solution.py:386
  76.7 46.9 %copy-start = (f32[2048,128]{1,0:T(8,128)S(1)}, f32[2048,128]{1,0:T(8,128)}, u32[]{:S(2)}) copy-start(f32[2048,128]{1,0:T(8,128)} %source.1) | copy-start | bytes 3145732
  122.3 19.3 %collective-permute-start.10 = (f16[8,136,128]{2,1,0:T(8,128)(2,1)S(1)}, f16[8,136,128]{2,1,0:T(8,128)(2,1)S(1)}, u32[]{:S(2)}, u32[]{:S(2)}) collective-permute-start(f16[8,136,128]{2,1,0:T(8,128)(2,1)S(1)} %all_to_all.28), channel_id=1, source_target_pairs={{0,8},{1,9},{2,10},{3,11},{4,12},{5,13},{6,14},{7,15},{8,0},{9,1},... | collective-permute-start | bytes 835592 | tf_op jit(solution)/shard_map/ppermute | solution.py:386

commit v9 on v7

--- a/solution.py
+++ b/solution.py
@@ -73,12 +73,12 @@
     forward_rows(begin, offsets, tiles, far, out, jnp.exp2(code))
 
 
-def forward_first_kernel(offsets, half, tiles, own_half, other_half, out, halves):
-    each, width, columns = own_half.shape
+def forward_first_kernel(offsets, half, tiles, low_rows, high_rows, out, halves):
+    each, width, columns = low_rows.shape
     start = half[0] * each
     squares = jnp.zeros((1, columns), jnp.float32)
     for block in range(each):
-        for source, base in ((own_half, start), (other_half, each - start)):
+        for source, base in ((low_rows, 0), (high_rows, each)):
             value = source[block]
             squares += jnp.sum(value * value, axis=0, keepdims=True)
             high = value.astype(jnp.bfloat16)
@@ -166,25 +166,23 @@
                 given[block] = total if step == 0 else given[block] + total
 
 
-def backward_kernel(offsets, half, tiles, own_half, other_half, out, squares, turned):
-    each = own_half.shape[0]
-    start = half[0] * each
+def backward_kernel(offsets, half, tiles, near, out, squares, turned):
+    blocks = near.shape[0]
     squares[...] = jnp.zeros_like(squares)
-    for block in range(each):
-        turn_rows(start + block, own_half[block], squares, turned)
-        turn_rows(each - start + block, other_half[block], squares, turned)
+    for block in range(blocks):
+        turn_rows(block, near[block], squares, turned)
     kinds = range(0, tiles.shape[1], 2)
-    backward_rows(start, kinds, offsets, tiles, squares, turned, None, out)
+    backward_rows(half[0] * (blocks // 2), kinds, offsets, tiles, squares, turned, None, out)
 
 
 def gram_kernel(half, start, first, second, out):
-    count, width, columns = first.shape
+    count, width, columns = second.shape
     begin = half[0] * count
 
     def total(function):
         sums = jnp.zeros((width, columns), jnp.float32)
         for block in range(count):
-            sums += function(start[begin + block], first[block], second[block])
+            sums += function(start[begin + block], first[begin + block], second[block])
         return jnp.sum(sums, axis=0, keepdims=True)
 
     weight = total(lambda s, u, v: s * s)
@@ -200,7 +198,7 @@
         out[copy] = values
 
 
-def last_kernel(count, half, found, start, first_own, first_other, second_own, second_other, alphas, betas, out):
+def last_kernel(count, half, found, start, first, second_own, second_other, alphas, betas, out):
     a, b, weight, uu, uv, vv = (found[:, k, :] for k in range(6))
 
     def mean(value):
@@ -223,16 +221,12 @@
     of_start = (k * alpha_one * alpha_two - beta_one * inverse) / beta_two
     of_first = -k * (alpha_one + alpha_two) / beta_two
     of_second = k / beta_two
-    each = first_own.shape[0]
+    each = second_own.shape[0]
     begin = half[0] * each
-    for first, second, base in (
-        (first_own, second_own, begin),
-        (first_other, second_other, each - begin),
-    ):
+    for second, base in ((second_own, begin), (second_other, each - begin)):
         for block in range(each):
-            out[base + block] = (
-                of_start * start[base + block] + of_first * first[block] + of_second * second[block]
-            )
+            at = base + block
+            out[at] = of_start * start[at] + of_first * first[at] + of_second * second[block]
 
 
 def small_call(kernel, name, out_shape, *values, first=None):
@@ -324,16 +318,15 @@
     return (out[0].astype(WIRE), out[1].astype(WIRE)), kept
 
 
-def backward_product(tiles, offsets, half, own_half, other_half):
+def backward_product(tiles, offsets, half, near):
     blocks, _, width, _ = tiles.shape
-    columns = own_half.shape[-1]
-    shape = (blocks // 2, width, columns)
+    columns = near.shape[-1]
     (out,) = call(
         backward_kernel,
         "backward",
         (jax.ShapeDtypeStruct(messages_shape(blocks, width, columns), jnp.float32),),
         backward_scratch(blocks, width, columns, 2),
-        offsets, half, tiles, own_half.reshape(shape), other_half.reshape(shape),
+        offsets, half, tiles, near.reshape(blocks, width, columns),
     )
     return out[0].astype(WIRE), out[1].astype(WIRE)
 
@@ -391,8 +384,12 @@
     parts = pack(partial.reshape(count, rows // count, columns), code)
     parts = lax.all_to_all(parts, "line", 0, 0)
     code = jnp.min(code_in(parts), axis=0) - (count - 1).bit_length()
-    share = pack(jnp.sum(decode(parts), axis=0), code)
-    return lax.all_to_all(jnp.broadcast_to(share[None], parts.shape), "line", 0, 0)
+    return pack(jnp.sum(decode(parts), axis=0), code)
+
+
+def gather(share, axes):
+    copies = jnp.broadcast_to(share[None], (lax.axis_size(axes),) + share.shape)
+    return lax.all_to_all(copies, axes, 0, 0)
 
 
 def body(start_block, tiles, band_offsets):
@@ -414,13 +411,13 @@
     rounded = start_block.astype(jnp.bfloat16)
     far = (fetch_whole(rounded),)
     back, kept = backward_loading(tiles[0, 0], offsets, place, rounded)
-    first = apply(kept, far, give_back(*back))
-
-    first_other = swap(first)
-    far = tuple(decode(message) for message in fetch(first))
-    first, first_other = decode(first), decode(first_other)
-    back = backward_product(kept, offsets, place, first, first_other)
-    second = apply(kept, far, give_back(*back))
+    first = gather(apply(kept, far, give_back(*back)), ("half", "line"))
+
+    far = fetch_whole(first)
+    far = (decode(far[:parts]), decode(far[parts:]))
+    first = decode(first)
+    back = backward_product(kept, offsets, place, first)
+    second = gather(apply(kept, far, give_back(*back)), "line")
 
     second_other = swap(second)
     second = decode(second)
@@ -434,7 +431,7 @@
     found, second_other = lax.optimization_barrier((found, second_other))
     in_blocks = [
         value.reshape(-1, height // blocks, columns)
-        for value in (start_block, first, first_other, second, decode(second_other))
+        for value in (start_block, first, second, decode(second_other))
     ]
     alphas, betas, q_third = small_call(
         functools.partial(last_kernel, height * rows),

time: 143 us -> 155 us (1.084)
  blocking collectives: 87.8 us -> 99.4 us
  waiting for transfers between devices: 12.1 us -> 18.7 us
  starting transfers between devices: 20.7 us -> 14.6 us
    ppermute x11 -> x9, waiting for transfers between devices: 12.1 us -> 18.7 us  [permute(): return lax.ppermute(value, AXES, pairs)]
    ppermute x11 -> x9, starting transfers between devices: 20.7 us -> 14.6 us  [permute(): return lax.ppermute(value, AXES, pairs)]
    all_to_all x2, blocking collectives: 45.2 us -> 49.7 us  [sum_line(): parts = lax.all_to_all(parts, 'line', 0, 0)]
    all_to_all x1, blocking collectives: 17.6 us -> 21.6 us  [body(): found = lax.all_to_all(found, ('row', 'half'), 0, 0)]
    all_to_all x2, blocking collectives: 25 us -> 28.1 us  [gather(): return lax.all_to_all(copies, axes, 0, 0)]
  transfers between devices with their start and end apart: 11 -> 9, of which waited for: 5 -> 6; matrix products, arithmetic and copies ran while one was open for 0% -> 0% of each run, Pallas kernels for 12% -> 11%
where the time goes in v9:
time: 155 us
  blocking collectives  99.4 us (64%)
  waiting for transfers between devices  18.7 us (12%)
  Pallas kernels  18.1 us (12%)
  starting transfers between devices  14.6 us (9%)
  other arithmetic  2.73 us (2%)
    all_to_all x2, blocking collectives, sum_line(): parts = lax.all_to_all(parts, 'line', 0, 0)  49.7 us
    all_to_all x2, blocking collectives, gather(): return lax.all_to_all(copies, axes, 0, 0)  28.1 us
    all_to_all x1, blocking collectives, body(): found = lax.all_to_all(found, ('row', 'half'), 0, 0)  21.6 us
    ppermute x9, waiting for transfers between devices, permute(): return lax.ppermute(value, AXES, pairs)  18.7 us
    pallas_call x6, Pallas kernels, call(): pl.pallas_call(kernel, out_shape=out_shape, in_specs=[whole_smem(), whole...  16.4 us
    ppermute x9, starting transfers between devices, permute(): return lax.ppermute(value, AXES, pairs)  14.6 us
  transfers between devices with their start and end apart: 9, of which 6 were waited for; matrix products, arithmetic and copies ran while one was open for 0% of the time, Pallas kernels for 11%

profile of v9, /device:TPU:1, one launch (start us, length us, event | category | flops | bytes accessed | tf_op | source)
XLA Modules:
  0.0 154.9 jit_solution(13306295678345604771)
XLA Ops:
  0.6 1.3 convert_element_type.147
  1.9 4.7 %collective-permute-start = (bf16[2048,128]{1,0:T(8,128)(2,1)S(1)}, bf16[2048,128]{1,0:T(8,128)(2,1)S(1)}, u32[]{:S(2)}, u32[]{:S(2)}) collective-permute-start(bf16[2048,128]{1,0:T(8,128)(2,1)S(1)} %convert_element_type.147), channel_id=1, source_target_pairs={{0,136},{1,121},{2,106},{3,91},{4,76},{5,61},{6,46},{7,31},{8,0},{... | collective-permute-start | bytes 1572872 | tf_op jit(solution)/shard_map/ppermute | solution.py:345
  6.7 5.3 %backward_loading.1 = (f32[2,1032,128]{2,1,0:T(8,128)S(1)}, bf16[16,12,128,128]{3,2,1,0:T(8,128)(2,1)S(1)}) custom-call(s32[12]{0:T(128)} %bitcast.48, s32[1]{0:T(128)} %bitcast.half, bf16[16,12,128,128]{3,2,1,0:T(8,128)(2,1)} %bitcast.54, bf16[16,128,128]{2,1,0:T(8,128)(2,1)} %bitcast.55), custom_call_target="tpu_custom_call" | custom-call | bytes 65536 | tf_op jit(solution)/shard_map/backward_loading/pallas_call | solution.py:251
  12.3 0.7 collective-permute-start.1
  13.0 4.3 %collective-permute-done = bf16[2048,128]{1,0:T(8,128)(2,1)S(1)} collective-permute-done((bf16[2048,128]{1,0:T(8,128)(2,1)S(1)}, bf16[2048,128]{1,0:T(8,128)(2,1)S(1)}, u32[]{:S(2)}, u32[]{:S(2)}) %collective-permute-start) | collective-permute-done | bytes 524320 | tf_op jit(solution)/shard_map/ppermute | solution.py:345
  17.3 1.7 %forward_start.1 = f32[1032,128]{1,0:T(8,128)S(1)} custom-call(s32[12]{0:T(128)S(1)} %bitcast.49, s32[1]{0:T(128)} %bitcast.half, bf16[16,12,128,128]{3,2,1,0:T(8,128)(2,1)S(1)} %get-tuple-element.18.tiles, bf16[16,128,128]{2,1,0:T(8,128)(2,1)S(1)} %bitcast.46), custom_call_target="tpu_custom_call" | custom-call | bytes 65536 | tf_op jit(solution)/shard_map/forward_start/pallas_call | solution.py:251
  19.0 2.1 %collective-permute-start.3 = (f16[1032,128]{1,0:T(8,128)(2,1)S(1)}, f16[1032,128]{1,0:T(8,128)(2,1)S(1)}, u32[]{:S(2)}, u32[]{:S(2)}) collective-permute-start(f16[1032,128]{1,0:T(8,128)(2,1)S(1)} %convert_element_type.154), channel_id=1, source_target_pairs={{0,8},{1,9},{2,10},{3,11},{4,12},{5,13},{6,14},{7,15},{8,0},{9,1},... | collective-permute-start | bytes 792584 | tf_op jit(solution)/shard_map/ppermute | solution.py:345
  21.1 1.6 %forward_second.2 = f32[1024,128]{1,0:T(8,128)S(1)} custom-call(s32[12]{0:T(128)S(1)} %bitcast.50, s32[1]{0:T(128)} %bitcast.half, bf16[16,12,128,128]{3,2,1,0:T(8,128)(2,1)S(1)} %get-tuple-element.18.tiles, bf16[16,128,128]{2,1,0:T(8,128)(2,1)S(1)} %bitcast.47), custom_call_target="tpu_custom_call" | custom-call | flops 1073741824 | bytes 1048576 | tf_op jit(solution)/shard_map/forward_second/pallas_call | solution.py:251
  22.6 1.3 collective-permute-done.2
  23.9 4.7 %collective-permute-done.3 = f16[1032,128]{1,0:T(8,128)(2,1)S(1)} collective-permute-done((f16[1032,128]{1,0:T(8,128)(2,1)S(1)}, f16[1032,128]{1,0:T(8,128)(2,1)S(1)}, u32[]{:S(2)}, u32[]{:S(2)}) %collective-permute-start.3) | collective-permute-done | bytes 264224 | tf_op jit(solution)/shard_map/ppermute | solution.py:345
  28.6 0.2 multiply_add_fusion.1
  29.0 19.2 %all_to_all.25 = f16[8,136,128]{2,1,0:T(8,128)(2,1)S(1)} all-to-all(f16[8,136,128]{2,1,0:T(8,128)(2,1)S(1)} %pad_maximum_fusion), channel_id=1, replica_groups=mesh['row'=16,'half'=2,'line'=8] {'line'}, dimensions={0} | all-to-all | bytes 557056 | tf_op jit(solution)/shard_map/all_to_all | solution.py:385
  48.4 16.2 %all_to_all.26 = f16[16,136,128]{2,1,0:T(8,128)(2,1)S(1)} all-to-all(f16[16,136,128]{2,1,0:T(8,128)(2,1)S(1)} %broadcast_in_dim.17), channel_id=1, replica_groups=mesh['row'=16,'half'=2,'line'=8] {'half','line'}, dimensions={0} | all-to-all | bytes 1114112 | tf_op jit(solution)/shard_map/all_to_all | solution.py:392
  64.7 0.3 collective-permute-start.4
  64.9 0.1 convert_multiply_fusion.near.first
  65.1 4.5 %backward.1 = f32[2,1032,128]{2,1,0:T(8,128)S(1)} custom-call(s32[12]{0:T(128)S(1)} %bitcast.51, s32[1]{0:T(128)} %bitcast.half, bf16[16,12,128,128]{3,2,1,0:T(8,128)(2,1)S(1)} %get-tuple-element.18.tiles, f32[16,128,128]{2,1,0:T(8,128)S(1)} %convert_multiply_fusion.near.first), custom_call_target="tpu_custom_call" | custom-call | bytes 65536 | tf_op jit(solution)/shard_map/backward/pallas_call | solution.py:251
  69.7 0.1 slice_bitcast_fusion
  69.8 1.5 collective-permute-start.6
  71.3 0.7 collective-permute-start.5
  72.0 1.4 collective-permute-done.4
  73.5 1.8 %forward_first.1 = (f32[1032,128]{1,0:T(8,128)S(1)}, bf16[16,128,256]{2,1,0:T(8,128)(2,1)S(1)}) custom-call(s32[12]{0:T(128)S(1)} %bitcast.52, s32[1]{0:T(128)} %bitcast.half, bf16[16,12,128,128]{3,2,1,0:T(8,128)(2,1)S(1)} %get-tuple-element.18.tiles, f32[8,128,128]{2,1,0:T(8,128)S(1)} %get-tuple-element.38.low_rows, ...), custom_call_target="tpu_custom_call" | custom-call | bytes 65536 | tf_op jit(solution)/shard_map/forward_first/pallas_call | solution.py:251
  75.3 3.1 %collective-permute-start.7 = (f16[1032,128]{1,0:T(8,128)(2,1)S(1)}, f16[1032,128]{1,0:T(8,128)(2,1)S(1)}, u32[]{:S(2)}, u32[]{:S(2)}) collective-permute-start(f16[1032,128]{1,0:T(8,128)(2,1)S(1)} %convert_element_type.176), channel_id=1, source_target_pairs={{0,8},{1,9},{2,10},{3,11},{4,12},{5,13},{6,14},{7,15},{8,0},{9,1},... | collective-permute-start | bytes 792584 | tf_op jit(solution)/shard_map/ppermute | solution.py:345
  78.4 1.6 %forward_second.3 = f32[1024,128]{1,0:T(8,128)S(1)} custom-call(s32[12]{0:T(128)S(1)} %bitcast.53, s32[1]{0:T(128)} %bitcast.half, bf16[16,12,128,128]{3,2,1,0:T(8,128)(2,1)S(1)} %get-tuple-element.18.tiles, bf16[16,128,256]{2,1,0:T(8,128)(2,1)S(1)} %get-tuple-element.23.halves), custom_call_target="tpu_custom_call" | custom-call | flops 1073741824 | bytes 1048576 | tf_op jit(solution)/shard_map/forward_second/pallas_call | solution.py:251
  80.0 0.3 collective-permute-done.6
  80.3 6.7 %collective-permute-done.7 = f16[1032,128]{1,0:T(8,128)(2,1)S(1)} collective-permute-done((f16[1032,128]{1,0:T(8,128)(2,1)S(1)}, f16[1032,128]{1,0:T(8,128)(2,1)S(1)}, u32[]{:S(2)}, u32[]{:S(2)}) %collective-permute-start.7) | collective-permute-done | bytes 264224 | tf_op jit(solution)/shard_map/ppermute | solution.py:345
  87.0 0.2 multiply_add_fusion
  87.3 30.4 %all_to_all.27 = f16[8,136,128]{2,1,0:T(8,128)(2,1)S(1)} all-to-all(f16[8,136,128]{2,1,0:T(8,128)(2,1)S(1)} %pad_maximum_fusion.1), channel_id=1, replica_groups=mesh['row'=16,'half'=2,'line'=8] {'line'}, dimensions={0} | all-to-all | bytes 557056 | tf_op jit(solution)/shard_map/all_to_all | solution.py:385
  118.0 11.9 %all_to_all.28 = f16[8,136,128]{2,1,0:T(8,128)(2,1)S(1)} all-to-all(f16[8,136,128]{2,1,0:T(8,128)(2,1)S(1)} %broadcast_in_dim.20), channel_id=1, replica_groups=mesh['row'=16,'half'=2,'line'=8] {'line'}, dimensions={0} | all-to-all | bytes 557056 | tf_op jit(solution)/shard_map/all_to_all | solution.py:392
  129.9 1.5 collective-permute-start.8
  131.5 0.4 gram.1
  131.9 21.6 %all_to_all.29.found = f32[32,8,128]{2,1,0:T(8,128)S(1)} all-to-all(f32[32,8,128]{2,1,0:T(8,128)S(1)} %gram.1), channel_id=1, replica_groups=mesh['row'=16,'half'=2,'line'=8] {'row','half'}, dimensions={0} | all-to-all | bytes 262144 | tf_op jit(solution)/shard_map/all_to_all | solution.py:430
  153.6 1.3 last.1
  (46 shorter events, 1.3 us)
Async XLA Ops:
  0.6 16.7 %copy-start.1 = (s32[1,1,12]{2,1,0:T(1,128)S(1)}, s32[1,1,12]{2,1,0:T(1,128)}, u32[]{:S(2)}) copy-start(s32[1,1,12]{2,1,0:T(1,128)} %param.5) | copy-start | bytes 148
  1.9 4.8 %copy-start.2 = (bf16[2048,128]{1,0:T(8,128)(2,1)}, bf16[2048,128]{1,0:T(8,128)(2,1)S(1)}, u32[]{:S(2)}) copy-start(bf16[2048,128]{1,0:T(8,128)(2,1)S(1)} %convert_element_type.147) | copy-start | bytes 1572868
  1.9 15.3 %collective-permute-start = (bf16[2048,128]{1,0:T(8,128)(2,1)S(1)}, bf16[2048,128]{1,0:T(8,128)(2,1)S(1)}, u32[]{:S(2)}, u32[]{:S(2)}) collective-permute-start(bf16[2048,128]{1,0:T(8,128)(2,1)S(1)} %convert_element_type.147), channel_id=1, source_target_pairs={{0,136},{1,121},{2,106},{3,91},{4,76},{5,61},{6,46},{7,31},{8,0},{... | collective-permute-start | bytes 1572872 | tf_op jit(solution)/shard_map/ppermute | solution.py:345
  12.2 11.7 %collective-permute-start.2 = (f16[1032,128]{1,0:T(8,128)(2,1)S(1)}, f16[1032,128]{1,0:T(8,128)(2,1)S(1)}, u32[]{:S(2)}, u32[]{:S(2)}) collective-permute-start(f16[1032,128]{1,0:T(8,128)(2,1)S(1)} %get-tuple-element.43), channel_id=1, source_target_pairs={{0,8},{1,25},{2,42},{3,59},{4,76},{5,93},{6,110},{7,127},{8,128},{... | collective-permute-start | bytes 792584 | tf_op jit(solution)/shard_map/ppermute | solution.py:345
  12.3 11.7 %collective-permute-start.1 = (f16[1032,128]{1,0:T(8,128)(2,1)S(1)}, f16[1032,128]{1,0:T(8,128)(2,1)S(1)}, u32[]{:S(2)}, u32[]{:S(2)}) collective-permute-start(f16[1032,128]{1,0:T(8,128)(2,1)S(1)} %get-tuple-element.44), channel_id=1, source_target_pairs={{0,0},{1,17},{2,34},{3,51},{4,68},{5,85},{6,102},{7,119},{8,136},{... | collective-permute-start | bytes 792584 | tf_op jit(solution)/shard_map/ppermute | solution.py:345
  19.0 9.6 %collective-permute-start.3 = (f16[1032,128]{1,0:T(8,128)(2,1)S(1)}, f16[1032,128]{1,0:T(8,128)(2,1)S(1)}, u32[]{:S(2)}, u32[]{:S(2)}) collective-permute-start(f16[1032,128]{1,0:T(8,128)(2,1)S(1)} %convert_element_type.154), channel_id=1, source_target_pairs={{0,8},{1,9},{2,10},{3,11},{4,12},{5,13},{6,14},{7,15},{8,0},{9,1},... | collective-permute-start | bytes 792584 | tf_op jit(solution)/shard_map/ppermute | solution.py:345
  64.7 8.7 %collective-permute-start.4 = (f16[16,136,128]{2,1,0:T(8,128)(2,1)S(1)}, f16[16,136,128]{2,1,0:T(8,128)(2,1)S(1)}, u32[]{:S(2)}, u32[]{:S(2)}) collective-permute-start(f16[16,136,128]{2,1,0:T(8,128)(2,1)S(1)} %all_to_all.26), channel_id=1, source_target_pairs={{0,136},{1,121},{2,106},{3,91},{4,76},{5,61},{6,46},{7,31},{8,0},{... | collective-permute-start | bytes 1671176 | tf_op jit(solution)/shard_map/ppermute | solution.py:345
  69.8 10.5 %collective-permute-start.6 = (f16[1032,128]{1,0:T(8,128)(2,1)S(1)}, f16[1032,128]{1,0:T(8,128)(2,1)S(1)}, u32[]{:S(2)}, u32[]{:S(2)}) collective-permute-start(f16[1032,128]{1,0:T(8,128)(2,1)S(1)} %get-tuple-element.41), channel_id=1, source_target_pairs={{0,8},{1,25},{2,42},{3,59},{4,76},{5,93},{6,110},{7,127},{8,128},{... | collective-permute-start | bytes 792584 | tf_op jit(solution)/shard_map/ppermute | solution.py:345
  71.3 8.9 %collective-permute-start.5 = (f16[1032,128]{1,0:T(8,128)(2,1)S(1)}, f16[1032,128]{1,0:T(8,128)(2,1)S(1)}, u32[]{:S(2)}, u32[]{:S(2)}) collective-permute-start(f16[1032,128]{1,0:T(8,128)(2,1)S(1)} %get-tuple-element.42), channel_id=1, source_target_pairs={{0,0},{1,17},{2,34},{3,51},{4,68},{5,85},{6,102},{7,119},{8,136},{... | collective-permute-start | bytes 792584 | tf_op jit(solution)/shard_map/ppermute | solution.py:345
  75.3 11.6 %collective-permute-start.7 = (f16[1032,128]{1,0:T(8,128)(2,1)S(1)}, f16[1032,128]{1,0:T(8,128)(2,1)S(1)}, u32[]{:S(2)}, u32[]{:S(2)}) collective-permute-start(f16[1032,128]{1,0:T(8,128)(2,1)S(1)} %convert_element_type.176), channel_id=1, source_target_pairs={{0,8},{1,9},{2,10},{3,11},{4,12},{5,13},{6,14},{7,15},{8,0},{9,1},... | collective-permute-start | bytes 792584 | tf_op jit(solution)/shard_map/ppermute | solution.py:345
  78.4 53.1 %copy-start = (f32[2048,128]{1,0:T(8,128)S(1)}, f32[2048,128]{1,0:T(8,128)}, u32[]{:S(2)}) copy-start(f32[2048,128]{1,0:T(8,128)} %param.3) | copy-start | bytes 3145732
  129.9 23.7 %collective-permute-start.8 = (f16[8,136,128]{2,1,0:T(8,128)(2,1)S(1)}, f16[8,136,128]{2,1,0:T(8,128)(2,1)S(1)}, u32[]{:S(2)}, u32[]{:S(2)}) collective-permute-start(f16[8,136,128]{2,1,0:T(8,128)(2,1)S(1)} %all_to_all.28), channel_id=1, source_target_pairs={{0,8},{1,9},{2,10},{3,11},{4,12},{5,13},{6,14},{7,15},{8,0},{9,1},... | collective-permute-start | bytes 835592 | tf_op jit(solution)/shard_map/ppermute | solution.py:345
